TPU v7x, 512 devices: a whole 4x4x16 slice. The times are simulated.
512 devices in a mesh: face: 2 (over core), row: 16 (over y, z_lo), col: 16 (over z_hi, x).
Axes of the slice: x: 4, y: 4, z: 16 (z_hi: 4, z_lo: 4; z = z_hi * 4 + z_lo), core: 2. Of those that a mesh axis runs over, the one named last changes fastest.
Arguments:
- fields: bfloat16 [2, 256, 256, 128], P('face', 'row', 'col'), may hold values from -6 to 6
- conv_kernel: float32 [3, 3, 128], replicated, may hold values from -2 to 2
- conv_bias: float32 [128], replicated, may hold values from -3 to 3
- norm_gain: float32 [128], replicated, may hold values from 0.1 to 1.9
- norm_bias: float32 [128], replicated, may hold values from -3 to 3
- expand_weight: bfloat16 [128, 512], replicated, may hold values from -0.5 to 0.5
- expand_bias: float32 [512], replicated, may hold values from -3 to 3
- reduce_weight: bfloat16 [512, 128], replicated, may hold values from -0.25 to 0.25
- reduce_bias: float32 [128], replicated, may hold values from -3 to 3
- adjacency: int32 [2, 4, 3], replicated, may hold values from 0 to 3, as said below
- out_grad: bfloat16 [2, 256, 256, 128], P('face', 'row', 'col'), may hold values from -6 to 6
Outputs:
- block_out: bfloat16 [2, 256, 256, 128], P('face', 'row', 'col')
- in_grad: bfloat16 [2, 256, 256, 128], P('face', 'row', 'col')
- grad_kernel: float32 [3, 3, 128], replicated
- grad_conv_bias: float32 [128], replicated
- grad_norm_gain: float32 [128], replicated
- grad_norm_bias: float32 [128], replicated
- grad_expand_weight: float32 [128, 512], replicated
- grad_expand_bias: float32 [512], replicated
- grad_reduce_weight: float32 [512, 128], replicated
- grad_reduce_bias: float32 [128], replicated
Inputs may be any that keep to these rules, and one draw needn't show every extreme that they name: adjacency[f, e] = (g, e2, r): edge e of face f (0 first row, 1 last row, 2 first column, 3 last column) is glued to edge e2 of the other face g, read in reverse order where r = 1; a row edge is always glued to a column edge and a column edge to a row edge; every edge is glued to exactly one edge, and the entry seen from that edge names it back with the same r.
All inputs are finite; a program needn't handle non-finite values.
Results may differ from a plain program's by a relative error of at most 0.007.
Values may be sent and summed in bfloat16 or wider, within the bound.
No kernel may reach another device: no remote copies, remote signals or barrier semaphores. Data moves between devices by JAX's collectives and lax.ppermute only.
A program may use at most 64 MiB of HBM per device.

v0:
```python
import math

import jax
import jax.numpy as jnp
from jax import lax
from jax.sharding import PartitionSpec as P

GELU_SCALE = math.sqrt(2.0 / math.pi)
NORM_EPS = 1e-06


def spread(value, axis, source):
    kept = jnp.where(lax.axis_index(axis) == source, value, 0).astype(value.dtype)
    return lax.psum(kept, axis)


def padded_2(block, sides, width):
    for axis, dim in sides:
        count = lax.axis_size(axis)
        forward = [(i, i + 1) for i in range(count - 1)]
        backward = [(target, source) for source, target in forward]
        low = lax.ppermute(
            lax.slice_in_dim(block, block.shape[dim] - width, None, axis=dim), axis, forward
        )
        high = lax.ppermute(lax.slice_in_dim(block, 0, width, axis=dim), axis, backward)
        block = jnp.concatenate([low, block, high], axis=dim)
    return block


def gelu_pair(preact):
    cubic_term = preact + 0.044715 * preact * preact * preact
    tangent = jnp.tanh(GELU_SCALE * cubic_term)
    gelu_value = 0.5 * preact * (1.0 + tangent)
    gelu_slope = 0.5 * (1.0 + tangent) + 0.5 * preact * (1.0 - tangent * tangent) * GELU_SCALE * (
        1.0 + 3.0 * 0.044715 * preact * preact
    )
    return (gelu_value, gelu_slope)


def cell_block(
    mixed_cells,
    resid_cells,
    grad_cells,
    norm_gain,
    norm_bias,
    expand_weight,
    expand_bias,
    reduce_weight,
    reduce_bias,
):
    center = mixed_cells - jnp.mean(mixed_cells, axis=-1, keepdims=True)
    inv_std = lax.rsqrt(jnp.mean(center * center, axis=-1, keepdims=True) + NORM_EPS)
    normalized = center * inv_std
    normed = (normalized * norm_gain + norm_bias).astype(jnp.bfloat16)
    preact = jnp.dot(normed, expand_weight, preferred_element_type=jnp.float32) + expand_bias
    gelu_value, gelu_slope = gelu_pair(preact)
    hidden = gelu_value.astype(jnp.bfloat16)
    block_out = (
        resid_cells.astype(jnp.float32)
        + jnp.dot(hidden, reduce_weight, preferred_element_type=jnp.float32)
        + reduce_bias
    ).astype(jnp.bfloat16)
    grad_hidden = lax.dot_general(
        grad_cells, reduce_weight, (((1,), (1,)), ((), ())), preferred_element_type=jnp.float32
    )
    grad_preact = (grad_hidden * gelu_slope).astype(jnp.bfloat16)
    grad_normed = lax.dot_general(
        grad_preact, expand_weight, (((1,), (1,)), ((), ())), preferred_element_type=jnp.float32
    )
    scaled = grad_normed * norm_gain
    grad_mixed = inv_std * (
        scaled
        - jnp.mean(scaled, axis=-1, keepdims=True)
        - normalized * jnp.mean(scaled * normalized, axis=-1, keepdims=True)
    )
    cell_sums = (
        jnp.sum(grad_mixed, axis=0),
        jnp.sum(grad_normed * normalized, axis=0),
        jnp.sum(grad_normed, axis=0),
        lax.dot_general(
            normed, grad_preact, (((0,), (0,)), ((), ())), preferred_element_type=jnp.float32
        ),
        jnp.sum(grad_preact.astype(jnp.float32), axis=0),
        lax.dot_general(
            hidden, grad_cells, (((0,), (0,)), ((), ())), preferred_element_type=jnp.float32
        ),
        jnp.sum(grad_cells.astype(jnp.float32), axis=0),
    )
    return (block_out, grad_mixed, cell_sums)


def conv_rows(padded, conv_kernel, conv_bias, row_count, col_count):
    running_sum = jnp.zeros((row_count, col_count, padded.shape[2]), jnp.float32) + conv_bias
    for shift_row in range(3):
        for shift_col in range(3):
            window_cells = padded[
                shift_row : shift_row + row_count, shift_col : shift_col + col_count
            ].astype(jnp.float32)
            running_sum = running_sum + conv_kernel[shift_row, shift_col] * window_cells
    return running_sum


def kernel_grad(padded, grad_mixed, row_count, col_count):
    kernel_rows = []
    for shift_row in range(3):
        kernel_cols = []
        for shift_col in range(3):
            window_cells = padded[
                shift_row : shift_row + row_count, shift_col : shift_col + col_count
            ].astype(jnp.float32)
            kernel_cols.append(jnp.sum(grad_mixed * window_cells, axis=(0, 1)))
        kernel_rows.append(jnp.stack(kernel_cols))
    return jnp.stack(kernel_rows)


def conv_back(grad_mixed, conv_kernel):
    row_count, col_count, channels = grad_mixed.shape
    running_sum = jnp.zeros((row_count + 2, col_count + 2, channels), jnp.float32)
    for shift_row in range(3):
        for shift_col in range(3):
            placed = jnp.pad(
                conv_kernel[shift_row, shift_col] * grad_mixed,
                ((shift_row, 2 - shift_row), (shift_col, 2 - shift_col), (0, 0)),
            )
            running_sum = running_sum + placed
    return running_sum


def read_edges(edge_lines, adjacency, face_slot, row_offset, col_offset, first_pos, count_pos):
    line_count = edge_lines.shape[2]
    flat_lines = edge_lines.reshape(edge_lines.shape[0] * 4, line_count, edge_lines.shape[3])
    steps_along = jnp.arange(count_pos, dtype=jnp.int32) + first_pos
    result = []
    for border in range(4):
        entry_row = adjacency[face_slot, border]
        offset = col_offset if border < 2 else row_offset
        positions = steps_along + offset
        source = lax.dynamic_index_in_dim(
            flat_lines, entry_row[0] * 4 + entry_row[1], 0, keepdims=False
        )
        line_index = jnp.where(entry_row[2] == 1, line_count - 1 - positions, positions)
        inside = (positions >= 0) & (positions < line_count)
        picked = jnp.take(source, jnp.clip(line_index, 0, line_count - 1), axis=0)
        result.append(jnp.where(inside[:, None], picked, jnp.zeros_like(picked)))
    return result


def spread_lines(strips):
    north_strip, south_strip, west_strip, east_strip = strips
    north_line, south_line = (
        lax.all_gather(north_strip, "col", axis=0, tiled=True),
        lax.all_gather(south_strip, "col", axis=0, tiled=True),
    )
    west_line, east_line = (
        lax.all_gather(west_strip, "row", axis=0, tiled=True),
        lax.all_gather(east_strip, "row", axis=0, tiled=True),
    )
    south_all = spread(south_line, "row", lax.axis_size("row") - 1)
    east_all = spread(east_line, "col", lax.axis_size("col") - 1)
    north_all, west_all = (
        spread(north_line, ("row", "col"), 0),
        spread(west_line, ("row", "col"), 0),
    )
    stacked = jnp.stack([north_all, south_all, west_all, east_all])[None]
    return lax.all_gather(stacked, "face", axis=0, tiled=True)


def fold_rims(grad_padded, outer_cells, tile_cells):
    far_edge = tile_cells + 3
    folded = grad_padded
    folded = folded.at[1].add(outer_cells[0, 1:far_edge])
    folded = folded.at[1, 1].add(outer_cells[0, 0])
    folded = folded.at[1, tile_cells].add(outer_cells[0, far_edge])
    folded = folded.at[tile_cells].add(outer_cells[far_edge, 1:far_edge])
    folded = folded.at[tile_cells, 1].add(outer_cells[far_edge, 0])
    folded = folded.at[tile_cells, tile_cells].add(outer_cells[far_edge, far_edge])
    folded = folded.at[:, 1].add(outer_cells[1:far_edge, 0])
    folded = folded.at[:, tile_cells].add(outer_cells[1:far_edge, far_edge])
    return folded


def on_device(
    fields,
    conv_kernel,
    conv_bias,
    norm_gain,
    norm_bias,
    expand_weight,
    expand_bias,
    reduce_weight,
    reduce_bias,
    adjacency,
    out_grad,
):
    local_tile = fields[0]
    tile_cells = local_tile.shape[0]
    channels = local_tile.shape[2]
    grid_side = lax.axis_size("row")
    face_side = tile_cells * grid_side
    row_index = lax.axis_index("row")
    col_index = lax.axis_index("col")
    face_index = lax.axis_index("face")
    on_top = row_index == 0
    on_bottom = row_index == grid_side - 1
    on_left = col_index == 0
    on_right = col_index == lax.axis_size("col") - 1
    row_offset = row_index * tile_cells
    col_offset = col_index * tile_cells
    rim_edge = tile_cells + 1
    padded = padded_2(local_tile, (("row", 0), ("col", 1)), 1)
    line_x = spread_lines(
        (local_tile[0], local_tile[tile_cells - 1], local_tile[:, 0], local_tile[:, tile_cells - 1])
    )
    rim_cells = read_edges(
        line_x, adjacency, face_index, row_offset, col_offset, -1, tile_cells + 2
    )
    padded = padded.at[0].set(jnp.where(on_top, rim_cells[0], padded[0]))
    padded = padded.at[rim_edge].set(jnp.where(on_bottom, rim_cells[1], padded[rim_edge]))
    padded = padded.at[:, 0].set(jnp.where(on_left, rim_cells[2], padded[:, 0]))
    padded = padded.at[:, rim_edge].set(jnp.where(on_right, rim_cells[3], padded[:, rim_edge]))
    mixed_cells = conv_rows(padded, conv_kernel, conv_bias, tile_cells, tile_cells)
    band_rows = 16
    band_count = tile_cells // band_rows
    band_mixed = mixed_cells.reshape(band_count, band_rows * tile_cells, channels)
    band_resid = local_tile.reshape(band_count, band_rows * tile_cells, channels)
    band_grad = out_grad[0].reshape(band_count, band_rows * tile_cells, channels)
    empty_sums = (
        jnp.zeros((channels,), jnp.float32),
        jnp.zeros((channels,), jnp.float32),
        jnp.zeros((channels,), jnp.float32),
        jnp.zeros(expand_weight.shape, jnp.float32),
        jnp.zeros((expand_weight.shape[1],), jnp.float32),
        jnp.zeros(reduce_weight.shape, jnp.float32),
        jnp.zeros((channels,), jnp.float32),
    )

    def band_step(totals, band_inputs):
        mixed_band, resid_band, grad_band = band_inputs
        out_band, grad_mixed_band, band_sums = cell_block(
            mixed_band,
            resid_band,
            grad_band,
            norm_gain,
            norm_bias,
            expand_weight,
            expand_bias,
            reduce_weight,
            reduce_bias,
        )
        updated = tuple((old_term + new_term for old_term, new_term in zip(totals, band_sums)))
        return (updated, (out_band, grad_mixed_band))

    cell_sums, (out_bands, grad_bands) = lax.scan(
        band_step, empty_sums, (band_mixed, band_resid, band_grad)
    )
    block_out = out_bands.reshape(tile_cells, tile_cells, channels)
    grad_mixed = grad_bands.reshape(tile_cells, tile_cells, channels)
    kernel_sum = kernel_grad(padded, grad_mixed, tile_cells, tile_cells)
    grad_padded = conv_back(grad_mixed, conv_kernel)
    outer_cells = padded_2(grad_padded.astype(jnp.bfloat16), (("row", 0), ("col", 1)), 1).astype(
        grad_padded.dtype
    )
    folded = fold_rims(grad_padded, outer_cells, tile_cells)
    back_strips = (
        folded[0, 1:rim_edge].astype(jnp.bfloat16),
        folded[rim_edge, 1:rim_edge].astype(jnp.bfloat16),
        folded[1:rim_edge, 0].astype(jnp.bfloat16),
        folded[1:rim_edge, rim_edge].astype(jnp.bfloat16),
    )
    rim_grad = spread_lines(back_strips)
    partner_adds = read_edges(
        rim_grad, adjacency, face_index, row_offset, col_offset, 0, tile_cells
    )
    base_grad = out_grad[0].astype(jnp.float32) + folded[1:rim_edge, 1:rim_edge]
    base_grad = base_grad.at[0].add(jnp.where(on_top, partner_adds[0].astype(jnp.float32), 0.0))
    base_grad = base_grad.at[tile_cells - 1].add(
        jnp.where(on_bottom, partner_adds[1].astype(jnp.float32), 0.0)
    )
    base_grad = base_grad.at[:, 0].add(jnp.where(on_left, partner_adds[2].astype(jnp.float32), 0.0))
    base_grad = base_grad.at[:, tile_cells - 1].add(
        jnp.where(on_right, partner_adds[3].astype(jnp.float32), 0.0)
    )
    in_grad = base_grad.astype(jnp.bfloat16)
    bias_sum, gain_sum, shift_sum, expand_sum, expand_bias_sum, reduce_sum, reduce_bias_sum = (
        cell_sums
    )
    totals = lax.psum(
        (
            kernel_sum,
            bias_sum,
            gain_sum,
            shift_sum,
            expand_sum,
            expand_bias_sum,
            reduce_sum,
            reduce_bias_sum,
        ),
        ("face", "row", "col"),
    )
    return (
        block_out.reshape(1, tile_cells, tile_cells, channels),
        in_grad[None],
        totals[0] / face_side,
        totals[1] / face_side,
        totals[2] / face_side,
        totals[3] / face_side,
        totals[4] / face_side,
        totals[5] / face_side,
        totals[6] / face_side,
        totals[7] / face_side,
    )


def solution(mesh):
    in_specs = (
        P("face", "row", "col", None),
        P(),
        P(),
        P(),
        P(),
        P(),
        P(),
        P(),
        P(),
        P(),
        P("face", "row", "col", None),
    )
    out_specs = (
        P("face", "row", "col", None),
        P("face", "row", "col", None),
        P(),
        P(),
        P(),
        P(),
        P(),
        P(),
        P(),
        P(),
    )
    return jax.shard_map(
        on_device, mesh=mesh, in_specs=in_specs, out_specs=out_specs, check_vma=False
    )
```

profile of v0, /device:TPU:1, one launch (start us, length us, event | category | flops | bytes accessed | tf_op | source)
XLA Modules:
  0.0 2183.4 jit_solution(13462490937771489375)
XLA Ops:
  8.0 4.4 collective-permute-start
  14.5 37.5 %all-gather.3 = bf16[256,1,128]{2,0,1:T(8,128)(2,1)S(1)} all-gather(bf16[16,1,128]{2,0,1:T(8,128)(2,1)S(1)} %copy.60), channel_id=5, replica_groups=mesh['face'=2,'row'=16,'col'=16] {'row'}, dimensions={0}, use_global_device_ids=true | all-gather | bytes 69632 | tf_op jit(solution)/shard_map/all_gather | solution.py:156
  52.7 48.6 %all-gather.1 = bf16[1,1,256,128]{3,2,1,0:T(8,128)(2,1)S(1)} all-gather(bf16[1,1,16,128]{3,2,1,0:T(8,128)(2,1)S(1)} %get-tuple-element.339), channel_id=3, replica_groups=mesh['face'=2,'row'=16,'col'=16] {'col'}, dimensions={2}, use_global_device_ids=true | all-gather | bytes 69632 | tf_op jit(solution)/shard_map/all_gather | solution.py:152
  101.9 31.9 %all-gather.2 = bf16[256,1,128]{2,0,1:T(8,128)(2,1)S(1)} all-gather(bf16[16,1,128]{2,0,1:T(8,128)(2,1)S(1)} %copy.59), channel_id=4, replica_groups=mesh['face'=2,'row'=16,'col'=16] {'row'}, dimensions={0}, use_global_device_ids=true | all-gather | bytes 69632 | tf_op jit(solution)/shard_map/all_gather | solution.py:155
  133.9 39.2 %all-gather = bf16[1,1,256,128]{3,2,1,0:T(8,128)(2,1)S(1)} all-gather(bf16[1,1,16,128]{3,2,1,0:T(8,128)(2,1)S(1)} %get-tuple-element.342), channel_id=2, replica_groups=mesh['face'=2,'row'=16,'col'=16] {'col'}, dimensions={2}, use_global_device_ids=true | all-gather | bytes 69632 | tf_op jit(solution)/shard_map/all_gather | solution.py:151
  179.2 3.5 collective-permute-start.2
  189.3 50.2 %all-reduce.23.cloned.1.call-done = bf16[1,256,128]{2,1,0:T(8,128)(2,1)} async-done(((bf16[1,256,128]{2,1,0:T(8,128)(2,1)}), bf16[1,256,128]{2,1,0:T(8,128)(2,1)}) %all-reduce.23.cloned.1.call-update) | async-done | bytes 65552 | tf_op jit(solution)/shard_map/psum | solution.py:14
  239.5 159.5 %all-reduce.21.cloned.1.call-done = bf16[1,256,128]{2,1,0:T(8,128)(2,1)} async-done(((bf16[1,256,128]{2,1,0:T(8,128)(2,1)}), bf16[1,256,128]{2,1,0:T(8,128)(2,1)}) %all-reduce.21.cloned.1.call-update) | async-done | bytes 65552 | tf_op jit(solution)/shard_map/psum | solution.py:14
  399.0 391.0 %all-reduce.33.cloned.1.call-done = (bf16[1,256,128]{2,1,0:T(8,128)(2,1)}, bf16[1,256,128]{2,1,0:T(8,128)(2,1)}) async-done(((bf16[1,256,128]{2,1,0:T(8,128)(2,1)}, bf16[1,256,128]{2,1,0:T(8,128)(2,1)}), (bf16[1,256,128]{2,1,0:T(8,128)(2,1)}, bf16[1,256,128]{2,1,0:T(8,128)(2,1)})) %all-reduce.33.cloned.1.call-update) | async-done | bytes 131088 | tf_op jit(solution)/shard_map/psum | solution.py:14
  791.0 12.9 all-gather.4
  812.7 101.1 %all-reduce.9 = (f32[3,3,128]{2,1,0:T(4,128)S(1)}, f32[128]{0:T(128)S(1)}, f32[128]{0:T(128)S(1)}, f32[128]{0:T(128)S(1)}, f32[512]{0:T(512)S(1)}, /*index=5*/f32[128]{0:T(128)S(1)}) all-reduce(f32[3,3,128]{2,1,0:T(4,128)S(1)} %pad_maximum_fusion.13, ...), channel_id=1, replica_groups=mesh['face'=2,'row'=16,'col'=16] {'face','row','col'}, use_global_device_ids=true, to_apply=%region_21.24 | all-reduce | flops 2176 | bytes 17408 | tf_op jit(solution)/shard_map/psum | solution.py:287
  915.8 3.7 collective-permute-start.4
  922.3 1.6 collective-permute-done.5
  927.3 2.6 collective-permute-done.7
  930.4 32.3 %all-gather.8 = bf16[256,1,128]{2,0,1:T(8,128)(2,1)S(1)} all-gather(bf16[16,1,128]{2,0,1:T(8,128)(2,1)S(1)} %copy.64), channel_id=10, replica_groups=mesh['face'=2,'row'=16,'col'=16] {'row'}, dimensions={0}, use_global_device_ids=true | all-gather | bytes 69632 | tf_op jit(solution)/shard_map/all_gather | solution.py:156
  963.3 43.0 %all-gather.6 = bf16[1,256,128]{2,1,0:T(8,128)(2,1)S(1)} all-gather(bf16[1,16,128]{2,1,0:T(8,128)(2,1)S(1)} %get-tuple-element.331), channel_id=8, replica_groups=mesh['face'=2,'row'=16,'col'=16] {'col'}, dimensions={1}, use_global_device_ids=true | all-gather | bytes 69632 | tf_op jit(solution)/shard_map/all_gather | solution.py:152
  1006.9 31.6 %all-gather.7 = bf16[256,1,128]{2,0,1:T(8,128)(2,1)S(1)} all-gather(bf16[16,1,128]{2,0,1:T(8,128)(2,1)S(1)} %copy.63), channel_id=9, replica_groups=mesh['face'=2,'row'=16,'col'=16] {'row'}, dimensions={0}, use_global_device_ids=true | all-gather | bytes 69632 | tf_op jit(solution)/shard_map/all_gather | solution.py:155
  1039.1 40.4 %all-gather.5 = bf16[1,256,128]{2,1,0:T(8,128)(2,1)S(1)} all-gather(bf16[1,16,128]{2,1,0:T(8,128)(2,1)S(1)} %get-tuple-element.332), channel_id=7, replica_groups=mesh['face'=2,'row'=16,'col'=16] {'col'}, dimensions={1}, use_global_device_ids=true | all-gather | bytes 69632 | tf_op jit(solution)/shard_map/all_gather | solution.py:151
  1081.1 73.4 %all-reduce.27.cloned.1.call-done = bf16[1,256,128]{2,1,0:T(8,128)(2,1)} async-done(((bf16[1,256,128]{2,1,0:T(8,128)(2,1)}), bf16[1,256,128]{2,1,0:T(8,128)(2,1)}) %all-reduce.27.cloned.1.call-update) | async-done | bytes 65552 | tf_op jit(solution)/shard_map/psum | solution.py:14
  1154.4 158.7 %all-reduce.25.cloned.1.call-done = bf16[1,256,128]{2,1,0:T(8,128)(2,1)} async-done(((bf16[1,256,128]{2,1,0:T(8,128)(2,1)}), bf16[1,256,128]{2,1,0:T(8,128)(2,1)}) %all-reduce.25.cloned.1.call-update) | async-done | bytes 65552 | tf_op jit(solution)/shard_map/psum | solution.py:14
  1313.1 390.3 %all-reduce.31.cloned.1.call-done = (bf16[1,256,128]{2,1,0:T(8,128)(2,1)}, bf16[1,256,128]{2,1,0:T(8,128)(2,1)}) async-done(((bf16[1,256,128]{2,1,0:T(8,128)(2,1)}, bf16[1,256,128]{2,1,0:T(8,128)(2,1)}), (bf16[1,256,128]{2,1,0:T(8,128)(2,1)}, bf16[1,256,128]{2,1,0:T(8,128)(2,1)})) %all-reduce.31.cloned.1.call-update) | async-done | bytes 131088 | tf_op jit(solution)/shard_map/psum | solution.py:14
  1704.4 12.9 all-gather.9
  1720.7 453.4 %all-reduce.29.cloned.1.call-done = (f32[128,512]{1,0:T(8,128)}, f32[512,128]{1,0:T(8,128)}) async-done(((f32[128,512]{1,0:T(8,128)}, f32[512,128]{1,0:T(8,128)}), (f32[128,512]{1,0:T(8,128)}, f32[512,128]{1,0:T(8,128)})) %all-reduce.29.cloned.1.call-update) | async-done | bytes 524304 | tf_op jit(solution)/shard_map/psum | solution.py:287
  2174.1 1.7 broadcast_multiply_fusion.1
  (165 shorter events, 35.7 us)
Async XLA Ops:
  7.2 801.5 %copy-start = (bf16[128,512]{1,0:T(8,128)(2,1)S(1)}, bf16[128,512]{1,0:T(8,128)(2,1)}, u32[]{:S(2)}) copy-start(bf16[128,512]{1,0:T(8,128)(2,1)} %param.52) | copy-start | bytes 393220
  7.2 232.3 %all-reduce.23.cloned.1.call-start = ((), (), s32[]{:S(2)}) async-start(), calls=%async_computation.1 | async-start | bytes 131072 | tf_op jit(solution)/shard_map/psum | solution.py:14
  8.0 171.2 %collective-permute-start = (bf16[1,16,128]{2,1,0:T(8,128)(2,1)S(1)}, bf16[1,16,128]{2,1,0:T(8,128)(2,1)S(1)}, u32[]{:S(2)}, u32[]{:S(2)}) collective-permute-start(bf16[1,16,128]{2,1,0:T(8,128)(2,1)S(1)} %get-tuple-element.340), channel_id=1, source_target_pairs={{0,16},{16,32},{32,48},{48,64},{64,80},{80,96},{96,112},{112,128},... | collective-permute-start | bytes 12296 | tf_op jit(solution)/shard_map/ppermute | solution.py:22
  12.3 166.9 %collective-permute-start.1 = (bf16[1,16,128]{2,1,0:T(8,128)(2,1)S(1)}, bf16[1,16,128]{2,1,0:T(8,128)(2,1)S(1)}, u32[]{:S(2)}, u32[]{:S(2)}) collective-permute-start(bf16[1,16,128]{2,1,0:T(8,128)(2,1)S(1)} %get-tuple-element.341), channel_id=1, source_target_pairs={{16,0},{32,16},{48,32},{64,48},{80,64},{96,80},{112,96},{128,112},... | collective-permute-start | bytes 12296 | tf_op jit(solution)/shard_map/ppermute | solution.py:25
  52.6 346.4 %all-reduce.21.cloned.1.call-start = ((), (), s32[]{:S(2)}) async-start(), calls=%async_computation | async-start | bytes 131072 | tf_op jit(solution)/shard_map/psum | solution.py:14
  101.9 688.1 %all-reduce.33.cloned.1.call-start = ((), (), s32[]{:S(2)}) async-start(), calls=%async_computation.6 | async-start | bytes 262144 | tf_op jit(solution)/shard_map/psum | solution.py:14
  174.3 0.7 copy-start.4
  174.4 4.0 copy-start.2
  174.4 980.0 %all-reduce.27.cloned.1.call-start = ((), (), s32[]{:S(2)}) async-start(), calls=%async_computation.3 | async-start | bytes 131072 | tf_op jit(solution)/shard_map/psum | solution.py:14
  178.3 0.9 copy-start.1
  178.5 0.7 copy-start.6
  179.2 10.0 collective-permute-start.2
  182.8 6.5 collective-permute-start.3
  808.6 0.7 copy-start.7
  809.5 1.1 copy-start.10
  915.8 6.5 collective-permute-start.4
  919.5 1.3 copy-start.11
  919.5 4.4 collective-permute-start.5
  923.9 3.4 collective-permute-start.6
  925.4 4.4 collective-permute-start.7
  963.3 349.8 %all-reduce.25.cloned.1.call-start = ((), (), s32[]{:S(2)}) async-start(), calls=%async_computation.2 | async-start | bytes 131072 | tf_op jit(solution)/shard_map/psum | solution.py:14
  1079.6 623.9 %all-reduce.31.cloned.1.call-start = ((), (), s32[]{:S(2)}) async-start(), calls=%async_computation.5 | async-start | bytes 262144 | tf_op jit(solution)/shard_map/psum | solution.py:14
  1080.3 1093.9 %all-reduce.29.cloned.1.call-start = ((), (), s32[]{:S(2)}) async-start(), calls=%async_computation.4 | async-start | bytes 1048576 | tf_op jit(solution)/shard_map/psum | solution.py:287
  2174.1 1.7 copy-start.3
  (3 other events, 2.0 us)
Sparse Core Ops, SparseCore 0:
  52.7 186.7 all-reduce.22
  243.3 155.7 all-reduce.20
  405.6 384.3 all-reduce.32
  963.4 190.9 all-reduce.26
  1157.2 155.8 all-reduce.24
  1319.2 384.1 all-reduce.30
  1710.1 464.0 all-reduce.28
where the time goes:
time: 2180 us
  waiting for transfers between devices  1680 us (77%)
  blocking collectives  431 us (20%)
  between operations  22.4 us (1%)
    psum x6, waiting for transfers between devices, spread(): return lax.psum(kept, axis)  1220 us
    psum x1, waiting for transfers between devices, on_device(): lax.psum((kernel_sum, bias_sum, gain_sum, shift_sum, expand_sum, expand_b...  453 us
    psum x1, blocking collectives, on_device(): lax.psum((kernel_sum, bias_sum, gain_sum, shift_sum, expand_sum, expand_b...  101 us
    all_gather x2, blocking collectives, spread_lines(): lax.all_gather(south_strip, 'col', axis=0, tiled=True)  91.5 us
    all_gather x2, blocking collectives, spread_lines(): lax.all_gather(north_strip, 'col', axis=0, tiled=True)  79.6 us
    all_gather x2, blocking collectives, spread_lines(): lax.all_gather(east_strip, 'row', axis=0, tiled=True)  69.7 us
    all_gather x2, blocking collectives, spread_lines(): lax.all_gather(west_strip, 'row', axis=0, tiled=True)  63.5 us
  transfers between devices with their start and end apart: 15, of which 9 were waited for; matrix products, arithmetic and copies ran while one was open for 1% of the time, Pallas kernels for 0%

commit v1 on v0

v1 whole, which is shorter than its diff:
```python
import math

import jax
import jax.numpy as jnp
from jax import lax
from jax.sharding import PartitionSpec as P

GELU_SCALE = math.sqrt(2.0 / math.pi)
NORM_EPS = 1e-06
BF = jnp.bfloat16
F32 = jnp.float32


def gelu_pair(preact):
    cubic_term = preact + 0.044715 * preact * preact * preact
    tangent = jnp.tanh(GELU_SCALE * cubic_term)
    gelu_value = 0.5 * preact * (1.0 + tangent)
    gelu_slope = 0.5 * (1.0 + tangent) + 0.5 * preact * (1.0 - tangent * tangent) * GELU_SCALE * (
        1.0 + 3.0 * 0.044715 * preact * preact
    )
    return (gelu_value, gelu_slope)


def cell_block(
    mixed_cells,
    resid_cells,
    grad_cells,
    norm_gain,
    norm_bias,
    expand_weight,
    expand_bias,
    reduce_weight,
    reduce_bias,
):
    center = mixed_cells - jnp.mean(mixed_cells, axis=-1, keepdims=True)
    inv_std = lax.rsqrt(jnp.mean(center * center, axis=-1, keepdims=True) + NORM_EPS)
    normalized = center * inv_std
    normed = (normalized * norm_gain + norm_bias).astype(BF)
    preact = jnp.dot(normed, expand_weight, preferred_element_type=F32) + expand_bias
    gelu_value, gelu_slope = gelu_pair(preact)
    hidden = gelu_value.astype(BF)
    block_out = (
        resid_cells.astype(F32)
        + jnp.dot(hidden, reduce_weight, preferred_element_type=F32)
        + reduce_bias
    ).astype(BF)
    grad_hidden = lax.dot_general(
        grad_cells, reduce_weight, (((1,), (1,)), ((), ())), preferred_element_type=F32
    )
    grad_preact = (grad_hidden * gelu_slope).astype(BF)
    grad_normed = lax.dot_general(
        grad_preact, expand_weight, (((1,), (1,)), ((), ())), preferred_element_type=F32
    )
    scaled = grad_normed * norm_gain
    grad_mixed = inv_std * (
        scaled
        - jnp.mean(scaled, axis=-1, keepdims=True)
        - normalized * jnp.mean(scaled * normalized, axis=-1, keepdims=True)
    )
    cell_sums = (
        jnp.sum(grad_mixed, axis=0),
        jnp.sum(grad_normed * normalized, axis=0),
        jnp.sum(grad_normed, axis=0),
        lax.dot_general(normed, grad_preact, (((0,), (0,)), ((), ())), preferred_element_type=F32),
        jnp.sum(grad_preact.astype(F32), axis=0),
        lax.dot_general(hidden, grad_cells, (((0,), (0,)), ((), ())), preferred_element_type=F32),
        jnp.sum(grad_cells.astype(F32), axis=0),
    )
    return (block_out, grad_mixed, cell_sums)


def conv_rows(padded, conv_kernel, conv_bias, row_count, col_count):
    running_sum = jnp.zeros((row_count, col_count, padded.shape[2]), F32) + conv_bias
    for shift_row in range(3):
        for shift_col in range(3):
            window_cells = padded[
                shift_row : shift_row + row_count, shift_col : shift_col + col_count
            ].astype(F32)
            running_sum = running_sum + conv_kernel[shift_row, shift_col] * window_cells
    return running_sum


def kernel_grad(padded, grad_mixed, row_count, col_count):
    taps = []
    for shift_row in range(3):
        for shift_col in range(3):
            window_cells = padded[
                shift_row : shift_row + row_count, shift_col : shift_col + col_count
            ].astype(F32)
            taps.append(jnp.sum(grad_mixed * window_cells, axis=(0, 1)))
    return jnp.stack(taps)


def conv_back(grad_mixed, conv_kernel):
    row_count, col_count, channels = grad_mixed.shape
    running_sum = jnp.zeros((row_count + 2, col_count + 2, channels), F32)
    for shift_row in range(3):
        for shift_col in range(3):
            placed = jnp.pad(
                conv_kernel[shift_row, shift_col] * grad_mixed,
                ((shift_row, 2 - shift_row), (shift_col, 2 - shift_col), (0, 0)),
            )
            running_sum = running_sum + placed
    return running_sum


def pick(wanted, held, cells):
    chosen = (wanted[:, None] == held[None, :]).astype(BF)
    return jnp.dot(chosen, cells, preferred_element_type=F32).astype(BF)


def swap(slots, axes):
    return lax.all_to_all(slots, axes, 0, 0)


def at(slots, index):
    return lax.dynamic_index_in_dim(slots, index, 0, keepdims=False)


def on_device(
    fields,
    conv_kernel,
    conv_bias,
    norm_gain,
    norm_bias,
    expand_weight,
    expand_bias,
    reduce_weight,
    reduce_bias,
    adjacency,
    out_grad,
):
    tile = fields[0]
    cells = tile.shape[0]
    channels = tile.shape[2]
    hid = expand_weight.shape[1]
    side = lax.axis_size("row")
    width = side * cells
    lanes = ("face", "row")
    f = lax.axis_index("face")
    r = lax.axis_index("row")
    c = lax.axis_index("col")
    last = side - 1
    base = f * side
    other = (1 - f) * side
    up, down = base + jnp.maximum(r - 1, 0), base + jnp.minimum(r + 1, last)
    west_of, east_of = jnp.maximum(c - 1, 0), jnp.minimum(c + 1, last)

    slot = jnp.arange(2 * side)
    first = jnp.where(slot // side == f, slot % side < r, r == 0)[:, None, None]
    column = jnp.arange(side)
    adjacent = (jnp.abs(column - c) == 1)[:, None, None]
    lower = (column < c)[:, None, None]
    at_first, at_last = (column == 0)[:, None, None], (column == last)[:, None, None]
    edge_col = (c == 0) | (c == last)

    row_entry = jnp.where(r == 0, adjacency[f, 0], adjacency[f, 1])
    row_source = jnp.where(row_entry[1] == 2, 0, last)
    west_entry, east_entry = adjacency[f, 2], adjacency[f, 3]

    def turned(position, entry):
        return jnp.where(entry[2] == 1, width - 1 - position, position)

    def column_parts(halo_low, halo_high, row_windows, west_window, east_window):
        near = jnp.where(adjacent, jnp.where(lower, halo_low, halo_high), row_windows)
        far = jnp.where(at_first, west_window, jnp.where(at_last, east_window, row_windows))
        return near, far

    wide = jnp.arange(cells + 2) - 1
    thin = jnp.arange(cells)

    sent = jnp.concatenate(
        [
            jnp.where(first, tile[0], tile[cells - 1]),
            jnp.broadcast_to(
                jnp.where(c == 0, tile[:, 0], tile[:, cells - 1]), (2 * side, cells, channels)
            ),
        ],
        axis=1,
    )
    got = swap(sent, lanes)
    north, south = at(got, up)[:cells], at(got, down)[:cells]
    line = lax.dynamic_slice_in_dim(got, other, side, 0)[:, cells:].reshape(width, channels)
    ends = (at(got, other)[:cells], at(got, other + last)[:cells])

    row_wanted = turned((column[:, None] * cells + wide[None, :]).reshape(-1), row_entry)
    row_windows = pick(row_wanted, jnp.arange(width), line).reshape(side, cells + 2, channels)
    side_windows = []
    for entry in (west_entry, east_entry):
        strip = jnp.where(entry[1] == 0, ends[0], ends[1])
        side_windows.append(pick(turned(r * cells + wide, entry), c * cells + thin, strip))
    near, far = column_parts(
        jnp.concatenate([north[:1], tile[:, 0], south[:1]]),
        jnp.concatenate([north[cells - 1 :], tile[:, cells - 1], south[cells - 1 :]]),
        row_windows,
        side_windows[0],
        side_windows[1],
    )
    rim = cells + 2
    got = swap(jnp.concatenate([near, far], axis=1), "col")
    rim_col = jnp.sum(got[:, rim:].astype(F32), axis=0).astype(BF)
    from_source = at(got, row_source)
    rim_row = jnp.where(edge_col, from_source[:rim], from_source[rim:])
    west = jnp.where(c == 0, rim_col, at(got, west_of)[:rim])
    east = jnp.where(c == last, rim_col, at(got, east_of)[:rim])
    top = jnp.where(r == 0, rim_row, jnp.concatenate([west[:1], north, east[:1]]))
    bottom = jnp.where(r == last, rim_row, jnp.concatenate([west[rim - 1 :], south, east[rim - 1 :]]))
    padded = jnp.concatenate(
        [
            top[None],
            jnp.concatenate([west[1:-1, None], tile, east[1:-1, None]], axis=1),
            bottom[None],
        ]
    )

    mixed = conv_rows(padded, conv_kernel, conv_bias, cells, cells)
    block_out, grad_mixed, cell_sums = cell_block(
        mixed.reshape(cells * cells, channels),
        tile.reshape(cells * cells, channels),
        out_grad[0].reshape(cells * cells, channels),
        norm_gain,
        norm_bias,
        expand_weight,
        expand_bias,
        reduce_weight,
        reduce_bias,
    )
    grad_mixed = grad_mixed.reshape(cells, cells, channels)
    bias_sum, gain_sum, shift_sum, expand_sum, expand_bias_sum, reduce_sum, reduce_bias_sum = (
        cell_sums
    )
    blocks = hid // channels
    weight_sums = jnp.concatenate(
        [expand_sum[:, k * channels : (k + 1) * channels] for k in range(blocks)] + [reduce_sum]
    )
    small_sums = jnp.concatenate(
        [
            kernel_grad(padded, grad_mixed, cells, cells),
            bias_sum[None],
            gain_sum[None],
            shift_sum[None],
            expand_bias_sum.reshape(blocks, channels),
            reduce_bias_sum[None],
        ]
    )
    small_count = small_sums.shape[0]
    few = -(-small_count // (2 * side))
    small_sums = jnp.pad(small_sums, ((0, 2 * side * few - small_count), (0, 0)))
    many = weight_sums.shape[0] // (2 * side)
    sums = many + 2 * few

    def packed(weights, small):
        high = small.astype(BF)
        low = (small - high.astype(F32)).astype(BF)
        return jnp.concatenate([weights.astype(BF), high, low], axis=-2)

    def unpacked(part):
        small = part[..., many : many + few, :].astype(F32) + part[..., many + few : sums, :].astype(F32)
        return part[..., :many, :].astype(F32), small

    grad_padded = conv_back(grad_mixed, conv_kernel)
    rims = grad_padded.astype(BF)
    sent = jnp.concatenate(
        [
            packed(
                weight_sums.reshape(2 * side, many, channels),
                small_sums.reshape(2 * side, few, channels),
            ),
            jnp.where(first, rims[0], rims[rim - 1]),
            jnp.broadcast_to(
                jnp.where(c == 0, rims[:, 0], rims[:, rim - 1]), (2 * side, rim, channels)
            ),
        ],
        axis=1,
    )
    got = swap(sent, lanes)
    weights, small = unpacked(got)
    weights, small = jnp.sum(weights, axis=0), jnp.sum(small, axis=0)
    north = jnp.where(r == 0, 0, at(got, up)[sums : sums + rim].astype(F32))
    south = jnp.where(r == last, 0, at(got, down)[sums : sums + rim].astype(F32))
    line = lax.dynamic_slice_in_dim(got, other, side, 0)[:, sums + rim :].reshape(side * rim, channels)
    ends = (at(got, other)[sums : sums + rim], at(got, other + last)[sums : sums + rim])

    row_wanted = turned(jnp.arange(width), row_entry)
    held = (column[:, None] * cells + wide[None, :]).reshape(-1)
    row_windows = pick(row_wanted, held, line).reshape(side, cells, channels)
    side_windows = []
    for entry in (west_entry, east_entry):
        strip = jnp.where(entry[1] == 0, ends[0], ends[1])
        side_windows.append(pick(turned(r * cells + thin, entry), c * cells + wide, strip))

    def folded(col):
        whole = grad_padded[1:-1, col]
        return jnp.concatenate(
            [whole[:1] + north[col][None], whole[1:-1], whole[-1:] + south[col][None]]
        ).astype(BF)

    near, far = column_parts(
        folded(0), folded(rim - 1), row_windows, side_windows[0], side_windows[1]
    )
    sent = jnp.concatenate(
        [jnp.broadcast_to(packed(weights, small), (side, sums, channels)), near, far], axis=1
    )
    got = swap(sent, "col")
    weights, small = unpacked(got)
    weights, small = jnp.sum(weights, axis=0) / width, jnp.sum(small, axis=0) / width
    spread = swap(jnp.broadcast_to(packed(weights, small), (2 * side, sums, channels)), lanes)

    near, far = got[:, sums : sums + cells], got[:, sums + cells :]
    rim_col = jnp.sum(far.astype(F32), axis=0)
    rim_row = jnp.where(edge_col, at(near, row_source), at(far, row_source)).astype(F32)
    west = jnp.where(c == 0, rim_col, at(near, west_of).astype(F32))
    east = jnp.where(c == last, rim_col, at(near, east_of).astype(F32))
    north = jnp.where(r == 0, rim_row, north[1:-1])
    south = jnp.where(r == last, rim_row, south[1:-1])
    in_grad = out_grad[0].astype(F32) + grad_padded[1:-1, 1:-1]
    in_grad = in_grad + jnp.pad(north[None], ((0, cells - 1), (0, 0), (0, 0)))
    in_grad = in_grad + jnp.pad(south[None], ((cells - 1, 0), (0, 0), (0, 0)))
    in_grad = in_grad + jnp.pad(west[:, None], ((0, 0), (0, cells - 1), (0, 0)))
    in_grad = in_grad + jnp.pad(east[:, None], ((0, 0), (cells - 1, 0), (0, 0)))

    weights, small = unpacked(spread)
    weights = weights.reshape(-1, channels)
    small = small.reshape(-1, channels)
    return (
        block_out.reshape(1, cells, cells, channels),
        in_grad.astype(BF)[None],
        small[:9].reshape(3, 3, channels),
        small[9],
        small[10],
        small[11],
        jnp.concatenate([weights[k * channels : (k + 1) * channels] for k in range(blocks)], axis=1),
        small[12 : 12 + blocks].reshape(hid),
        weights[hid:],
        small[12 + blocks],
    )


def solution(mesh):
    tiles = P("face", "row", "col", None)
    in_specs = (tiles,) + (P(),) * 9 + (tiles,)
    out_specs = (tiles, tiles) + (P(),) * 8
    return jax.shard_map(
        on_device, mesh=mesh, in_specs=in_specs, out_specs=out_specs, check_vma=False
    )
```

time: 2180 us -> 146 us (0.07)
  waiting for transfers between devices: 1680 us -> 58.4 us
  blocking collectives: 431 us -> 0 us
  starting transfers between devices: 18.6 us -> 52.5 us
    psum x7 -> x0, waiting for transfers between devices: 1680 us -> none  [the longest x6 1220 us: spread(): return lax.psum(kept, axis)]
    all_gather x10 -> x0, blocking collectives: 330 us -> none  [the longest x2 91.5 us: spread_lines(): lax.all_gather(south_strip, 'col', axis=0, tiled=True)]
    psum x1 -> x0, blocking collectives: 101 us -> none  [on_device(): lax.psum((kernel_sum, bias_sum, gain_sum, shift_sum, expand_sum, expand_b...]
    all_to_all x0 -> x5, waiting for transfers between devices: none -> 58.4 us  [swap(): return lax.all_to_all(slots, axes, 0, 0)]
    all_to_all x0 -> x5, starting transfers between devices: none -> 52.5 us  [swap(): return lax.all_to_all(slots, axes, 0, 0)]
  transfers between devices with their start and end apart: 15 -> 5, of which waited for: 9 -> 5; matrix products, arithmetic and copies ran while one was open for 1% -> 2% of each run, Pallas kernels for 0% -> 0%
where the time goes in v1:
time: 146 us; the launch traced here: 145 us
  waiting for transfers between devices  58.4 us (40%)
  starting transfers between devices  52.5 us (36%)
  local copies, waits for them, and re-layouts  19.6 us (13%)
  other arithmetic  5.5 us (4%)
  between operations  5.31 us (4%)
  matrix products  3.8 us (3%)
    all_to_all x5, waiting for transfers between devices, swap(): return lax.all_to_all(slots, axes, 0, 0)  58.4 us
    all_to_all x5, starting transfers between devices, swap(): return lax.all_to_all(slots, axes, 0, 0)  52.5 us
    concatenate x1, local copies, waits for them, and re-layouts, on_device(): jnp.concatenate([packed(weight_sums.reshape(2 * side, many, channels), sm...  7.17 us
    unnamed x30, local copies, waits for them, and re-layouts  6.46 us
  transfers between devices with their start and end apart: 5, of which 5 were waited for; matrix products, arithmetic and copies ran while one was open for 2% of the time, Pallas kernels for 0%

profile of v1, /device:TPU:1, one launch (start us, length us, event | category | flops | bytes accessed | tf_op | source)
XLA Modules:
  0.0 145.1 jit_solution(13091337379023435871)
XLA Ops:
  0.7 0.7 slice_bitcast_fusion.7
  1.4 0.9 copy.233
  2.4 0.7 pad_maximum_fusion.1
  3.2 10.5 %all-to-all-start = ((bf16[32,32,128]{2,1,0:T(8,128)(2,1)}), bf16[32,32,128]{2,1,0:T(8,128)(2,1)S(1)}, u32[]{:S(2)}, u32[]{:S(2)}) async-start(bf16[32,32,128]{2,1,0:T(8,128)(2,1)} %pad_maximum_fusion.1), calls=%async_computation | async-start | bytes 524288 | tf_op jit(solution)/shard_map/all_to_all | solution.py:113
  13.7 0.7 copy-done.3
  19.1 4.9 %all-to-all-done = bf16[32,32,128]{2,1,0:T(8,128)(2,1)S(1)} async-done(((bf16[32,32,128]{2,1,0:T(8,128)(2,1)}), bf16[32,32,128]{2,1,0:T(8,128)(2,1)S(1)}, u32[]{:S(2)}, u32[]{:S(2)}) %all-to-all-start) | async-done | bytes 262176 | tf_op jit(solution)/shard_map/all_to_all | solution.py:113
  24.9 0.7 pad_maximum_fusion.3
  25.6 14.4 %all-to-all-start.1 = ((bf16[16,36,128]{2,1,0:T(8,128)(2,1)}), bf16[16,36,128]{2,1,0:T(8,128)(2,1)S(1)}, u32[]{:S(2)}, u32[]{:S(2)}) async-start(bf16[16,36,128]{2,1,0:T(8,128)(2,1)} %pad_maximum_fusion.3), calls=%async_computation.1 | async-start | bytes 327680 | tf_op jit(solution)/shard_map/all_to_all | solution.py:113
  41.4 13.0 %all-to-all-done.1 = bf16[16,36,128]{2,1,0:T(8,128)(2,1)S(1)} async-done(((bf16[16,36,128]{2,1,0:T(8,128)(2,1)}), bf16[16,36,128]{2,1,0:T(8,128)(2,1)S(1)}, u32[]{:S(2)}, u32[]{:S(2)}) %all-to-all-start.1) | async-done | bytes 147488 | tf_op jit(solution)/shard_map/all_to_all | solution.py:113
  57.5 0.7 copy-done.9
  61.1 7.2 %concatenate.95 = bf16[32,70,128]{2,1,0:T(8,128)(2,1)} concatenate(bf16[32,32,128]{2,1,0:T(8,128)(2,1)S(1)} %bitcast.216, bf16[32,1,128]{2,1,0:T(2,128)(2,1)S(1)} %copy.150, bf16[32,1,128]{2,1,0:T(2,128)(2,1)S(1)} %copy.151, bf16[32,18,128]{2,1,0:T(8,128)(2,1)S(1)} %broadcast_select_fusion, bf16[32,18,128]{2,1,0:T(8,128)(2,1)S(1)} %broadcast_in_dim.220), dimensions={1} | concatenate | bytes 1146880 | tf_op jit(solution)/shard_map/concatenate | solution.py:263
  68.3 9.4 %all-to-all-start.2 = ((bf16[32,70,128]{2,1,0:T(8,128)(2,1)}), bf16[32,70,128]{2,1,0:T(8,128)(2,1)S(1)}, u32[]{:S(2)}, u32[]{:S(2)}) async-start(bf16[32,70,128]{2,1,0:T(8,128)(2,1)} %concatenate.95), calls=%async_computation.2 | async-start | bytes 1179648 | tf_op jit(solution)/shard_map/all_to_all | solution.py:113
  77.8 16.5 %all-to-all-done.2 = bf16[32,70,128]{2,1,0:T(8,128)(2,1)S(1)} async-done(((bf16[32,70,128]{2,1,0:T(8,128)(2,1)}), bf16[32,70,128]{2,1,0:T(8,128)(2,1)S(1)}, u32[]{:S(2)}, u32[]{:S(2)}) %all-to-all-start.2) | async-done | bytes 573472 | tf_op jit(solution)/shard_map/all_to_all | solution.py:113
  95.4 0.8 pad_maximum_fusion
  96.2 3.5 %all-to-all-start.3 = ((bf16[16,66,128]{2,1,0:T(8,128)(2,1)}), bf16[16,66,128]{2,1,0:T(8,128)(2,1)S(1)}, u32[]{:S(2)}, u32[]{:S(2)}) async-start(bf16[16,66,128]{2,1,0:T(8,128)(2,1)} %pad_maximum_fusion), calls=%async_computation.3 | async-start | bytes 589824 | tf_op jit(solution)/shard_map/all_to_all | solution.py:113
  99.7 0.6 copy-done.10
  100.4 0.9 fusion.3
  101.3 13.6 %all-to-all-done.3 = bf16[16,66,128]{2,1,0:T(8,128)(2,1)S(1)} async-done(((bf16[16,66,128]{2,1,0:T(8,128)(2,1)}), bf16[16,66,128]{2,1,0:T(8,128)(2,1)S(1)}, u32[]{:S(2)}, u32[]{:S(2)}) %all-to-all-start.3) | async-done | bytes 270368 | tf_op jit(solution)/shard_map/all_to_all | solution.py:113
  115.0 0.8 broadcast_in_dim.232
  115.8 14.6 %all-to-all-start.4 = ((bf16[32,34,128]{2,1,0:T(8,128)(2,1)}), bf16[32,34,128]{2,1,0:T(8,128)(2,1)S(1)}, u32[]{:S(2)}, u32[]{:S(2)}) async-start(bf16[32,34,128]{2,1,0:T(8,128)(2,1)} %broadcast_in_dim.232), calls=%async_computation.4 | async-start | bytes 655360 | tf_op jit(solution)/shard_map/all_to_all | solution.py:113
  130.7 0.6 copy.159
  131.3 10.5 %all-to-all-done.4 = bf16[32,34,128]{2,1,0:T(8,128)(2,1)S(1)} async-done(((bf16[32,34,128]{2,1,0:T(8,128)(2,1)}), bf16[32,34,128]{2,1,0:T(8,128)(2,1)S(1)}, u32[]{:S(2)}, u32[]{:S(2)}) %all-to-all-start.4) | async-done | bytes 278560 | tf_op jit(solution)/shard_map/all_to_all | solution.py:113
  143.0 0.7 slice.574
  144.4 0.7 pad_maximum_fusion.2
  (137 shorter events, 12.1 us)
Async XLA Ops:
  0.6 56.1 %copy-start = (bf16[128,512]{1,0:T(8,128)(2,1)S(1)}, bf16[128,512]{1,0:T(8,128)(2,1)}, u32[]{:S(2)}) copy-start(bf16[128,512]{1,0:T(8,128)(2,1)} %param.16) | copy-start | bytes 393220
  3.2 20.9 %all-to-all-start = ((bf16[32,32,128]{2,1,0:T(8,128)(2,1)}), bf16[32,32,128]{2,1,0:T(8,128)(2,1)S(1)}, u32[]{:S(2)}, u32[]{:S(2)}) async-start(bf16[32,32,128]{2,1,0:T(8,128)(2,1)} %pad_maximum_fusion.1), calls=%async_computation | async-start | bytes 524288 | tf_op jit(solution)/shard_map/all_to_all | solution.py:113
  13.7 0.7 copy-start.3
  25.6 15.1 %copy-start.2 = (bf16[1,16,16,128]{3,2,1,0:T(8,128)(2,1)S(1)}, bf16[1,16,16,128]{3,2,1,0:T(8,128)(2,1)}, u32[]{:S(2)}) copy-start(bf16[1,16,16,128]{3,2,1,0:T(8,128)(2,1)} %param.21) | copy-start | bytes 196612
  25.6 28.8 %all-to-all-start.1 = ((bf16[16,36,128]{2,1,0:T(8,128)(2,1)}), bf16[16,36,128]{2,1,0:T(8,128)(2,1)S(1)}, u32[]{:S(2)}, u32[]{:S(2)}) async-start(bf16[16,36,128]{2,1,0:T(8,128)(2,1)} %pad_maximum_fusion.3), calls=%async_computation.1 | async-start | bytes 327680 | tf_op jit(solution)/shard_map/all_to_all | solution.py:113
  40.7 0.7 copy-start.5
  54.6 0.7 copy-start.7
  55.9 0.7 copy-start.4
  55.9 0.7 copy-start.8
  56.6 0.7 copy-start.6
  57.3 0.9 copy-start.9
  58.9 0.8 copy-start.1
  68.3 25.9 %all-to-all-start.2 = ((bf16[32,70,128]{2,1,0:T(8,128)(2,1)}), bf16[32,70,128]{2,1,0:T(8,128)(2,1)S(1)}, u32[]{:S(2)}, u32[]{:S(2)}) async-start(bf16[32,70,128]{2,1,0:T(8,128)(2,1)} %concatenate.95), calls=%async_computation.2 | async-start | bytes 1179648 | tf_op jit(solution)/shard_map/all_to_all | solution.py:113
  96.2 18.8 %all-to-all-start.3 = ((bf16[16,66,128]{2,1,0:T(8,128)(2,1)}), bf16[16,66,128]{2,1,0:T(8,128)(2,1)S(1)}, u32[]{:S(2)}, u32[]{:S(2)}) async-start(bf16[16,66,128]{2,1,0:T(8,128)(2,1)} %pad_maximum_fusion), calls=%async_computation.3 | async-start | bytes 589824 | tf_op jit(solution)/shard_map/all_to_all | solution.py:113
  99.7 0.7 copy-start.10
  115.8 26.0 %all-to-all-start.4 = ((bf16[32,34,128]{2,1,0:T(8,128)(2,1)}), bf16[32,34,128]{2,1,0:T(8,128)(2,1)S(1)}, u32[]{:S(2)}, u32[]{:S(2)}) async-start(bf16[32,34,128]{2,1,0:T(8,128)(2,1)} %broadcast_in_dim.232), calls=%async_computation.4 | async-start | bytes 655360 | tf_op jit(solution)/shard_map/all_to_all | solution.py:113

commit v2 on v1

v2 whole, which is shorter than its diff:
```python
import math

import jax
import jax.numpy as jnp
from jax import lax
from jax.experimental import pallas as pl
from jax.experimental.pallas import tpu as pltpu
from jax.sharding import PartitionSpec as P

GELU_SCALE = math.sqrt(2.0 / math.pi)
NORM_EPS = 1e-06
BF = jnp.bfloat16
F32 = jnp.float32


def gelu_pair(preact):
    cubic_term = preact + 0.044715 * preact * preact * preact
    tangent = jnp.tanh(GELU_SCALE * cubic_term)
    gelu_value = 0.5 * preact * (1.0 + tangent)
    gelu_slope = 0.5 * (1.0 + tangent) + 0.5 * preact * (1.0 - tangent * tangent) * GELU_SCALE * (
        1.0 + 3.0 * 0.044715 * preact * preact
    )
    return (gelu_value, gelu_slope)


def block_kernel(
    plan_ref,
    padded_ref,
    tile_ref,
    grad_ref,
    tap_ref,
    conv_bias_ref,
    gain_ref,
    shift_ref,
    expand_ref,
    expand_bias_ref,
    reduce_ref,
    reduce_bias_ref,
    out_ref,
    sent_ref,
    base_ref,
    cols_ref,
    wide_ref,
):
    rows, columns, channels = tile_ref.shape
    count = rows * columns
    rim = rows + 2
    hid = expand_ref.shape[1]
    slots, _, _ = sent_ref.shape
    side = slots // 2
    padded = padded_ref[...].astype(F32)
    shifted = [padded[:, b : b + columns] for b in range(3)]

    mixed = jnp.zeros((rows, columns, channels), F32) + conv_bias_ref[...].reshape(1, 1, channels)
    for a in range(3):
        for b in range(3):
            mixed = mixed + tap_ref[3 * a + b].reshape(1, 1, channels) * shifted[b][a : a + rows]
    mixed = mixed.reshape(count, channels)
    center = mixed - jnp.mean(mixed, axis=-1, keepdims=True)
    inv_std = lax.rsqrt(jnp.mean(center * center, axis=-1, keepdims=True) + NORM_EPS)
    normalized = center * inv_std
    normed = (normalized * gain_ref[...] + shift_ref[...]).astype(BF)
    preact = jnp.dot(normed, expand_ref[...], preferred_element_type=F32) + expand_bias_ref[...]
    gelu_value, gelu_slope = gelu_pair(preact)
    hidden = gelu_value.astype(BF)
    grad_cells = grad_ref[...].reshape(count, channels)
    grad_hidden = lax.dot_general(
        grad_cells, reduce_ref[...], (((1,), (1,)), ((), ())), preferred_element_type=F32
    )
    grad_preact = (grad_hidden * gelu_slope).astype(BF)
    grad_normed = lax.dot_general(
        grad_preact, expand_ref[...], (((1,), (1,)), ((), ())), preferred_element_type=F32
    )
    scaled = grad_normed * gain_ref[...]
    grad_mixed = inv_std * (
        scaled
        - jnp.mean(scaled, axis=-1, keepdims=True)
        - normalized * jnp.mean(scaled * normalized, axis=-1, keepdims=True)
    )
    out = tile_ref[...].reshape(count, channels).astype(F32)
    out = out + jnp.dot(hidden, reduce_ref[...], preferred_element_type=F32) + reduce_bias_ref[...]
    out_ref[...] = out.astype(BF).reshape(rows, columns, channels)

    def total(cells):
        return jnp.sum(cells, axis=0, keepdims=True)

    square = grad_mixed.reshape(rows, columns, channels)
    small = [
        total((square * shifted[b][a : a + rows]).reshape(count, channels))
        for a in range(3)
        for b in range(3)
    ]
    small += [total(grad_mixed), total(grad_normed * normalized), total(grad_normed)]
    preact_total = total(grad_preact.astype(F32))
    small += [preact_total[:, k : k + channels] for k in range(0, hid, channels)]
    small += [total(grad_cells.astype(F32))]

    across = (((0,), (0,)), ((), ()))
    expand_sum = lax.dot_general(normed, grad_preact, across, preferred_element_type=F32).astype(BF)
    reduce_sum = lax.dot_general(hidden, grad_cells, across, preferred_element_type=F32).astype(BF)
    many = 2 * hid // slots
    for k in range(0, hid, channels):
        for j in range(0, channels, many):
            sent_ref[(k + j) // many, 0:many] = expand_sum[j : j + many, k : k + channels]
    for k in range(0, hid, many):
        sent_ref[(hid + k) // many, 0:many] = reduce_sum[k : k + many]

    wide_ref[...] = jnp.zeros(wide_ref.shape, F32)
    for b in range(3):
        parts = [tap_ref[3 * a + b].reshape(1, 1, channels) * square for a in range(3)]
        wide_ref[0, b : b + columns] += parts[0][0]
        wide_ref[1, b : b + columns] += parts[0][1] + parts[1][0]
        wide_ref[2:rows, b : b + columns] += (
            parts[0][2:] + parts[1][1 : rows - 1] + parts[2][: rows - 2]
        )
        wide_ref[rows, b : b + columns] += parts[1][rows - 1] + parts[2][rows - 2]
        wide_ref[rows + 1, b : b + columns] += parts[2][rows - 1]
    base_ref[...] = grad_ref[...].astype(F32) + wide_ref[1 : rows + 1, 1 : columns + 1]
    west = jnp.concatenate([wide_ref[k, 0:1] for k in range(rim)])
    east = jnp.concatenate([wide_ref[k, rim - 1 : rim] for k in range(rim)])
    cols_ref[0] = west[1 : rim - 1]
    cols_ref[1] = east[1 : rim - 1]
    north = wide_ref[0, 0:rim]
    south = wide_ref[rim - 1, 0:rim]

    face, row, col = plan_ref[0], plan_ref[1], plan_ref[2]
    few = -(-len(small) // slots)
    extra = sent_ref.shape[1] - many - 2 * rows
    side_strip = jnp.where(col == 0, west, east)
    side_cells = side_strip[1 : rim - 1].astype(BF)
    place = lax.broadcasted_iota(jnp.int32, (extra, channels), 0)
    near = many + rows
    for slot in range(slots):
        first = jnp.where(face == slot // side, slot % side < row, row == 0)
        strip = jnp.where(first, north, south)
        sent_ref[slot, many:near] = strip[1 : rim - 1].astype(BF)
        sent_ref[slot, near : near + rows] = side_cells
        ends = [strip[0:1], strip[rim - 1 : rim], side_strip[0:1], side_strip[rim - 1 : rim]]
        values = ends
        for k in range(few * slot, min(few * slot + few, len(small))):
            high = small[k].astype(BF).astype(F32)
            values = values + [high, small[k] - high]
        block = jnp.zeros((extra, channels), F32)
        for k, value in enumerate(values):
            block = jnp.where(place == k, value, block)
        sent_ref[slot, near + rows : near + rows + extra] = block.astype(BF)


def block_on_tile(plan, padded, tile, grad, taps, *params):
    rows, columns, channels = tile.shape
    slots, depth = params[-2:]
    return pl.pallas_call(
        block_kernel,
        out_shape=(
            jax.ShapeDtypeStruct(tile.shape, BF),
            jax.ShapeDtypeStruct((slots, depth, channels), BF),
            jax.ShapeDtypeStruct(tile.shape, F32),
            jax.ShapeDtypeStruct((2, rows, channels), F32),
        ),
        in_specs=[pl.BlockSpec(memory_space=pltpu.SMEM)]
        + [pl.BlockSpec(memory_space=pltpu.VMEM)] * 11,
        out_specs=(pl.BlockSpec(memory_space=pltpu.VMEM),) * 4,
        scratch_shapes=[pltpu.VMEM((rows + 2, columns + 8, channels), F32)],
        compiler_params=pltpu.CompilerParams(vmem_limit_bytes=24 * 1024 * 1024),
        name="block",
    )(plan, padded, tile, grad, taps, *params[:-2])


def finish_kernel(got_ref, *out_refs):
    tap_ref, bias_ref, gain_ref, shift_ref, expand_ref, expand_bias_ref, reduce_ref, reduce_bias_ref = (
        out_refs
    )
    slots, depth, channels = got_ref.shape
    hid = reduce_ref.shape[0]
    many = 2 * hid // slots
    for k in range(0, hid, channels):
        for j in range(0, channels, many):
            expand_ref[j : j + many, k : k + channels] = got_ref[(k + j) // many, 0:many].astype(F32)
    for k in range(0, hid, many):
        reduce_ref[k : k + many] = got_ref[(hid + k) // many, 0:many].astype(F32)
    blocks = hid // channels
    few = -(-(13 + blocks) // slots)
    small = []
    for slot in range(slots):
        rest = got_ref[slot, many:depth].astype(F32)
        small += [rest[2 * k : 2 * k + 1] + rest[2 * k + 1 : 2 * k + 2] for k in range(few)]
    for k in range(9):
        tap_ref[k : k + 1] = small[k]
    bias_ref[...] = small[9]
    gain_ref[...] = small[10]
    shift_ref[...] = small[11]
    for k in range(blocks):
        expand_bias_ref[:, k * channels : (k + 1) * channels] = small[12 + k]
    reduce_bias_ref[...] = small[12 + blocks]


def finish(got, hid):
    channels = got.shape[2]
    shapes = [(9, channels)] + [(1, channels)] * 3
    shapes += [(channels, hid), (1, hid), (hid, channels), (1, channels)]
    return pl.pallas_call(
        finish_kernel,
        out_shape=tuple(jax.ShapeDtypeStruct(shape, F32) for shape in shapes),
        in_specs=[pl.BlockSpec(memory_space=pltpu.VMEM)],
        out_specs=(pl.BlockSpec(memory_space=pltpu.VMEM),) * len(shapes),
        compiler_params=pltpu.CompilerParams(vmem_limit_bytes=16 * 1024 * 1024),
        name="finish",
    )(got)


def pick(wanted, held, cells):
    chosen = (wanted[:, None] == held[None, :]).astype(BF)
    return jnp.dot(chosen, cells, preferred_element_type=F32).astype(BF)


def swap(slots, axes):
    return lax.all_to_all(slots, axes, 0, 0)


def at(slots, index):
    return lax.dynamic_index_in_dim(slots, index, 0, keepdims=False)


def on_device(
    fields,
    conv_kernel,
    conv_bias,
    norm_gain,
    norm_bias,
    expand_weight,
    expand_bias,
    reduce_weight,
    reduce_bias,
    adjacency,
    out_grad,
):
    tile = fields[0]
    cells = tile.shape[0]
    channels = tile.shape[2]
    hid = expand_weight.shape[1]
    side = lax.axis_size("row")
    width = side * cells
    lanes = ("face", "row")
    f = lax.axis_index("face")
    r = lax.axis_index("row")
    c = lax.axis_index("col")
    last = side - 1
    base = f * side
    other = (1 - f) * side
    up, down = base + jnp.maximum(r - 1, 0), base + jnp.minimum(r + 1, last)
    west_of, east_of = jnp.maximum(c - 1, 0), jnp.minimum(c + 1, last)

    slot = jnp.arange(2 * side)
    first = jnp.where(slot // side == f, slot % side < r, r == 0)[:, None, None]
    column = jnp.arange(side)
    adjacent = (jnp.abs(column - c) == 1)[:, None, None]
    lower = (column < c)[:, None, None]
    at_first, at_last = (column == 0)[:, None, None], (column == last)[:, None, None]
    edge_col = (c == 0) | (c == last)

    row_entry = jnp.where(r == 0, adjacency[f, 0], adjacency[f, 1])
    row_source = jnp.where(row_entry[1] == 2, 0, last)
    west_entry, east_entry = adjacency[f, 2], adjacency[f, 3]

    def turned(position, entry):
        return jnp.where(entry[2] == 1, width - 1 - position, position)

    def column_parts(halo_low, halo_high, row_windows, west_window, east_window):
        near = jnp.where(adjacent, jnp.where(lower, halo_low, halo_high), row_windows)
        far = jnp.where(at_first, west_window, jnp.where(at_last, east_window, row_windows))
        return near, far

    wide = jnp.arange(cells + 2) - 1
    thin = jnp.arange(cells)

    sent = jnp.concatenate(
        [
            jnp.where(first, tile[0], tile[cells - 1]),
            jnp.broadcast_to(
                jnp.where(c == 0, tile[:, 0], tile[:, cells - 1]), (2 * side, cells, channels)
            ),
        ],
        axis=1,
    )
    got = swap(sent, lanes)
    north, south = at(got, up)[:cells], at(got, down)[:cells]
    line = lax.dynamic_slice_in_dim(got, other, side, 0)[:, cells:].reshape(width, channels)
    ends = (at(got, other)[:cells], at(got, other + last)[:cells])

    row_wanted = turned((column[:, None] * cells + wide[None, :]).reshape(-1), row_entry)
    row_windows = pick(row_wanted, jnp.arange(width), line).reshape(side, cells + 2, channels)
    side_windows = []
    for entry in (west_entry, east_entry):
        strip = jnp.where(entry[1] == 0, ends[0], ends[1])
        side_windows.append(pick(turned(r * cells + wide, entry), c * cells + thin, strip))
    near, far = column_parts(
        jnp.concatenate([north[:1], tile[:, 0], south[:1]]),
        jnp.concatenate([north[cells - 1 :], tile[:, cells - 1], south[cells - 1 :]]),
        row_windows,
        side_windows[0],
        side_windows[1],
    )
    rim = cells + 2
    got = swap(jnp.concatenate([near, far], axis=1), "col")
    rim_col = jnp.sum(got[:, rim:].astype(F32), axis=0).astype(BF)
    from_source = at(got, row_source)
    rim_row = jnp.where(edge_col, from_source[:rim], from_source[rim:])
    west = jnp.where(c == 0, rim_col, at(got, west_of)[:rim])
    east = jnp.where(c == last, rim_col, at(got, east_of)[:rim])
    top = jnp.where(r == 0, rim_row, jnp.concatenate([west[:1], north, east[:1]]))
    bottom = jnp.where(r == last, rim_row, jnp.concatenate([west[rim - 1 :], south, east[rim - 1 :]]))
    padded = jnp.concatenate(
        [
            top[None],
            jnp.concatenate([west[1:-1, None], tile, east[1:-1, None]], axis=1),
            bottom[None],
        ]
    )

    small_count = 13 + hid // channels
    many = 2 * hid // (2 * side)
    few = -(-small_count // (2 * side))
    extra = -(-(2 * few + 4) // 8) * 8
    block_out, sent, base_grad, edge_cols = block_on_tile(
        jnp.stack([f, r, c]).astype(jnp.int32),
        padded,
        tile,
        out_grad[0],
        conv_kernel.reshape(9, channels),
        conv_bias.reshape(1, channels),
        norm_gain.reshape(1, channels),
        norm_bias.reshape(1, channels),
        expand_weight,
        expand_bias.reshape(1, hid),
        reduce_weight,
        reduce_bias.reshape(1, channels),
        2 * side,
        many + 2 * cells + extra,
    )
    got = swap(sent, lanes)
    near_at, far_at, rest_at = many, many + cells, many + 2 * cells

    def packed(small):
        high = small.astype(BF)
        low = (small - high.astype(F32)).astype(BF)
        pairs = jnp.stack([high, low], axis=-2).reshape(2 * few, channels)
        return jnp.pad(pairs, ((0, 8 * (-(-few // 4)) - 2 * few), (0, 0)))

    def small_total(rest):
        pairs = jnp.sum(rest.astype(F32), axis=0).reshape(few, 2, channels)
        return pairs[:, 0] + pairs[:, 1]

    weights = jnp.sum(got[:, :many].astype(F32), axis=0)
    small = small_total(got[:, rest_at + 4 : rest_at + 4 + 2 * few])

    def strip(part, main, spare):
        return jnp.concatenate(
            [
                part[..., rest_at + spare : rest_at + spare + 1, :],
                part[..., main : main + cells, :],
                part[..., rest_at + spare + 1 : rest_at + spare + 2, :],
            ],
            axis=-2,
        )

    north = jnp.where(r == 0, 0, strip(at(got, up), near_at, 0).astype(F32))
    south = jnp.where(r == last, 0, strip(at(got, down), near_at, 0).astype(F32))
    line = strip(lax.dynamic_slice_in_dim(got, other, side, 0), far_at, 2).reshape(
        side * rim, channels
    )
    ends = (strip(at(got, other), near_at, 0), strip(at(got, other + last), near_at, 0))

    row_wanted = turned(jnp.arange(width), row_entry)
    held = (column[:, None] * cells + wide[None, :]).reshape(-1)
    row_windows = pick(row_wanted, held, line).reshape(side, cells, channels)
    side_windows = []
    for entry in (west_entry, east_entry):
        strip = jnp.where(entry[1] == 0, ends[0], ends[1])
        side_windows.append(pick(turned(r * cells + thin, entry), c * cells + wide, strip))

    def folded(end, col):
        whole = edge_cols[end]
        return jnp.concatenate(
            [whole[:1] + north[col][None], whole[1:-1], whole[-1:] + south[col][None]]
        ).astype(BF)

    near, far = column_parts(
        folded(0, 0), folded(1, rim - 1), row_windows, side_windows[0], side_windows[1]
    )
    rest = packed(small)
    sent = jnp.concatenate(
        [
            jnp.broadcast_to(weights.astype(BF), (side, many, channels)),
            near,
            far,
            jnp.broadcast_to(rest, (side,) + rest.shape),
        ],
        axis=1,
    )
    got = swap(sent, "col")
    weights = jnp.sum(got[:, :many].astype(F32), axis=0) / width
    small = small_total(got[:, rest_at : rest_at + 2 * few]) / width
    share = jnp.concatenate([weights.astype(BF), packed(small)])
    spread = swap(jnp.broadcast_to(share, (2 * side,) + share.shape), lanes)

    near, far = got[:, near_at:far_at], got[:, far_at:rest_at]
    rim_col = jnp.sum(far.astype(F32), axis=0)
    rim_row = jnp.where(edge_col, at(near, row_source), at(far, row_source)).astype(F32)
    west = jnp.where(c == 0, rim_col, at(near, west_of).astype(F32))
    east = jnp.where(c == last, rim_col, at(near, east_of).astype(F32))
    north = jnp.where(r == 0, rim_row, north[1:-1])
    south = jnp.where(r == last, rim_row, south[1:-1])
    in_grad = base_grad
    in_grad = in_grad + jnp.pad(north[None], ((0, cells - 1), (0, 0), (0, 0)))
    in_grad = in_grad + jnp.pad(south[None], ((cells - 1, 0), (0, 0), (0, 0)))
    in_grad = in_grad + jnp.pad(west[:, None], ((0, 0), (0, cells - 1), (0, 0)))
    in_grad = in_grad + jnp.pad(east[:, None], ((0, 0), (cells - 1, 0), (0, 0)))

    taps, bias, gain, shift, expand, expand_vector, reduce, reduce_vector = finish(spread, hid)
    return (
        block_out[None],
        in_grad.astype(BF)[None],
        taps.reshape(3, 3, channels),
        bias.reshape(channels),
        gain.reshape(channels),
        shift.reshape(channels),
        expand,
        expand_vector.reshape(hid),
        reduce,
        reduce_vector.reshape(channels),
    )


def solution(mesh):
    tiles = P("face", "row", "col", None)
    in_specs = (tiles,) + (P(),) * 9 + (tiles,)
    out_specs = (tiles, tiles) + (P(),) * 8
    return jax.shard_map(
        on_device, mesh=mesh, in_specs=in_specs, out_specs=out_specs, check_vma=False
    )
```

time: 146 us -> 133 us (0.911)
  blocking collectives: 0 us -> 18.1 us
  waiting for transfers between devices: 58.4 us -> 44.9 us
  local copies, waits for them, and re-layouts: 19.6 us -> 6.99 us
  starting transfers between devices: 52.5 us -> 48.6 us
  Pallas kernels: 0 us -> 3.56 us
  matrix products: 3.8 us -> 1.25 us
  other arithmetic: 5.5 us -> 3.3 us
    all_to_all x0 -> x1, blocking collectives: none -> 18.1 us  [swap(): return lax.all_to_all(slots, axes, 0, 0)]
    all_to_all x5 -> x4, waiting for transfers between devices: 58.4 us -> 44.9 us  [swap(): return lax.all_to_all(slots, axes, 0, 0)]
    concatenate x2 -> x0, local copies, waits for them, and re-layouts: 7.23 us -> none  [the longest x1 7.17 us: on_device(): jnp.concatenate([packed(weight_sums.reshape(2 * side, many, channels), sm...]
    all_to_all x5 -> x4, starting transfers between devices: 52.5 us -> 48.6 us  [swap(): return lax.all_to_all(slots, axes, 0, 0)]
    unnamed x30 -> x22, local copies, waits for them, and re-layouts: 6.46 us -> 2.67 us
    pallas_call x0 -> x2, Pallas kernels: none -> 3.56 us  [the longest x1 2.74 us: block_on_tile(): pl.pallas_call(block_kernel, out_shape=(jax.ShapeDtypeStruct(tile.shape,...]
    dot_general x6 -> x0, matrix products: 2.55 us -> none  [the longest x1 0.93 us: cell_block(): jnp.dot(hidden, reduce_weight, preferred_element_type=F32)]
  transfers between devices with their start and end apart: 5 -> 4, of which waited for: 5 -> 4; matrix products, arithmetic and copies ran while one was open for 2% -> 2% of each run, Pallas kernels for 0% -> 0%
where the time goes in v2:
time: 133 us; the launch traced here: 132 us
  starting transfers between devices  48.6 us (37%)
  waiting for transfers between devices  44.9 us (34%)
  blocking collectives  18.1 us (14%)
  local copies, waits for them, and re-layouts  6.99 us (5%)
  between operations  5.12 us (4%)
  Pallas kernels  3.56 us (3%)
  other arithmetic  3.3 us (2%)
    all_to_all x4, starting transfers between devices, swap(): return lax.all_to_all(slots, axes, 0, 0)  48.6 us
    all_to_all x4, waiting for transfers between devices, swap(): return lax.all_to_all(slots, axes, 0, 0)  44.9 us
    all_to_all x1, blocking collectives, swap(): return lax.all_to_all(slots, axes, 0, 0)  18.1 us
    pallas_call x1, Pallas kernels, block_on_tile(): pl.pallas_call(block_kernel, out_shape=(jax.ShapeDtypeStruct(tile.shape,...  2.74 us
    unnamed x22, local copies, waits for them, and re-layouts  2.67 us
  transfers between devices with their start and end apart: 4, of which 4 were waited for; matrix products, arithmetic and copies ran while one was open for 2% of the time, Pallas kernels for 0%

profile of v2, /device:TPU:1, one launch (start us, length us, event | category | flops | bytes accessed | tf_op | source)
XLA Modules:
  0.0 131.8 jit_solution(16598157649643339157)
XLA Ops:
  0.6 0.7 slice_bitcast_fusion.5
  1.4 0.8 fusion.67
  2.3 0.7 pad_maximum_fusion.1
  3.0 10.5 %all-to-all-start = ((bf16[32,32,128]{2,1,0:T(8,128)(2,1)}), bf16[32,32,128]{2,1,0:T(8,128)(2,1)S(1)}, u32[]{:S(2)}, u32[]{:S(2)}) async-start(bf16[32,32,128]{2,1,0:T(8,128)(2,1)} %pad_maximum_fusion.1), calls=%async_computation | async-start | bytes 524288 | tf_op jit(solution)/shard_map/all_to_all | solution.py:217
  13.6 0.7 copy-done.9
  14.3 0.5 fusion.68
  14.8 0.6 constant_dynamic-slice_fusion.41
  18.9 5.0 %all-to-all-done = bf16[32,32,128]{2,1,0:T(8,128)(2,1)S(1)} async-done(((bf16[32,32,128]{2,1,0:T(8,128)(2,1)}), bf16[32,32,128]{2,1,0:T(8,128)(2,1)S(1)}, u32[]{:S(2)}, u32[]{:S(2)}) %all-to-all-start) | async-done | bytes 262176 | tf_op jit(solution)/shard_map/all_to_all | solution.py:217
  24.7 0.7 pad_maximum_fusion.2
  25.5 14.3 %all-to-all-start.1 = ((bf16[16,36,128]{2,1,0:T(8,128)(2,1)}), bf16[16,36,128]{2,1,0:T(8,128)(2,1)S(1)}, u32[]{:S(2)}, u32[]{:S(2)}) async-start(bf16[16,36,128]{2,1,0:T(8,128)(2,1)} %pad_maximum_fusion.2), calls=%async_computation.1 | async-start | bytes 327680 | tf_op jit(solution)/shard_map/all_to_all | solution.py:217
  39.8 0.7 copy-done.10
  41.2 12.9 %all-to-all-done.1 = bf16[16,36,128]{2,1,0:T(8,128)(2,1)S(1)} async-done(((bf16[16,36,128]{2,1,0:T(8,128)(2,1)}), bf16[16,36,128]{2,1,0:T(8,128)(2,1)S(1)}, u32[]{:S(2)}, u32[]{:S(2)}) %all-to-all-start.1) | async-done | bytes 147488 | tf_op jit(solution)/shard_map/all_to_all | solution.py:217
  54.4 0.6 copy-done
  55.3 0.5 copy-done.5
  55.8 2.7 %block.1 = (bf16[16,16,128]{2,1,0:T(8,128)(2,1)}, bf16[32,72,128]{2,1,0:T(8,128)(2,1)}, f32[16,16,128]{2,1,0:T(8,128)S(1)}, f32[2,16,128]{2,1,0:T(8,128)S(1)}) custom-call(s32[3]{0:T(128)S(1)} %pad_add_fusion.1.plan_ref, bf16[18,18,128]{2,1,0:T(8,128)(2,1)S(1)} %pad_maximum_fusion.3.padded_ref, bf16[16,16,128]{2,1,0:T(8,128)(2,1)S(1)} %bitcast.141, ...), custom_call_target="tpu_custom_call" | custom-call | tf_op jit(solution)/shard_map/block/pallas_call | solution.py:152
  58.5 9.4 %all-to-all-start.2 = ((bf16[32,72,128]{2,1,0:T(8,128)(2,1)}), bf16[32,72,128]{2,1,0:T(8,128)(2,1)S(1)}, u32[]{:S(2)}, u32[]{:S(2)}) async-start(bf16[32,72,128]{2,1,0:T(8,128)(2,1)} %get-tuple-element.24), calls=%async_computation.2 | async-start | bytes 1179648 | tf_op jit(solution)/shard_map/all_to_all | solution.py:217
  67.9 16.4 %all-to-all-done.2 = bf16[32,72,128]{2,1,0:T(8,128)(2,1)S(1)} async-done(((bf16[32,72,128]{2,1,0:T(8,128)(2,1)}), bf16[32,72,128]{2,1,0:T(8,128)(2,1)S(1)}, u32[]{:S(2)}, u32[]{:S(2)}) %all-to-all-start.2) | async-done | bytes 589856 | tf_op jit(solution)/shard_map/all_to_all | solution.py:217
  85.6 18.1 %all_to_all.25 = bf16[16,72,128]{2,1,0:T(8,128)(2,1)S(1)} all-to-all(bf16[16,72,128]{2,1,0:T(8,128)(2,1)S(1)} %pad_maximum_fusion), channel_id=1, replica_groups=mesh['face'=2,'row'=16,'col'=16] {'col'}, dimensions={0} | all-to-all | bytes 589824 | tf_op jit(solution)/shard_map/all_to_all | solution.py:217
  103.8 0.8 broadcast_in_dim.197
  104.6 14.4 %all-to-all-start.4 = ((bf16[32,40,128]{2,1,0:T(8,128)(2,1)}), bf16[32,40,128]{2,1,0:T(8,128)(2,1)S(1)}, u32[]{:S(2)}, u32[]{:S(2)}) async-start(bf16[32,40,128]{2,1,0:T(8,128)(2,1)} %broadcast_in_dim.197), calls=%async_computation.4 | async-start | bytes 655360 | tf_op jit(solution)/shard_map/all_to_all | solution.py:217
  119.1 0.7 fusion.6
  119.8 10.6 %all-to-all-done.4.got_ref = bf16[32,40,128]{2,1,0:T(8,128)(2,1)S(1)} async-done(((bf16[32,40,128]{2,1,0:T(8,128)(2,1)}), bf16[32,40,128]{2,1,0:T(8,128)(2,1)S(1)}, u32[]{:S(2)}, u32[]{:S(2)}) %all-to-all-start.4) | async-done | bytes 327712 | tf_op jit(solution)/shard_map/all_to_all | solution.py:217
  130.4 0.8 finish.1
  131.2 0.6 reshape.353
  (94 shorter events, 3.1 us)
Async XLA Ops:
  3.0 20.9 %all-to-all-start = ((bf16[32,32,128]{2,1,0:T(8,128)(2,1)}), bf16[32,32,128]{2,1,0:T(8,128)(2,1)S(1)}, u32[]{:S(2)}, u32[]{:S(2)}) async-start(bf16[32,32,128]{2,1,0:T(8,128)(2,1)} %pad_maximum_fusion.1), calls=%async_computation | async-start | bytes 524288 | tf_op jit(solution)/shard_map/all_to_all | solution.py:217
  13.5 0.7 copy-start.9
  25.5 28.7 %all-to-all-start.1 = ((bf16[16,36,128]{2,1,0:T(8,128)(2,1)}), bf16[16,36,128]{2,1,0:T(8,128)(2,1)S(1)}, u32[]{:S(2)}, u32[]{:S(2)}) async-start(bf16[16,36,128]{2,1,0:T(8,128)(2,1)} %pad_maximum_fusion.2), calls=%async_computation.1 | async-start | bytes 327680 | tf_op jit(solution)/shard_map/all_to_all | solution.py:217
  39.8 0.7 copy-start.10
  54.1 1.0 copy-start.3
  54.2 0.8 copy-start
  54.2 0.8 copy-start.4
  54.2 0.8 copy-start.7
  54.3 0.8 copy-start.8
  54.3 0.9 copy-start.2
  54.3 1.0 copy-start.1
  55.0 0.7 copy-start.5
  55.1 0.7 copy-start.6
  58.5 25.9 %all-to-all-start.2 = ((bf16[32,72,128]{2,1,0:T(8,128)(2,1)}), bf16[32,72,128]{2,1,0:T(8,128)(2,1)S(1)}, u32[]{:S(2)}, u32[]{:S(2)}) async-start(bf16[32,72,128]{2,1,0:T(8,128)(2,1)} %get-tuple-element.24), calls=%async_computation.2 | async-start | bytes 1179648 | tf_op jit(solution)/shard_map/all_to_all | solution.py:217
  104.6 25.8 %all-to-all-start.4 = ((bf16[32,40,128]{2,1,0:T(8,128)(2,1)}), bf16[32,40,128]{2,1,0:T(8,128)(2,1)S(1)}, u32[]{:S(2)}, u32[]{:S(2)}) async-start(bf16[32,40,128]{2,1,0:T(8,128)(2,1)} %broadcast_in_dim.197), calls=%async_computation.4 | async-start | bytes 655360 | tf_op jit(solution)/shard_map/all_to_all | solution.py:217

commit v3 on v2

--- a/solution.py
+++ b/solution.py
@@ -39,7 +39,6 @@
     out_ref,
     sent_ref,
     base_ref,
-    cols_ref,
     wide_ref,
 ):
     rows, columns, channels = tile_ref.shape
@@ -118,23 +117,29 @@
     base_ref[...] = grad_ref[...].astype(F32) + wide_ref[1 : rows + 1, 1 : columns + 1]
     west = jnp.concatenate([wide_ref[k, 0:1] for k in range(rim)])
     east = jnp.concatenate([wide_ref[k, rim - 1 : rim] for k in range(rim)])
-    cols_ref[0] = west[1 : rim - 1]
-    cols_ref[1] = east[1 : rim - 1]
     north = wide_ref[0, 0:rim]
     south = wide_ref[rim - 1, 0:rim]
 
     face, row, col = plan_ref[0], plan_ref[1], plan_ref[2]
+    cut = math.isqrt(side)
+    here_y, here_x = row // cut, col % cut
     few = -(-len(small) // slots)
     extra = sent_ref.shape[1] - many - 2 * rows
-    side_strip = jnp.where(col == 0, west, east)
-    side_cells = side_strip[1 : rim - 1].astype(BF)
     place = lax.broadcasted_iota(jnp.int32, (extra, channels), 0)
     near = many + rows
+    edge_row = jnp.where(row == 0, north, south)
+    edge_col = jnp.where(col == 0, west, east)
     for slot in range(slots):
-        first = jnp.where(face == slot // side, slot % side < row, row == 0)
-        strip = jnp.where(first, north, south)
+        same = face == slot // side
+        y, x = slot % side // cut, slot % cut
+        level = jnp.where(
+            x == (here_x + cut - 1) % cut, west, jnp.where(x == (here_x + 1) % cut, east, north)
+        )
+        inner = jnp.where(y < here_y, north, jnp.where(y > here_y, south, level))
+        strip = jnp.where(same, inner, edge_row)
+        side_strip = jnp.where(same, south, edge_col)
         sent_ref[slot, many:near] = strip[1 : rim - 1].astype(BF)
-        sent_ref[slot, near : near + rows] = side_cells
+        sent_ref[slot, near : near + rows] = side_strip[1 : rim - 1].astype(BF)
         ends = [strip[0:1], strip[rim - 1 : rim], side_strip[0:1], side_strip[rim - 1 : rim]]
         values = ends
         for k in range(few * slot, min(few * slot + few, len(small))):
@@ -155,11 +160,10 @@
             jax.ShapeDtypeStruct(tile.shape, BF),
             jax.ShapeDtypeStruct((slots, depth, channels), BF),
             jax.ShapeDtypeStruct(tile.shape, F32),
-            jax.ShapeDtypeStruct((2, rows, channels), F32),
         ),
         in_specs=[pl.BlockSpec(memory_space=pltpu.SMEM)]
         + [pl.BlockSpec(memory_space=pltpu.VMEM)] * 11,
-        out_specs=(pl.BlockSpec(memory_space=pltpu.VMEM),) * 4,
+        out_specs=(pl.BlockSpec(memory_space=pltpu.VMEM),) * 3,
         scratch_shapes=[pltpu.VMEM((rows + 2, columns + 8, channels), F32)],
         compiler_params=pltpu.CompilerParams(vmem_limit_bytes=24 * 1024 * 1024),
         name="block",
@@ -208,17 +212,119 @@
     )(got)
 
 
-def pick(wanted, held, cells):
-    chosen = (wanted[:, None] == held[None, :]).astype(BF)
-    return jnp.dot(chosen, cells, preferred_element_type=F32).astype(BF)
-
-
-def swap(slots, axes):
-    return lax.all_to_all(slots, axes, 0, 0)
+def swap(slots, groups):
+    return lax.all_to_all(slots, ("face", "row", "col"), 0, 0, axis_index_groups=groups)
 
 
 def at(slots, index):
     return lax.dynamic_index_in_dim(slots, index, 0, keepdims=False)
+
+
+def plane_and_line_groups(side):
+    cut = math.isqrt(side)
+    steps = range(cut)
+
+    def device(f, y, x, high, low):
+        return (f * side + y * cut + low) * side + high * cut + x
+
+    planes = [
+        [device(f, y, x, high, low) for f in range(2) for y in steps for x in steps]
+        for high in steps
+        for low in steps
+    ]
+    lines = [
+        [device(f, y, x, high, low) for high in steps for low in steps]
+        for f in range(2)
+        for y in steps
+        for x in steps
+    ]
+    return planes, lines
+
+
+def frame_sources(adjacency, f, y, x, sender, target, side, cells, stride, rims):
+    cut = math.isqrt(side)
+    last = side - 1
+    width = side * cells
+    high, low = sender // cut, sender % cut
+    row, col = y * cut + target % cut, target // cut * cut + x
+    step = jnp.arange(cells + 2, dtype=jnp.int32) - 1
+    high, low, row, col = (jnp.asarray(v)[..., None] for v in (high, low, row, col))
+
+    def held(face, tile_row, tile_col, part, cell, valid, virtual):
+        valid = valid & (tile_row % cut == low) & (tile_col // cut == high)
+        slot = face * side + tile_row // cut * cut + tile_col % cut
+        index = slot * stride + part * cells + cell
+        if rims:
+            end = slot * stride + 2 * cells + 2 * part + jnp.where(cell == 0, 0, 1)
+            index = jnp.where(virtual, end, index)
+        return jnp.where(valid, index, -1)
+
+    virtual = (step < 0) | (step >= cells)
+
+    def glued(edge, along, on_rows):
+        entry = adjacency[f, edge]
+        position = along * cells + step
+        turned = jnp.where(entry[2] == 1, width - 1 - position, position)
+        valid = (position >= 0) & (position < width)
+        tile, cell = turned // cells, turned % cells
+        if on_rows:
+            end = jnp.where(entry[1] == 2, 0, last)
+            return held(1 - f, tile, end, 1, cell, valid, virtual)
+        end = jnp.where(entry[1] == 0, 0, last)
+        return held(1 - f, end, tile, 0, cell, valid, virtual)
+
+    def beside(next_row, far_cell, own_part):
+        position = col * cells + step
+        valid = (position >= 0) & (position < width)
+        tile, cell = position // cells, position % cells
+        level = next_row // cut == y
+        own = level & ~virtual
+        part = jnp.where(own, own_part, 0)
+        cell = jnp.where(level & virtual, far_cell, cell)
+        return held(f, next_row, tile, part, cell, valid, virtual)
+
+    top = jnp.where(row == 0, glued(0, col, True), beside(row - 1, cells - 1, 1))
+    bottom = jnp.where(row == last, glued(1, col, True), beside(row + 1, 0, 0))
+    west = jnp.where(
+        col == 0, glued(2, row, False), held(f, row, col - 1, 0, step, ~virtual, virtual)
+    )
+    east = jnp.where(
+        col == last, glued(3, row, False), held(f, row, col + 1, 0, step, ~virtual, virtual)
+    )
+    west = jnp.where(x == 0, west, -1)
+    east = jnp.where(x == cut - 1, east, -1)
+    return [top, bottom, west, east]
+
+
+def two_sides(sources):
+    need = [jnp.any(source >= 0, axis=-1) for source in sources]
+    near = jnp.where(need[0], 0, jnp.where(need[1], 1, jnp.where(need[2], 2, 3)))
+    after_one = jnp.where(need[2], 2, 3)
+    far = jnp.where(
+        need[0], jnp.where(need[1], 1, after_one), jnp.where(need[1], after_one, jnp.where(need[2], 3, 2))
+    )
+    return near, far
+
+
+def slot_order(near, far):
+    return jnp.concatenate(
+        [
+            near[..., 1:-1],
+            far[..., 1:-1],
+            near[..., :1],
+            near[..., -1:],
+            far[..., :1],
+            far[..., -1:],
+            jnp.full(near.shape[:-1] + (4,), -1, jnp.int32),
+        ],
+        axis=-1,
+    )
+
+
+def picked(wanted, held):
+    chosen = (wanted.reshape(-1, 1) == jnp.arange(held.shape[0], dtype=jnp.int32)).astype(BF)
+    cells = jnp.dot(chosen, held, preferred_element_type=F32).astype(BF)
+    return cells.reshape(wanted.shape + held.shape[1:])
 
 
 def on_device(
@@ -240,79 +346,79 @@
     hid = expand_weight.shape[1]
     side = lax.axis_size("row")
     width = side * cells
-    lanes = ("face", "row")
+    rim = cells + 2
+    cut = math.isqrt(side)
     f = lax.axis_index("face")
     r = lax.axis_index("row")
     c = lax.axis_index("col")
-    last = side - 1
-    base = f * side
-    other = (1 - f) * side
-    up, down = base + jnp.maximum(r - 1, 0), base + jnp.minimum(r + 1, last)
-    west_of, east_of = jnp.maximum(c - 1, 0), jnp.minimum(c + 1, last)
-
-    slot = jnp.arange(2 * side)
-    first = jnp.where(slot // side == f, slot % side < r, r == 0)[:, None, None]
-    column = jnp.arange(side)
-    adjacent = (jnp.abs(column - c) == 1)[:, None, None]
-    lower = (column < c)[:, None, None]
-    at_first, at_last = (column == 0)[:, None, None], (column == last)[:, None, None]
-    edge_col = (c == 0) | (c == last)
-
-    row_entry = jnp.where(r == 0, adjacency[f, 0], adjacency[f, 1])
-    row_source = jnp.where(row_entry[1] == 2, 0, last)
-    west_entry, east_entry = adjacency[f, 2], adjacency[f, 3]
-
-    def turned(position, entry):
-        return jnp.where(entry[2] == 1, width - 1 - position, position)
-
-    def column_parts(halo_low, halo_high, row_windows, west_window, east_window):
-        near = jnp.where(adjacent, jnp.where(lower, halo_low, halo_high), row_windows)
-        far = jnp.where(at_first, west_window, jnp.where(at_last, east_window, row_windows))
-        return near, far
-
-    wide = jnp.arange(cells + 2) - 1
-    thin = jnp.arange(cells)
-
-    sent = jnp.concatenate(
-        [
-            jnp.where(first, tile[0], tile[cells - 1]),
-            jnp.broadcast_to(
-                jnp.where(c == 0, tile[:, 0], tile[:, cells - 1]), (2 * side, cells, channels)
-            ),
-        ],
-        axis=1,
-    )
-    got = swap(sent, lanes)
-    north, south = at(got, up)[:cells], at(got, down)[:cells]
-    line = lax.dynamic_slice_in_dim(got, other, side, 0)[:, cells:].reshape(width, channels)
-    ends = (at(got, other)[:cells], at(got, other + last)[:cells])
-
-    row_wanted = turned((column[:, None] * cells + wide[None, :]).reshape(-1), row_entry)
-    row_windows = pick(row_wanted, jnp.arange(width), line).reshape(side, cells + 2, channels)
-    side_windows = []
-    for entry in (west_entry, east_entry):
-        strip = jnp.where(entry[1] == 0, ends[0], ends[1])
-        side_windows.append(pick(turned(r * cells + wide, entry), c * cells + thin, strip))
-    near, far = column_parts(
-        jnp.concatenate([north[:1], tile[:, 0], south[:1]]),
-        jnp.concatenate([north[cells - 1 :], tile[:, cells - 1], south[cells - 1 :]]),
-        row_windows,
-        side_windows[0],
-        side_windows[1],
-    )
-    rim = cells + 2
-    got = swap(jnp.concatenate([near, far], axis=1), "col")
-    rim_col = jnp.sum(got[:, rim:].astype(F32), axis=0).astype(BF)
-    from_source = at(got, row_source)
-    rim_row = jnp.where(edge_col, from_source[:rim], from_source[rim:])
-    west = jnp.where(c == 0, rim_col, at(got, west_of)[:rim])
-    east = jnp.where(c == last, rim_col, at(got, east_of)[:rim])
-    top = jnp.where(r == 0, rim_row, jnp.concatenate([west[:1], north, east[:1]]))
-    bottom = jnp.where(r == last, rim_row, jnp.concatenate([west[rim - 1 :], south, east[rim - 1 :]]))
+    y, x = r // cut, c % cut
+    place = c // cut * cut + r % cut
+    planes, lines = plane_and_line_groups(side)
+    line_slots = jnp.arange(side, dtype=jnp.int32)
+
+    def wanted(stride, rims):
+        sources = frame_sources(
+            adjacency, f, y, x, place, line_slots, side, cells, stride, rims
+        )
+        near, far = two_sides(sources)
+
+        def chosen(which):
+            which = which[:, None]
+            return jnp.where(
+                which == 0,
+                sources[0],
+                jnp.where(which == 1, sources[1], jnp.where(which == 2, sources[2], sources[3])),
+            )
+
+        return slot_order(chosen(near), chosen(far))
+
+    near, far = two_sides(
+        frame_sources(adjacency, f, y, x, line_slots, place, side, cells, 2 * cells, False)
+    )
+    step = jnp.arange(rim, dtype=jnp.int32)
+    arrival = slot_order(near[:, None] * rim + step, far[:, None] * rim + step)
+    frame_rows = jnp.arange(4 * rim, dtype=jnp.int32)[:, None]
+    gather_frame = (frame_rows == arrival.reshape(1, -1)).astype(BF)
+
+    def frame_of(strips):
+        flat = strips.reshape(-1, channels)
+        return jnp.dot(gather_frame, flat, preferred_element_type=F32).reshape(4, rim, channels)
+
+    def direct(strips, frame):
+        base = f * side + y * cut
+        west = at(strips, base + jnp.maximum(x - 1, 0)).astype(F32)
+        east = at(strips, base + jnp.minimum(x + 1, cut - 1)).astype(F32)
+        return jnp.where(x == 0, frame[2], west), jnp.where(x == cut - 1, frame[3], east)
+
+    slot = jnp.arange(2 * side, dtype=jnp.int32)[:, None, None]
+    same, slot_y, slot_x = slot // side == f, slot % side // cut, slot % cut
+    top_row, bottom_row = tile[0], tile[cells - 1]
+    first_col, last_col = tile[:, 0], tile[:, cells - 1]
+    upper = jnp.where(same, slot_y <= y, r == 0)
+    level = same & (slot_y == y)
+    near_strip = jnp.where(
+        level & (slot_x == (x + cut - 1) % cut),
+        first_col,
+        jnp.where(
+            level & (slot_x == (x + 1) % cut), last_col, jnp.where(upper, top_row, bottom_row)
+        ),
+    )
+    far_strip = jnp.where(same, bottom_row, jnp.where(c == 0, first_col, last_col))
+    got = swap(jnp.concatenate([near_strip, far_strip], axis=1), planes)
+    passed = picked(wanted(2 * cells, False), got.reshape(-1, channels))
+    frame = frame_of(swap(passed, lines))
+    west, east = direct(got[:, :cells], frame[:, 1:-1])
+    ends = frame[2:, ::rim - 1]
+    top = jnp.concatenate(
+        [frame[0, :1] + ends[0, :1], frame[0, 1:-1], frame[0, -1:] + ends[1, :1]]
+    ).astype(BF)
+    bottom = jnp.concatenate(
+        [frame[1, :1] + ends[0, 1:], frame[1, 1:-1], frame[1, -1:] + ends[1, 1:]]
+    ).astype(BF)
     padded = jnp.concatenate(
         [
             top[None],
-            jnp.concatenate([west[1:-1, None], tile, east[1:-1, None]], axis=1),
+            jnp.concatenate([west.astype(BF)[:, None], tile, east.astype(BF)[:, None]], axis=1),
             bottom[None],
         ]
     )
@@ -320,8 +426,9 @@
     small_count = 13 + hid // channels
     many = 2 * hid // (2 * side)
     few = -(-small_count // (2 * side))
-    extra = -(-(2 * few + 4) // 8) * 8
-    block_out, sent, base_grad, edge_cols = block_on_tile(
+    extra = 8
+    assert 2 * few <= 4
+    block_out, sent, base_grad = block_on_tile(
         jnp.stack([f, r, c]).astype(jnp.int32),
         padded,
         tile,
@@ -337,82 +444,49 @@
         2 * side,
         many + 2 * cells + extra,
     )
-    got = swap(sent, lanes)
-    near_at, far_at, rest_at = many, many + cells, many + 2 * cells
-
-    def packed(small):
+    got = swap(sent, planes)
+
+    def pairs(small):
         high = small.astype(BF)
         low = (small - high.astype(F32)).astype(BF)
-        pairs = jnp.stack([high, low], axis=-2).reshape(2 * few, channels)
-        return jnp.pad(pairs, ((0, 8 * (-(-few // 4)) - 2 * few), (0, 0)))
+        return jnp.stack([high, low], axis=-2).reshape(2 * few, channels)
 
     def small_total(rest):
-        pairs = jnp.sum(rest.astype(F32), axis=0).reshape(few, 2, channels)
-        return pairs[:, 0] + pairs[:, 1]
-
+        sums = jnp.sum(rest.astype(F32), axis=0).reshape(few, 2, channels)
+        return sums[:, 0] + sums[:, 1]
+
+    spare = many + 2 * cells + 4
     weights = jnp.sum(got[:, :many].astype(F32), axis=0)
-    small = small_total(got[:, rest_at + 4 : rest_at + 4 + 2 * few])
-
-    def strip(part, main, spare):
-        return jnp.concatenate(
-            [
-                part[..., rest_at + spare : rest_at + spare + 1, :],
-                part[..., main : main + cells, :],
-                part[..., rest_at + spare + 1 : rest_at + spare + 2, :],
-            ],
-            axis=-2,
-        )
-
-    north = jnp.where(r == 0, 0, strip(at(got, up), near_at, 0).astype(F32))
-    south = jnp.where(r == last, 0, strip(at(got, down), near_at, 0).astype(F32))
-    line = strip(lax.dynamic_slice_in_dim(got, other, side, 0), far_at, 2).reshape(
-        side * rim, channels
-    )
-    ends = (strip(at(got, other), near_at, 0), strip(at(got, other + last), near_at, 0))
-
-    row_wanted = turned(jnp.arange(width), row_entry)
-    held = (column[:, None] * cells + wide[None, :]).reshape(-1)
-    row_windows = pick(row_wanted, held, line).reshape(side, cells, channels)
-    side_windows = []
-    for entry in (west_entry, east_entry):
-        strip = jnp.where(entry[1] == 0, ends[0], ends[1])
-        side_windows.append(pick(turned(r * cells + thin, entry), c * cells + wide, strip))
-
-    def folded(end, col):
-        whole = edge_cols[end]
-        return jnp.concatenate(
-            [whole[:1] + north[col][None], whole[1:-1], whole[-1:] + south[col][None]]
-        ).astype(BF)
-
-    near, far = column_parts(
-        folded(0, 0), folded(1, rim - 1), row_windows, side_windows[0], side_windows[1]
-    )
-    rest = packed(small)
+    small = small_total(got[:, spare : spare + 2 * few])
+    strips = got[:, many:]
+    passed = picked(wanted(2 * cells + extra, True), strips.reshape(-1, channels))
+    tail = jnp.pad(pairs(small), ((0, 4 - 2 * few), (0, 0)))
     sent = jnp.concatenate(
         [
             jnp.broadcast_to(weights.astype(BF), (side, many, channels)),
-            near,
-            far,
-            jnp.broadcast_to(rest, (side,) + rest.shape),
+            passed[:, : 2 * cells],
+            jnp.concatenate(
+                [passed[:, 2 * cells : 2 * cells + 4], jnp.broadcast_to(tail, (side, 4, channels))],
+                axis=1,
+            ),
         ],
         axis=1,
     )
-    got = swap(sent, "col")
+    got = swap(sent, lines)
     weights = jnp.sum(got[:, :many].astype(F32), axis=0) / width
-    small = small_total(got[:, rest_at : rest_at + 2 * few]) / width
-    share = jnp.concatenate([weights.astype(BF), packed(small)])
-    spread = swap(jnp.broadcast_to(share, (2 * side,) + share.shape), lanes)
-
-    near, far = got[:, near_at:far_at], got[:, far_at:rest_at]
-    rim_col = jnp.sum(far.astype(F32), axis=0)
-    rim_row = jnp.where(edge_col, at(near, row_source), at(far, row_source)).astype(F32)
-    west = jnp.where(c == 0, rim_col, at(near, west_of).astype(F32))
-    east = jnp.where(c == last, rim_col, at(near, east_of).astype(F32))
-    north = jnp.where(r == 0, rim_row, north[1:-1])
-    south = jnp.where(r == last, rim_row, south[1:-1])
+    small = small_total(got[:, spare : spare + 2 * few]) / width
+    share = jnp.concatenate(
+        [weights.astype(BF), jnp.pad(pairs(small), ((0, 8 - 2 * few), (0, 0)))]
+    )
+    spread = swap(jnp.broadcast_to(share, (2 * side,) + share.shape), planes)
+
+    frame = frame_of(got[:, many:])
+    folded = frame[:, 1:-1]
+    folded = folded.at[:, 0].add(frame[:, 0]).at[:, -1].add(frame[:, -1])
+    west, east = direct(strips[:, :cells], folded)
     in_grad = base_grad
-    in_grad = in_grad + jnp.pad(north[None], ((0, cells - 1), (0, 0), (0, 0)))
-    in_grad = in_grad + jnp.pad(south[None], ((cells - 1, 0), (0, 0), (0, 0)))
+    in_grad = in_grad + jnp.pad(folded[:1], ((0, cells - 1), (0, 0), (0, 0)))
+    in_grad = in_grad + jnp.pad(folded[1:2], ((cells - 1, 0), (0, 0), (0, 0)))
     in_grad = in_grad + jnp.pad(west[:, None], ((0, 0), (0, cells - 1), (0, 0)))
     in_grad = in_grad + jnp.pad(east[:, None], ((0, 0), (cells - 1, 0), (0, 0)))
 

time: 133 us -> 119 us (0.89)
  blocking collectives: 18.1 us -> 0 us
  other arithmetic: 3.3 us -> 5.1 us
  between operations: 5.12 us -> 6.91 us
  local copies, waits for them, and re-layouts: 6.99 us -> 5.23 us
    all_to_all x1 -> x0, blocking collectives: 18.1 us -> none  [swap(): return lax.all_to_all(slots, axes, 0, 0)]
    unnamed x22 -> x24, local copies, waits for them, and re-layouts: 2.67 us -> 0.06 us
    all_to_all x4 -> x5, starting transfers between devices: 48.6 us -> 49.9 us  [swap(): lax.all_to_all(slots, ('face', 'row', 'col'), 0, 0, axis_index_groups=gro...]
    all_to_all x4 -> x5, waiting for transfers between devices: 44.9 us -> 44.9 us  [swap(): lax.all_to_all(slots, ('face', 'row', 'col'), 0, 0, axis_index_groups=gro...]
  transfers between devices with their start and end apart: 4 -> 5, of which waited for: 4 -> 4; matrix products, arithmetic and copies ran while one was open for 2% -> 4% of each run, Pallas kernels for 0% -> 0%
where the time goes in v3:
time: 119 us; the launch traced here: 118 us
  starting transfers between devices  49.9 us (42%)
  waiting for transfers between devices  44.9 us (38%)
  between operations  6.91 us (6%)
  local copies, waits for them, and re-layouts  5.23 us (4%)
  other arithmetic  5.1 us (4%)
  Pallas kernels  3.59 us (3%)
  matrix products  2.43 us (2%)
    all_to_all x5, starting transfers between devices, swap(): lax.all_to_all(slots, ('face', 'row', 'col'), 0, 0, axis_index_groups=gro...  49.9 us
    all_to_all x5, waiting for transfers between devices, swap(): lax.all_to_all(slots, ('face', 'row', 'col'), 0, 0, axis_index_groups=gro...  44.9 us
    pallas_call x1, Pallas kernels, block_on_tile(): pl.pallas_call(block_kernel, out_shape=(jax.ShapeDtypeStruct(tile.shape,...  2.76 us
  transfers between devices with their start and end apart: 5, of which 4 were waited for; matrix products, arithmetic and copies ran while one was open for 4% of the time, Pallas kernels for 0%

profile of v3, /device:TPU:1, one launch (start us, length us, event | category | flops | bytes accessed | tf_op | source)
XLA Modules:
  0.0 118.0 jit_solution(12881361075515368493)
XLA Ops:
  0.7 0.7 slice_bitcast_fusion.1
  1.4 0.8 fusion.141
  2.5 0.7 pad_maximum_fusion.1
  3.2 10.5 %all-to-all-start = ((bf16[32,32,128]{2,1,0:T(8,128)(2,1)}), bf16[32,32,128]{2,1,0:T(8,128)(2,1)S(1)}, u32[]{:S(2)}, u32[]{:S(2)}) async-start(bf16[32,32,128]{2,1,0:T(8,128)(2,1)} %pad_maximum_fusion.1), calls=%async_computation | async-start | bytes 524288 | tf_op jit(solution)/shard_map/all_to_all | solution.py:216
  14.1 0.7 constant_dynamic-slice_fusion.5
  20.4 0.2 compare_reduce_fusion.1
  20.6 0.2 compare_reduce_fusion.2
  23.0 1.3 %fusion.4 = bf16[640,128]{1,0:T(8,128)(2,1)} fusion(bf16[1024,128]{1,0:T(8,128)(2,1)S(1)} %bitcast.100, s32[640]{0:T(1024)S(1)} %eq.893), kind=kOutput, calls=%fused_computation.6 | convolution fusion | flops 168509440 | bytes 428544 | tf_op jit(solution)/shard_map/dot_general | solution.py:326
  24.4 13.2 %all-to-all-start.1 = ((bf16[16,40,128]{2,1,0:T(8,128)(2,1)}), bf16[16,40,128]{2,1,0:T(8,128)(2,1)S(1)}, u32[]{:S(2)}, u32[]{:S(2)}) async-start(bf16[16,40,128]{2,1,0:T(8,128)(2,1)} %bitcast.39), calls=%async_computation.1 | async-start | bytes 327680 | tf_op jit(solution)/shard_map/all_to_all | solution.py:216
  37.9 12.2 %all-to-all-done.1 = bf16[16,40,128]{2,1,0:T(8,128)(2,1)S(1)} async-done(((bf16[16,40,128]{2,1,0:T(8,128)(2,1)}), bf16[16,40,128]{2,1,0:T(8,128)(2,1)S(1)}, u32[]{:S(2)}, u32[]{:S(2)}) %all-to-all-start.1) | async-done | bytes 163872 | tf_op jit(solution)/shard_map/all_to_all | solution.py:216
  50.6 2.8 %block.1 = (bf16[16,16,128]{2,1,0:T(8,128)(2,1)}, bf16[32,72,128]{2,1,0:T(8,128)(2,1)}, f32[16,16,128]{2,1,0:T(8,128)S(1)}) custom-call(s32[3]{0:T(128)S(1)} %pad_add_fusion.1.plan_ref, bf16[18,18,128]{2,1,0:T(8,128)(2,1)S(1)} %maximum_maximum_fusion.padded_ref, bf16[16,16,128]{2,1,0:T(8,128)(2,1)S(1)} %bitcast.91, bf16[16,16,128]{2,1,0:T(8,128)(2,1)S(1)} %bitcast.92, ...), custom_call_target="tpu_custom_call" | custom-call | tf_op jit(solution)/shard_map/block/pallas_call | solution.py:157
  53.4 10.2 %all-to-all-start.2 = ((bf16[32,72,128]{2,1,0:T(8,128)(2,1)}), bf16[32,72,128]{2,1,0:T(8,128)(2,1)S(1)}, u32[]{:S(2)}, u32[]{:S(2)}) async-start(bf16[32,72,128]{2,1,0:T(8,128)(2,1)} %get-tuple-element.47), calls=%async_computation.2 | async-start | bytes 1179648 | tf_op jit(solution)/shard_map/all_to_all | solution.py:216
  64.2 11.1 %all-to-all-done.2 = bf16[32,72,128]{2,1,0:T(8,128)(2,1)S(1)} async-done(((bf16[32,72,128]{2,1,0:T(8,128)(2,1)}), bf16[32,72,128]{2,1,0:T(8,128)(2,1)S(1)}, u32[]{:S(2)}, u32[]{:S(2)}) %all-to-all-start.2) | async-done | bytes 589856 | tf_op jit(solution)/shard_map/all_to_all | solution.py:216
  75.4 0.7 fusion.5
  76.3 0.8 pad_maximum_fusion
  77.0 4.8 %all-to-all-start.3 = ((bf16[16,72,128]{2,1,0:T(8,128)(2,1)}), bf16[16,72,128]{2,1,0:T(8,128)(2,1)S(1)}, u32[]{:S(2)}, u32[]{:S(2)}) async-start(bf16[16,72,128]{2,1,0:T(8,128)(2,1)} %pad_maximum_fusion), calls=%async_computation.3 | async-start | bytes 589824 | tf_op jit(solution)/shard_map/all_to_all | solution.py:216
  81.8 13.4 %all-to-all-done.3 = bf16[16,72,128]{2,1,0:T(8,128)(2,1)S(1)} async-done(((bf16[16,72,128]{2,1,0:T(8,128)(2,1)}), bf16[16,72,128]{2,1,0:T(8,128)(2,1)S(1)}, u32[]{:S(2)}, u32[]{:S(2)}) %all-to-all-start.3) | async-done | bytes 294944 | tf_op jit(solution)/shard_map/all_to_all | solution.py:216
  95.2 0.2 fusion.6
  95.7 0.8 broadcast_in_dim.436
  96.5 11.2 %all-to-all-start.4 = ((bf16[32,40,128]{2,1,0:T(8,128)(2,1)}), bf16[32,40,128]{2,1,0:T(8,128)(2,1)S(1)}, u32[]{:S(2)}, u32[]{:S(2)}) async-start(bf16[32,40,128]{2,1,0:T(8,128)(2,1)} %broadcast_in_dim.436), calls=%async_computation.4 | async-start | bytes 655360 | tf_op jit(solution)/shard_map/all_to_all | solution.py:216
  107.7 0.7 fusion.16
  108.4 8.2 %all-to-all-done.4.got_ref = bf16[32,40,128]{2,1,0:T(8,128)(2,1)S(1)} async-done(((bf16[32,40,128]{2,1,0:T(8,128)(2,1)}), bf16[32,40,128]{2,1,0:T(8,128)(2,1)S(1)}, u32[]{:S(2)}, u32[]{:S(2)}) %all-to-all-start.4) | async-done | bytes 327712 | tf_op jit(solution)/shard_map/all_to_all | solution.py:216
  116.6 0.8 finish.1
  117.4 0.6 reshape.1374
  (124 shorter events, 4.4 us)
Async XLA Ops:
  2.5 11.6 %copy-start.11 = (s32[2,4,3]{1,0,2:T(2,128)S(1)}, s32[2,4,3]{1,0,2:T(2,128)}, u32[]{:S(2)}) copy-start(s32[2,4,3]{1,0,2:T(2,128)} %param.24) | copy-start | bytes 292
  3.2 19.8 %all-to-all-start = ((bf16[32,32,128]{2,1,0:T(8,128)(2,1)}), bf16[32,32,128]{2,1,0:T(8,128)(2,1)S(1)}, u32[]{:S(2)}, u32[]{:S(2)}) async-start(bf16[32,32,128]{2,1,0:T(8,128)(2,1)} %pad_maximum_fusion.1), calls=%async_computation | async-start | bytes 524288 | tf_op jit(solution)/shard_map/all_to_all | solution.py:216
  13.7 9.0 %copy-start.10 = (f32[3,3,128]{2,1,0:T(4,128)S(1)}, f32[3,3,128]{2,1,0:T(4,128)}, u32[]{:S(2)}) copy-start(f32[3,3,128]{2,1,0:T(4,128)} %param.16) | copy-start | bytes 13828
  24.3 26.2 %copy-start = (bf16[1,16,16,128]{3,2,1,0:T(8,128)(2,1)S(1)}, bf16[1,16,16,128]{3,2,1,0:T(8,128)(2,1)}, u32[]{:S(2)}) copy-start(bf16[1,16,16,128]{3,2,1,0:T(8,128)(2,1)} %param.15) | copy-start | bytes 196612
  24.3 26.2 %copy-start.1 = (bf16[128,512]{1,0:T(8,128)(2,1)S(1)}, bf16[128,512]{1,0:T(8,128)(2,1)}, u32[]{:S(2)}) copy-start(bf16[128,512]{1,0:T(8,128)(2,1)} %expand_ref.1) | copy-start | bytes 393220
  24.3 26.2 %copy-start.2 = (bf16[512,128]{1,0:T(8,128)(2,1)S(1)}, bf16[512,128]{1,0:T(8,128)(2,1)}, u32[]{:S(2)}) copy-start(bf16[512,128]{1,0:T(8,128)(2,1)} %reduce_ref.1) | copy-start | bytes 393220
  24.3 26.2 %copy-start.3 = (bf16[1,16,16,128]{3,2,1,0:T(8,128)(2,1)S(1)}, bf16[1,16,16,128]{3,2,1,0:T(8,128)(2,1)}, u32[]{:S(2)}) copy-start(bf16[1,16,16,128]{3,2,1,0:T(8,128)(2,1)} %param.25) | copy-start | bytes 196612
  24.3 26.3 %copy-start.4 = (f32[512]{0:T(512)S(1)}, f32[512]{0:T(512)}, u32[]{:S(2)}) copy-start(f32[512]{0:T(512)} %param.21) | copy-start | bytes 6148
  24.3 26.3 %copy-start.5 = (f32[128]{0:T(128)S(1)}, f32[128]{0:T(128)}, u32[]{:S(2)}) copy-start(f32[128]{0:T(128)} %param.17) | copy-start | bytes 1540
  24.3 26.2 %copy-start.6 = (f32[128]{0:T(128)S(1)}, f32[128]{0:T(128)}, u32[]{:S(2)}) copy-start(f32[128]{0:T(128)} %param.18) | copy-start | bytes 1540
  24.3 26.2 %copy-start.7 = (f32[128]{0:T(128)S(1)}, f32[128]{0:T(128)}, u32[]{:S(2)}) copy-start(f32[128]{0:T(128)} %param.19) | copy-start | bytes 1540
  24.4 26.2 %copy-start.8 = (f32[128]{0:T(128)S(1)}, f32[128]{0:T(128)}, u32[]{:S(2)}) copy-start(f32[128]{0:T(128)} %param.23) | copy-start | bytes 1540
  24.4 25.8 %all-to-all-start.1 = ((bf16[16,40,128]{2,1,0:T(8,128)(2,1)}), bf16[16,40,128]{2,1,0:T(8,128)(2,1)S(1)}, u32[]{:S(2)}, u32[]{:S(2)}) async-start(bf16[16,40,128]{2,1,0:T(8,128)(2,1)} %bitcast.39), calls=%async_computation.1 | async-start | bytes 327680 | tf_op jit(solution)/shard_map/all_to_all | solution.py:216
  53.4 21.9 %all-to-all-start.2 = ((bf16[32,72,128]{2,1,0:T(8,128)(2,1)}), bf16[32,72,128]{2,1,0:T(8,128)(2,1)S(1)}, u32[]{:S(2)}, u32[]{:S(2)}) async-start(bf16[32,72,128]{2,1,0:T(8,128)(2,1)} %get-tuple-element.47), calls=%async_computation.2 | async-start | bytes 1179648 | tf_op jit(solution)/shard_map/all_to_all | solution.py:216
  75.3 6.5 %copy-start.9 = (bf16[32,72,128]{2,1,0:T(8,128)(2,1)}, bf16[32,72,128]{2,1,0:T(8,128)(2,1)S(1)}, u32[]{:S(2)}) copy-start(bf16[32,72,128]{2,1,0:T(8,128)(2,1)S(1)} %all-to-all-done.2) | copy-start | bytes 1769476
  77.0 18.2 %all-to-all-start.3 = ((bf16[16,72,128]{2,1,0:T(8,128)(2,1)}), bf16[16,72,128]{2,1,0:T(8,128)(2,1)S(1)}, u32[]{:S(2)}, u32[]{:S(2)}) async-start(bf16[16,72,128]{2,1,0:T(8,128)(2,1)} %pad_maximum_fusion), calls=%async_computation.3 | async-start | bytes 589824 | tf_op jit(solution)/shard_map/all_to_all | solution.py:216
  95.6 12.2 %slice-start = ((bf16[32,72,128]{2,1,0:T(8,128)(2,1)}), bf16[32,16,128]{2,1,0:T(8,128)(2,1)S(1)}, s32[]{:S(2)}) async-start(bf16[32,72,128]{2,1,0:T(8,128)(2,1)} %copy-done.9), calls=%async_computation.5 | async-start | bytes 262144 | tf_op jit(solution)/shard_map/slice | solution.py:486
  96.5 20.1 %all-to-all-start.4 = ((bf16[32,40,128]{2,1,0:T(8,128)(2,1)}), bf16[32,40,128]{2,1,0:T(8,128)(2,1)S(1)}, u32[]{:S(2)}, u32[]{:S(2)}) async-start(bf16[32,40,128]{2,1,0:T(8,128)(2,1)} %broadcast_in_dim.436), calls=%async_computation.4 | async-start | bytes 655360 | tf_op jit(solution)/shard_map/all_to_all | solution.py:216

commit v4 on v3

--- a/solution.py
+++ b/solution.py
@@ -1,3 +1,4 @@
+import functools
 import math
 
 import jax
@@ -21,6 +22,50 @@
         1.0 + 3.0 * 0.044715 * preact * preact
     )
     return (gelu_value, gelu_slope)
+
+
+def slot_strips(face, row, col, slot, side, north, south, west, east):
+    cut = math.isqrt(side)
+    here_y, here_x = row // cut, col % cut
+    same = face == slot // side
+    y, x = slot % side // cut, slot % cut
+    level = jnp.where(
+        x == (here_x + cut - 1) % cut, west, jnp.where(x == (here_x + 1) % cut, east, north)
+    )
+    inner = jnp.where(y < here_y, north, jnp.where(y > here_y, south, level))
+    near = jnp.where(same, inner, jnp.where(row == 0, north, south))
+    far = jnp.where(same, south, jnp.where(col == 0, west, east))
+    return near, far
+
+
+def edges_kernel(place_ref, tile_ref, sent_ref):
+    slots, depth, _ = sent_ref.shape
+    rows = depth // 2
+    tile = tile_ref[...].astype(F32)
+    north, south = tile[0], tile[rows - 1]
+    west = jnp.concatenate([tile[k, 0:1] for k in range(rows)])
+    east = jnp.concatenate([tile[k, rows - 1 : rows] for k in range(rows)])
+    for slot in range(slots):
+        near, far = slot_strips(
+            place_ref[0], place_ref[1], place_ref[2], slot, slots // 2, north, south, west, east
+        )
+        sent_ref[slot, 0:rows] = near.astype(BF)
+        sent_ref[slot, rows:depth] = far.astype(BF)
+
+
+def edges_of(place, tile, slots):
+    rows, _, channels = tile.shape
+    return pl.pallas_call(
+        edges_kernel,
+        out_shape=jax.ShapeDtypeStruct((slots, 2 * rows, channels), BF),
+        in_specs=[
+            pl.BlockSpec(memory_space=pltpu.SMEM),
+            pl.BlockSpec(memory_space=pltpu.VMEM),
+        ],
+        out_specs=pl.BlockSpec(memory_space=pltpu.VMEM),
+        compiler_params=pltpu.CompilerParams(vmem_limit_bytes=8 * 1024 * 1024),
+        name="edges",
+    )(place, tile)
 
 
 def block_kernel(
@@ -121,23 +166,12 @@
     south = wide_ref[rim - 1, 0:rim]
 
     face, row, col = plan_ref[0], plan_ref[1], plan_ref[2]
-    cut = math.isqrt(side)
-    here_y, here_x = row // cut, col % cut
     few = -(-len(small) // slots)
     extra = sent_ref.shape[1] - many - 2 * rows
     place = lax.broadcasted_iota(jnp.int32, (extra, channels), 0)
     near = many + rows
-    edge_row = jnp.where(row == 0, north, south)
-    edge_col = jnp.where(col == 0, west, east)
     for slot in range(slots):
-        same = face == slot // side
-        y, x = slot % side // cut, slot % cut
-        level = jnp.where(
-            x == (here_x + cut - 1) % cut, west, jnp.where(x == (here_x + 1) % cut, east, north)
-        )
-        inner = jnp.where(y < here_y, north, jnp.where(y > here_y, south, level))
-        strip = jnp.where(same, inner, edge_row)
-        side_strip = jnp.where(same, south, edge_col)
+        strip, side_strip = slot_strips(face, row, col, slot, side, north, south, west, east)
         sent_ref[slot, many:near] = strip[1 : rim - 1].astype(BF)
         sent_ref[slot, near : near + rows] = side_strip[1 : rim - 1].astype(BF)
         ends = [strip[0:1], strip[rim - 1 : rim], side_strip[0:1], side_strip[rim - 1 : rim]]
@@ -170,6 +204,40 @@
     )(plan, padded, tile, grad, taps, *params[:-2])
 
 
+def share_kernel(scale, few, got_ref, share_ref):
+    slots, depth, channels = share_ref.shape
+    many = depth - 8
+    spare = got_ref.shape[1] - 4
+    weights = jnp.zeros((many, channels), F32)
+    rest = jnp.zeros((4, channels), F32)
+    for k in range(got_ref.shape[0]):
+        weights = weights + got_ref[k, 0:many].astype(F32)
+        rest = rest + got_ref[k, spare - 4 : spare + 4].astype(F32)[4:8]
+    weights = (weights * scale).astype(BF)
+    place = lax.broadcasted_iota(jnp.int32, (8, channels), 0)
+    block = jnp.zeros((8, channels), F32)
+    for k in range(few):
+        small = (rest[2 * k : 2 * k + 1] + rest[2 * k + 1 : 2 * k + 2]) * scale
+        high = small.astype(BF).astype(F32)
+        block = jnp.where(place == 2 * k, high, jnp.where(place == 2 * k + 1, small - high, block))
+    block = block.astype(BF)
+    for slot in range(slots):
+        share_ref[slot, 0:many] = weights
+        share_ref[slot, many:depth] = block
+
+
+def share_of(got, slots, many, few, scale):
+    channels = got.shape[2]
+    return pl.pallas_call(
+        functools.partial(share_kernel, scale, few),
+        out_shape=jax.ShapeDtypeStruct((slots, many + 8, channels), BF),
+        in_specs=[pl.BlockSpec(memory_space=pltpu.VMEM)],
+        out_specs=pl.BlockSpec(memory_space=pltpu.VMEM),
+        compiler_params=pltpu.CompilerParams(vmem_limit_bytes=8 * 1024 * 1024),
+        name="share",
+    )(got)
+
+
 def finish_kernel(got_ref, *out_refs):
     tap_ref, bias_ref, gain_ref, shift_ref, expand_ref, expand_bias_ref, reduce_ref, reduce_bias_ref = (
         out_refs
@@ -189,7 +257,7 @@
         rest = got_ref[slot, many:depth].astype(F32)
         small += [rest[2 * k : 2 * k + 1] + rest[2 * k + 1 : 2 * k + 2] for k in range(few)]
     for k in range(9):
-        tap_ref[k : k + 1] = small[k]
+        tap_ref[k // 3, k % 3 : k % 3 + 1] = small[k]
     bias_ref[...] = small[9]
     gain_ref[...] = small[10]
     shift_ref[...] = small[11]
@@ -200,7 +268,7 @@
 
 def finish(got, hid):
     channels = got.shape[2]
-    shapes = [(9, channels)] + [(1, channels)] * 3
+    shapes = [(3, 3, channels)] + [(1, channels)] * 3
     shapes += [(channels, hid), (1, hid), (hid, channels), (1, channels)]
     return pl.pallas_call(
         finish_kernel,
@@ -241,63 +309,58 @@
     return planes, lines
 
 
-def frame_sources(adjacency, f, y, x, sender, target, side, cells, stride, rims):
+def frame_sources(entries, f, y, x, sender, target, step, side, cells):
     cut = math.isqrt(side)
-    last = side - 1
-    width = side * cells
-    high, low = sender // cut, sender % cut
-    row, col = y * cut + target % cut, target // cut * cut + x
-    step = jnp.arange(cells + 2, dtype=jnp.int32) - 1
-    high, low, row, col = (jnp.asarray(v)[..., None] for v in (high, low, row, col))
-
-    def held(face, tile_row, tile_col, part, cell, valid, virtual):
-        valid = valid & (tile_row % cut == low) & (tile_col // cut == high)
-        slot = face * side + tile_row // cut * cut + tile_col % cut
-        index = slot * stride + part * cells + cell
-        if rims:
-            end = slot * stride + 2 * cells + 2 * part + jnp.where(cell == 0, 0, 1)
-            index = jnp.where(virtual, end, index)
-        return jnp.where(valid, index, -1)
-
+    last, width, low_bits, cell_bits = side - 1, side * cells, cut - 1, cells - 1
+    shift, cell_shift = low_bits.bit_length(), cell_bits.bit_length()
+    high, low = sender >> shift, sender & low_bits
+    row, col = y * cut + (target & low_bits), (target >> shift) * cut + x
     virtual = (step < 0) | (step >= cells)
 
+    def held(face, tile_row, tile_col, part, cell, valid):
+        valid = valid & ((tile_row & low_bits) == low) & ((tile_col >> shift) == high)
+        slot = face * side + ((tile_row >> shift) << shift) + (tile_col & low_bits)
+        inner = part * cells + cell
+        end = 2 * cells + 2 * part + jnp.where(cell == 0, 0, 1)
+        inner_index = slot * (2 * cells) + inner
+        end_index = slot * (2 * cells + 8) + jnp.where(virtual, end, inner)
+        return jnp.where(valid, inner_index, -1), jnp.where(valid, end_index, -1)
+
     def glued(edge, along, on_rows):
-        entry = adjacency[f, edge]
+        other_edge, reverse = entries[edge]
         position = along * cells + step
-        turned = jnp.where(entry[2] == 1, width - 1 - position, position)
+        turned = jnp.where(reverse == 1, width - 1 - position, position)
         valid = (position >= 0) & (position < width)
-        tile, cell = turned // cells, turned % cells
+        tile, cell = turned >> cell_shift, turned & cell_bits
         if on_rows:
-            end = jnp.where(entry[1] == 2, 0, last)
-            return held(1 - f, tile, end, 1, cell, valid, virtual)
-        end = jnp.where(entry[1] == 0, 0, last)
-        return held(1 - f, end, tile, 0, cell, valid, virtual)
+            end = jnp.where(other_edge == 2, 0, last)
+            return held(1 - f, tile, end, 1, cell, valid)
+        end = jnp.where(other_edge == 0, 0, last)
+        return held(1 - f, end, tile, 0, cell, valid)
 
     def beside(next_row, far_cell, own_part):
         position = col * cells + step
         valid = (position >= 0) & (position < width)
-        tile, cell = position // cells, position % cells
-        level = next_row // cut == y
-        own = level & ~virtual
-        part = jnp.where(own, own_part, 0)
+        tile, cell = position >> cell_shift, position & cell_bits
+        level = (next_row >> shift) == y
+        part = jnp.where(level & (step >= 0) & (step < cells), own_part, 0)
         cell = jnp.where(level & virtual, far_cell, cell)
-        return held(f, next_row, tile, part, cell, valid, virtual)
-
-    top = jnp.where(row == 0, glued(0, col, True), beside(row - 1, cells - 1, 1))
-    bottom = jnp.where(row == last, glued(1, col, True), beside(row + 1, 0, 0))
-    west = jnp.where(
-        col == 0, glued(2, row, False), held(f, row, col - 1, 0, step, ~virtual, virtual)
-    )
-    east = jnp.where(
-        col == last, glued(3, row, False), held(f, row, col + 1, 0, step, ~virtual, virtual)
-    )
-    west = jnp.where(x == 0, west, -1)
-    east = jnp.where(x == cut - 1, east, -1)
-    return [top, bottom, west, east]
+        return held(f, next_row, tile, part, cell, valid)
+
+    def either(condition, first, second):
+        return tuple(jnp.where(condition, p, q) for p, q in zip(first, second))
+
+    inner = (step >= 0) & (step < cells)
+    nothing = (-1, -1)
+    top = either(row == 0, glued(0, col, True), beside(row - 1, cells - 1, 1))
+    bottom = either(row == last, glued(1, col, True), beside(row + 1, 0, 0))
+    west = either(col == 0, glued(2, row, False), held(f, row, col - 1, 0, step, inner))
+    east = either(col == last, glued(3, row, False), held(f, row, col + 1, 0, step, inner))
+    return [top, bottom, either(x == 0, west, nothing), either(x == cut - 1, east, nothing)]
 
 
 def two_sides(sources):
-    need = [jnp.any(source >= 0, axis=-1) for source in sources]
+    need = [jnp.max(source[1].astype(F32), axis=-1, keepdims=True) >= 0.0 for source in sources]
     near = jnp.where(need[0], 0, jnp.where(need[1], 1, jnp.where(need[2], 2, 3)))
     after_one = jnp.where(need[2], 2, 3)
     far = jnp.where(
@@ -306,19 +369,55 @@
     return near, far
 
 
-def slot_order(near, far):
-    return jnp.concatenate(
-        [
-            near[..., 1:-1],
-            far[..., 1:-1],
-            near[..., :1],
-            near[..., -1:],
-            far[..., :1],
-            far[..., -1:],
-            jnp.full(near.shape[:-1] + (4,), -1, jnp.int32),
-        ],
-        axis=-1,
-    )
+def plan_arrays(entries, f, r, c, side, cells):
+    cut = math.isqrt(side)
+    y, x = r // cut, c % cut
+    here = c // cut * cut + r % cut
+    others = lax.broadcasted_iota(jnp.int32, (side, 128), 0)
+    lane = lax.broadcasted_iota(jnp.int32, (side, 128), 1)
+    main = lane < 2 * cells
+    step = jnp.where(main, lane & (cells - 1), jnp.where((lane & 1) == 0, -1, cells))
+    second = jnp.where(main, lane - cells, lane - 2 * cells - 2) >= 0
+    used = lane < 2 * cells + 4
+    sources = frame_sources(entries, f, y, x, here, others, step, side, cells)
+    near, far = two_sides(sources)
+    which = jnp.where(second, far, near)
+    passed = []
+    for form in range(2):
+        index = jnp.where(
+            which == 0,
+            sources[0][form],
+            jnp.where(
+                which == 1, sources[1][form], jnp.where(which == 2, sources[2][form], sources[3][form])
+            ),
+        )
+        passed.append(jnp.where(used, index, -1))
+    sources = frame_sources(entries, f, y, x, others, here, step, side, cells)
+    near, far = two_sides(sources)
+    which = jnp.where(second, far, near)
+    return passed[0], passed[1], jnp.where(used, which * (cells + 2) + step + 1, -1)
+
+
+def plan_kernel(side, cells, place_ref, adjacency_ref, plan_ref):
+    f = place_ref[0]
+    entries = [
+        (adjacency_ref[f * 12 + 3 * edge + 1], adjacency_ref[f * 12 + 3 * edge + 2])
+        for edge in range(4)
+    ]
+    arrays = plan_arrays(entries, f, place_ref[1], place_ref[2], side, cells)
+    for k, array in enumerate(arrays):
+        plan_ref[k] = array
+
+
+def plan_of(place, adjacency, side, cells):
+    return pl.pallas_call(
+        functools.partial(plan_kernel, side, cells),
+        out_shape=jax.ShapeDtypeStruct((3, side, 128), jnp.int32),
+        in_specs=[pl.BlockSpec(memory_space=pltpu.SMEM)] * 2,
+        out_specs=pl.BlockSpec(memory_space=pltpu.VMEM),
+        compiler_params=pltpu.CompilerParams(vmem_limit_bytes=4 * 1024 * 1024),
+        name="plan",
+    )(place, adjacency.reshape(-1))
 
 
 def picked(wanted, held):
@@ -352,36 +451,22 @@
     r = lax.axis_index("row")
     c = lax.axis_index("col")
     y, x = r // cut, c % cut
-    place = c // cut * cut + r % cut
     planes, lines = plane_and_line_groups(side)
-    line_slots = jnp.arange(side, dtype=jnp.int32)
-
-    def wanted(stride, rims):
-        sources = frame_sources(
-            adjacency, f, y, x, place, line_slots, side, cells, stride, rims
-        )
-        near, far = two_sides(sources)
-
-        def chosen(which):
-            which = which[:, None]
-            return jnp.where(
-                which == 0,
-                sources[0],
-                jnp.where(which == 1, sources[1], jnp.where(which == 2, sources[2], sources[3])),
-            )
-
-        return slot_order(chosen(near), chosen(far))
-
-    near, far = two_sides(
-        frame_sources(adjacency, f, y, x, line_slots, place, side, cells, 2 * cells, False)
-    )
-    step = jnp.arange(rim, dtype=jnp.int32)
-    arrival = slot_order(near[:, None] * rim + step, far[:, None] * rim + step)
+    place = jnp.stack([f, r, c]).astype(jnp.int32)
+    few = -(-(13 + hid // channels) // (2 * side))
+    extra = 8
+    assert 2 * few <= 4 and cells & (cells - 1) == 0 and cut & (cut - 1) == 0
+
+    plan = plan_of(place, adjacency, side, cells)
+    inner_wanted = plan[0, :, : 2 * cells + 4]
+    end_wanted = plan[1, :, : 2 * cells + extra]
     frame_rows = jnp.arange(4 * rim, dtype=jnp.int32)[:, None]
-    gather_frame = (frame_rows == arrival.reshape(1, -1)).astype(BF)
 
     def frame_of(strips):
+        depth = strips.shape[1]
+        arrival = plan[2, :, :depth].reshape(1, -1)
         flat = strips.reshape(-1, channels)
+        gather_frame = (frame_rows == arrival).astype(BF)
         return jnp.dot(gather_frame, flat, preferred_element_type=F32).reshape(4, rim, channels)
 
     def direct(strips, frame):
@@ -390,23 +475,10 @@
         east = at(strips, base + jnp.minimum(x + 1, cut - 1)).astype(F32)
         return jnp.where(x == 0, frame[2], west), jnp.where(x == cut - 1, frame[3], east)
 
-    slot = jnp.arange(2 * side, dtype=jnp.int32)[:, None, None]
-    same, slot_y, slot_x = slot // side == f, slot % side // cut, slot % cut
-    top_row, bottom_row = tile[0], tile[cells - 1]
-    first_col, last_col = tile[:, 0], tile[:, cells - 1]
-    upper = jnp.where(same, slot_y <= y, r == 0)
-    level = same & (slot_y == y)
-    near_strip = jnp.where(
-        level & (slot_x == (x + cut - 1) % cut),
-        first_col,
-        jnp.where(
-            level & (slot_x == (x + 1) % cut), last_col, jnp.where(upper, top_row, bottom_row)
-        ),
-    )
-    far_strip = jnp.where(same, bottom_row, jnp.where(c == 0, first_col, last_col))
-    got = swap(jnp.concatenate([near_strip, far_strip], axis=1), planes)
-    passed = picked(wanted(2 * cells, False), got.reshape(-1, channels))
-    frame = frame_of(swap(passed, lines))
+    got = swap(edges_of(place, tile, 2 * side), planes)
+    passed = picked(inner_wanted, got.reshape(-1, channels))
+    passed = swap(passed.reshape(side, -1, 4, channels), lines)
+    frame = frame_of(passed.reshape(side, 2 * cells + 4, channels))
     west, east = direct(got[:, :cells], frame[:, 1:-1])
     ends = frame[2:, ::rim - 1]
     top = jnp.concatenate(
@@ -423,13 +495,9 @@
         ]
     )
 
-    small_count = 13 + hid // channels
     many = 2 * hid // (2 * side)
-    few = -(-small_count // (2 * side))
-    extra = 8
-    assert 2 * few <= 4
     block_out, sent, base_grad = block_on_tile(
-        jnp.stack([f, r, c]).astype(jnp.int32),
+        place,
         padded,
         tile,
         out_grad[0],
@@ -459,7 +527,7 @@
     weights = jnp.sum(got[:, :many].astype(F32), axis=0)
     small = small_total(got[:, spare : spare + 2 * few])
     strips = got[:, many:]
-    passed = picked(wanted(2 * cells + extra, True), strips.reshape(-1, channels))
+    passed = picked(end_wanted, strips.reshape(-1, channels))
     tail = jnp.pad(pairs(small), ((0, 4 - 2 * few), (0, 0)))
     sent = jnp.concatenate(
         [
@@ -473,12 +541,7 @@
         axis=1,
     )
     got = swap(sent, lines)
-    weights = jnp.sum(got[:, :many].astype(F32), axis=0) / width
-    small = small_total(got[:, spare : spare + 2 * few]) / width
-    share = jnp.concatenate(
-        [weights.astype(BF), jnp.pad(pairs(small), ((0, 8 - 2 * few), (0, 0)))]
-    )
-    spread = swap(jnp.broadcast_to(share, (2 * side,) + share.shape), planes)
+    spread = swap(share_of(got, 2 * side, many, few, 1.0 / width), planes)
 
     frame = frame_of(got[:, many:])
     folded = frame[:, 1:-1]
@@ -494,7 +557,7 @@
     return (
         block_out[None],
         in_grad.astype(BF)[None],
-        taps.reshape(3, 3, channels),
+        taps,
         bias.reshape(channels),
         gain.reshape(channels),
         shift.reshape(channels),

time: 119 us -> 113 us (0.950)
  waiting for transfers between devices: 44.9 us -> 52.2 us
  between operations: 6.91 us -> 1.11 us
  local copies, waits for them, and re-layouts: 5.23 us -> 1.63 us
  other arithmetic: 5.1 us -> 1.72 us
  starting transfers between devices: 49.9 us -> 46.7 us
  Pallas kernels: 3.59 us -> 6.47 us
    all_to_all x5, waiting for transfers between devices: 44.9 us -> 52.2 us  [swap(): lax.all_to_all(slots, ('face', 'row', 'col'), 0, 0, axis_index_groups=gro...]
    all_to_all x5, starting transfers between devices: 49.9 us -> 46.7 us  [swap(): lax.all_to_all(slots, ('face', 'row', 'col'), 0, 0, axis_index_groups=gro...]
    pallas_call x0 -> x3, Pallas kernels: none -> 2.88 us  [the longest x1 1.39 us: edges_of(): pl.pallas_call(edges_kernel, out_shape=jax.ShapeDtypeStruct((slots, 2 * r...]
    slice x15 -> x2, local copies, waits for them, and re-layouts: 2.35 us -> 0.01 us  [frame_of(): arrival = plan[2, :, :depth].reshape(1, -1)]
  transfers between devices with their start and end apart: 5 -> 5, of which waited for: 4 -> 5; matrix products, arithmetic and copies ran while one was open for 4% -> 1% of each run, Pallas kernels for 0% -> 1%
where the time goes in v4:
time: 113 us; the launch traced here: 112 us
  waiting for transfers between devices  52.2 us (46%)
  starting transfers between devices  46.7 us (41%)
  Pallas kernels  6.47 us (6%)
  matrix products  2.38 us (2%)
  other arithmetic  1.72 us (2%)
  local copies, waits for them, and re-layouts  1.63 us (1%)
    all_to_all x5, waiting for transfers between devices, swap(): lax.all_to_all(slots, ('face', 'row', 'col'), 0, 0, axis_index_groups=gro...  52.2 us
    all_to_all x5, starting transfers between devices, swap(): lax.all_to_all(slots, ('face', 'row', 'col'), 0, 0, axis_index_groups=gro...  46.7 us
    pallas_call x1, Pallas kernels, block_on_tile(): pl.pallas_call(block_kernel, out_shape=(jax.ShapeDtypeStruct(tile.shape,...  2.77 us
  transfers between devices with their start and end apart: 5, of which 5 were waited for; matrix products, arithmetic and copies ran while one was open for 1% of the time, Pallas kernels for 1%

profile of v4, /device:TPU:1, one launch (start us, length us, event | category | flops | bytes accessed | tf_op | source)
XLA Modules:
  0.0 112.2 jit_solution(9225634443952532637)
XLA Ops:
  0.7 0.8 copy-done
  1.6 1.4 %edges.1 = bf16[32,32,128]{2,1,0:T(8,128)(2,1)} custom-call(s32[3]{0:T(128)S(1)} %pad_add_fusion.1.place_ref.plan_ref, bf16[16,16,128]{2,1,0:T(8,128)(2,1)S(1)} %bitcast.44), custom_call_target="tpu_custom_call" | custom-call | tf_op jit(solution)/shard_map/edges/pallas_call | solution.py:58
  3.0 10.5 %all-to-all-start = ((bf16[32,32,128]{2,1,0:T(8,128)(2,1)}), bf16[32,32,128]{2,1,0:T(8,128)(2,1)S(1)}, u32[]{:S(2)}, u32[]{:S(2)}) async-start(bf16[32,32,128]{2,1,0:T(8,128)(2,1)} %edges.1), calls=%async_computation | async-start | bytes 524288 | tf_op jit(solution)/shard_map/all_to_all | solution.py:284
  13.5 0.1 copy.29
  13.6 0.1 reshape.387.adjacency_ref
  13.7 0.7 plan.1
  14.5 7.3 %all-to-all-done = bf16[32,32,128]{2,1,0:T(8,128)(2,1)S(1)} async-done(((bf16[32,32,128]{2,1,0:T(8,128)(2,1)}), bf16[32,32,128]{2,1,0:T(8,128)(2,1)S(1)}, u32[]{:S(2)}, u32[]{:S(2)}) %all-to-all-start) | async-done | bytes 262176 | tf_op jit(solution)/shard_map/all_to_all | solution.py:284
  21.8 1.2 %fusion.5 = bf16[576,128]{1,0:T(8,128)(2,1)} fusion(bf16[1024,128]{1,0:T(8,128)(2,1)S(1)} %bitcast.54, s32[576]{0:T(1024)S(1)} %eq.97), kind=kOutput, calls=%fused_computation.7 | convolution fusion | flops 151658496 | bytes 411904 | tf_op jit(solution)/shard_map/dot_general | solution.py:425
  23.0 13.2 %all-to-all-start.1 = ((bf16[16,9,4,128]{3,2,1,0:T(4,128)(2,1)}), bf16[16,9,4,128]{3,2,1,0:T(4,128)(2,1)S(1)}, u32[]{:S(2)}, u32[]{:S(2)}) async-start(bf16[16,9,4,128]{3,2,1,0:T(4,128)(2,1)} %bitcast.5), calls=%async_computation.1 | async-start | bytes 294912 | tf_op jit(solution)/shard_map/all_to_all | solution.py:284
  36.4 11.9 %all-to-all-done.1 = bf16[16,9,4,128]{3,2,1,0:T(4,128)(2,1)S(1)} async-done(((bf16[16,9,4,128]{3,2,1,0:T(4,128)(2,1)}), bf16[16,9,4,128]{3,2,1,0:T(4,128)(2,1)S(1)}, u32[]{:S(2)}, u32[]{:S(2)}) %all-to-all-start.1) | async-done | bytes 147488 | tf_op jit(solution)/shard_map/all_to_all | solution.py:284
  48.3 0.2 fusion.29
  48.8 2.8 %block.1 = (bf16[16,16,128]{2,1,0:T(8,128)(2,1)}, bf16[32,72,128]{2,1,0:T(8,128)(2,1)}, f32[16,16,128]{2,1,0:T(8,128)S(1)}) custom-call(s32[3]{0:T(128)S(1)} %pad_add_fusion.1.place_ref.plan_ref, bf16[18,18,128]{2,1,0:T(8,128)(2,1)S(1)} %maximum_maximum_fusion.padded_ref, bf16[16,16,128]{2,1,0:T(8,128)(2,1)S(1)} %bitcast.46, ...), custom_call_target="tpu_custom_call" | custom-call | tf_op jit(solution)/shard_map/block/pallas_call | solution.py:191
  51.5 7.8 %all-to-all-start.2 = ((bf16[32,72,128]{2,1,0:T(8,128)(2,1)}), bf16[32,72,128]{2,1,0:T(8,128)(2,1)S(1)}, u32[]{:S(2)}, u32[]{:S(2)}) async-start(bf16[32,72,128]{2,1,0:T(8,128)(2,1)} %get-tuple-element.47), calls=%async_computation.2 | async-start | bytes 1179648 | tf_op jit(solution)/shard_map/all_to_all | solution.py:284
  59.4 11.6 %all-to-all-done.2 = bf16[32,72,128]{2,1,0:T(8,128)(2,1)S(1)} async-done(((bf16[32,72,128]{2,1,0:T(8,128)(2,1)}), bf16[32,72,128]{2,1,0:T(8,128)(2,1)S(1)}, u32[]{:S(2)}, u32[]{:S(2)}) %all-to-all-start.2) | async-done | bytes 589856 | tf_op jit(solution)/shard_map/all_to_all | solution.py:284
  71.1 0.7 fusion.4
  72.0 0.8 pad_maximum_fusion
  72.7 4.0 %all-to-all-start.3 = ((bf16[16,72,128]{2,1,0:T(8,128)(2,1)}), bf16[16,72,128]{2,1,0:T(8,128)(2,1)S(1)}, u32[]{:S(2)}, u32[]{:S(2)}) async-start(bf16[16,72,128]{2,1,0:T(8,128)(2,1)} %pad_maximum_fusion), calls=%async_computation.3 | async-start | bytes 589824 | tf_op jit(solution)/shard_map/all_to_all | solution.py:284
  76.8 13.3 %all-to-all-done.3.got_ref = bf16[16,72,128]{2,1,0:T(8,128)(2,1)S(1)} async-done(((bf16[16,72,128]{2,1,0:T(8,128)(2,1)}), bf16[16,72,128]{2,1,0:T(8,128)(2,1)S(1)}, u32[]{:S(2)}, u32[]{:S(2)}) %all-to-all-start.3) | async-done | bytes 294944 | tf_op jit(solution)/shard_map/all_to_all | solution.py:284
  90.2 0.2 fusion.6
  90.5 0.8 share.1
  91.3 11.2 %all-to-all-start.4 = ((bf16[32,40,128]{2,1,0:T(8,128)(2,1)}), bf16[32,40,128]{2,1,0:T(8,128)(2,1)S(1)}, u32[]{:S(2)}, u32[]{:S(2)}) async-start(bf16[32,40,128]{2,1,0:T(8,128)(2,1)} %share.1), calls=%async_computation.4 | async-start | bytes 655360 | tf_op jit(solution)/shard_map/all_to_all | solution.py:284
  102.5 0.7 fusion.16
  103.2 8.2 %all-to-all-done.4.got_ref = bf16[32,40,128]{2,1,0:T(8,128)(2,1)S(1)} async-done(((bf16[32,40,128]{2,1,0:T(8,128)(2,1)}), bf16[32,40,128]{2,1,0:T(8,128)(2,1)S(1)}, u32[]{:S(2)}, u32[]{:S(2)}) %all-to-all-start.4) | async-done | bytes 327712 | tf_op jit(solution)/shard_map/all_to_all | solution.py:284
  111.4 0.8 finish.1
  (58 shorter events, 0.9 us)
Async XLA Ops:
  0.6 12.8 %copy-start.12 = (s32[2,4,3]{1,0,2:T(2,128)S(1)}, s32[2,4,3]{1,0,2:T(2,128)}, u32[]{:S(2)}) copy-start(s32[2,4,3]{1,0,2:T(2,128)} %param.24) | copy-start | bytes 292
  0.7 0.8 copy-start
  3.0 18.8 %all-to-all-start = ((bf16[32,32,128]{2,1,0:T(8,128)(2,1)}), bf16[32,32,128]{2,1,0:T(8,128)(2,1)S(1)}, u32[]{:S(2)}, u32[]{:S(2)}) async-start(bf16[32,32,128]{2,1,0:T(8,128)(2,1)} %edges.1), calls=%async_computation | async-start | bytes 524288 | tf_op jit(solution)/shard_map/all_to_all | solution.py:284
  21.8 14.5 %copy-start.11 = (f32[3,3,128]{2,1,0:T(4,128)S(1)}, f32[3,3,128]{2,1,0:T(4,128)}, u32[]{:S(2)}) copy-start(f32[3,3,128]{2,1,0:T(4,128)} %param.16) | copy-start | bytes 13828
  23.0 25.6 %copy-start.1 = (bf16[1,16,16,128]{3,2,1,0:T(8,128)(2,1)S(1)}, bf16[1,16,16,128]{3,2,1,0:T(8,128)(2,1)}, u32[]{:S(2)}) copy-start(bf16[1,16,16,128]{3,2,1,0:T(8,128)(2,1)} %param.15) | copy-start | bytes 196612
  23.0 25.7 %copy-start.2 = (bf16[128,512]{1,0:T(8,128)(2,1)S(1)}, bf16[128,512]{1,0:T(8,128)(2,1)}, u32[]{:S(2)}) copy-start(bf16[128,512]{1,0:T(8,128)(2,1)} %expand_ref.1) | copy-start | bytes 393220
  23.0 25.7 %copy-start.3 = (bf16[512,128]{1,0:T(8,128)(2,1)S(1)}, bf16[512,128]{1,0:T(8,128)(2,1)}, u32[]{:S(2)}) copy-start(bf16[512,128]{1,0:T(8,128)(2,1)} %reduce_ref.1) | copy-start | bytes 393220
  23.0 25.7 %copy-start.4 = (bf16[1,16,16,128]{3,2,1,0:T(8,128)(2,1)S(1)}, bf16[1,16,16,128]{3,2,1,0:T(8,128)(2,1)}, u32[]{:S(2)}) copy-start(bf16[1,16,16,128]{3,2,1,0:T(8,128)(2,1)} %param.25) | copy-start | bytes 196612
  23.0 25.7 %copy-start.5 = (f32[512]{0:T(512)S(1)}, f32[512]{0:T(512)}, u32[]{:S(2)}) copy-start(f32[512]{0:T(512)} %param.21) | copy-start | bytes 6148
  23.0 25.7 %copy-start.6 = (f32[128]{0:T(128)S(1)}, f32[128]{0:T(128)}, u32[]{:S(2)}) copy-start(f32[128]{0:T(128)} %param.17) | copy-start | bytes 1540
  23.0 25.7 %copy-start.7 = (f32[128]{0:T(128)S(1)}, f32[128]{0:T(128)}, u32[]{:S(2)}) copy-start(f32[128]{0:T(128)} %param.18) | copy-start | bytes 1540
  23.0 25.7 %copy-start.8 = (f32[128]{0:T(128)S(1)}, f32[128]{0:T(128)}, u32[]{:S(2)}) copy-start(f32[128]{0:T(128)} %param.19) | copy-start | bytes 1540
  23.0 25.7 %copy-start.9 = (f32[128]{0:T(128)S(1)}, f32[128]{0:T(128)}, u32[]{:S(2)}) copy-start(f32[128]{0:T(128)} %param.23) | copy-start | bytes 1540
  23.0 25.2 %all-to-all-start.1 = ((bf16[16,9,4,128]{3,2,1,0:T(4,128)(2,1)}), bf16[16,9,4,128]{3,2,1,0:T(4,128)(2,1)S(1)}, u32[]{:S(2)}, u32[]{:S(2)}) async-start(bf16[16,9,4,128]{3,2,1,0:T(4,128)(2,1)} %bitcast.5), calls=%async_computation.1 | async-start | bytes 294912 | tf_op jit(solution)/shard_map/all_to_all | solution.py:284
  51.5 19.5 %all-to-all-start.2 = ((bf16[32,72,128]{2,1,0:T(8,128)(2,1)}), bf16[32,72,128]{2,1,0:T(8,128)(2,1)S(1)}, u32[]{:S(2)}, u32[]{:S(2)}) async-start(bf16[32,72,128]{2,1,0:T(8,128)(2,1)} %get-tuple-element.47), calls=%async_computation.2 | async-start | bytes 1179648 | tf_op jit(solution)/shard_map/all_to_all | solution.py:284
  71.0 5.8 %copy-start.10 = (bf16[32,72,128]{2,1,0:T(8,128)(2,1)}, bf16[32,72,128]{2,1,0:T(8,128)(2,1)S(1)}, u32[]{:S(2)}) copy-start(bf16[32,72,128]{2,1,0:T(8,128)(2,1)S(1)} %all-to-all-done.2) | copy-start | bytes 1769476
  72.7 17.4 %all-to-all-start.3 = ((bf16[16,72,128]{2,1,0:T(8,128)(2,1)}), bf16[16,72,128]{2,1,0:T(8,128)(2,1)S(1)}, u32[]{:S(2)}, u32[]{:S(2)}) async-start(bf16[16,72,128]{2,1,0:T(8,128)(2,1)} %pad_maximum_fusion), calls=%async_computation.3 | async-start | bytes 589824 | tf_op jit(solution)/shard_map/all_to_all | solution.py:284
  90.5 12.0 %slice-start = ((bf16[32,72,128]{2,1,0:T(8,128)(2,1)}), bf16[32,16,128]{2,1,0:T(8,128)(2,1)S(1)}, s32[]{:S(2)}) async-start(bf16[32,72,128]{2,1,0:T(8,128)(2,1)} %copy-done.10), calls=%async_computation.5 | async-start | bytes 262144 | tf_op jit(solution)/shard_map/slice | solution.py:549
  91.3 20.1 %all-to-all-start.4 = ((bf16[32,40,128]{2,1,0:T(8,128)(2,1)}), bf16[32,40,128]{2,1,0:T(8,128)(2,1)S(1)}, u32[]{:S(2)}, u32[]{:S(2)}) async-start(bf16[32,40,128]{2,1,0:T(8,128)(2,1)} %share.1), calls=%async_computation.4 | async-start | bytes 655360 | tf_op jit(solution)/shard_map/all_to_all | solution.py:284

commit v5 on v4

--- a/solution.py
+++ b/solution.py
@@ -71,22 +71,20 @@
 def block_kernel(
     plan_ref,
     padded_ref,
-    tile_ref,
     grad_ref,
+    grad_hidden_ref,
     tap_ref,
     conv_bias_ref,
     gain_ref,
     shift_ref,
     expand_ref,
     expand_bias_ref,
-    reduce_ref,
-    reduce_bias_ref,
-    out_ref,
+    hidden_ref,
     sent_ref,
     base_ref,
     wide_ref,
 ):
-    rows, columns, channels = tile_ref.shape
+    rows, columns, channels = grad_ref.shape
     count = rows * columns
     rim = rows + 2
     hid = expand_ref.shape[1]
@@ -107,11 +105,9 @@
     preact = jnp.dot(normed, expand_ref[...], preferred_element_type=F32) + expand_bias_ref[...]
     gelu_value, gelu_slope = gelu_pair(preact)
     hidden = gelu_value.astype(BF)
+    hidden_ref[...] = hidden
     grad_cells = grad_ref[...].reshape(count, channels)
-    grad_hidden = lax.dot_general(
-        grad_cells, reduce_ref[...], (((1,), (1,)), ((), ())), preferred_element_type=F32
-    )
-    grad_preact = (grad_hidden * gelu_slope).astype(BF)
+    grad_preact = (grad_hidden_ref[...] * gelu_slope).astype(BF)
     grad_normed = lax.dot_general(
         grad_preact, expand_ref[...], (((1,), (1,)), ((), ())), preferred_element_type=F32
     )
@@ -121,9 +117,6 @@
         - jnp.mean(scaled, axis=-1, keepdims=True)
         - normalized * jnp.mean(scaled * normalized, axis=-1, keepdims=True)
     )
-    out = tile_ref[...].reshape(count, channels).astype(F32)
-    out = out + jnp.dot(hidden, reduce_ref[...], preferred_element_type=F32) + reduce_bias_ref[...]
-    out_ref[...] = out.astype(BF).reshape(rows, columns, channels)
 
     def total(cells):
         return jnp.sum(cells, axis=0, keepdims=True)
@@ -185,52 +178,49 @@
         sent_ref[slot, near + rows : near + rows + extra] = block.astype(BF)
 
 
-def block_on_tile(plan, padded, tile, grad, taps, *params):
-    rows, columns, channels = tile.shape
+def block_on_tile(place, padded, grad, grad_hidden, *params):
+    rows, columns, channels = grad.shape
     slots, depth = params[-2:]
     return pl.pallas_call(
         block_kernel,
         out_shape=(
-            jax.ShapeDtypeStruct(tile.shape, BF),
+            jax.ShapeDtypeStruct(grad_hidden.shape, BF),
             jax.ShapeDtypeStruct((slots, depth, channels), BF),
-            jax.ShapeDtypeStruct(tile.shape, F32),
+            jax.ShapeDtypeStruct(grad.shape, F32),
         ),
         in_specs=[pl.BlockSpec(memory_space=pltpu.SMEM)]
-        + [pl.BlockSpec(memory_space=pltpu.VMEM)] * 11,
+        + [pl.BlockSpec(memory_space=pltpu.VMEM)] * 9,
         out_specs=(pl.BlockSpec(memory_space=pltpu.VMEM),) * 3,
         scratch_shapes=[pltpu.VMEM((rows + 2, columns + 8, channels), F32)],
         compiler_params=pltpu.CompilerParams(vmem_limit_bytes=24 * 1024 * 1024),
         name="block",
-    )(plan, padded, tile, grad, taps, *params[:-2])
-
-
-def share_kernel(scale, few, got_ref, share_ref):
-    slots, depth, channels = share_ref.shape
-    many = depth - 8
+    )(place, padded, grad, grad_hidden, *params[:-2])
+
+
+def share_kernel(scale, few, many, got_ref, share_ref):
+    total, channels = share_ref.shape
     spare = got_ref.shape[1] - 4
     weights = jnp.zeros((many, channels), F32)
     rest = jnp.zeros((4, channels), F32)
     for k in range(got_ref.shape[0]):
         weights = weights + got_ref[k, 0:many].astype(F32)
         rest = rest + got_ref[k, spare - 4 : spare + 4].astype(F32)[4:8]
-    weights = (weights * scale).astype(BF)
-    place = lax.broadcasted_iota(jnp.int32, (8, channels), 0)
-    block = jnp.zeros((8, channels), F32)
+    parts = [weights * scale]
     for k in range(few):
         small = (rest[2 * k : 2 * k + 1] + rest[2 * k + 1 : 2 * k + 2]) * scale
         high = small.astype(BF).astype(F32)
-        block = jnp.where(place == 2 * k, high, jnp.where(place == 2 * k + 1, small - high, block))
-    block = block.astype(BF)
-    for slot in range(slots):
-        share_ref[slot, 0:many] = weights
-        share_ref[slot, many:depth] = block
+        parts += [high, small - high]
+    block = jnp.concatenate(parts * 8).astype(BF)
+    depth = block.shape[0]
+    for k in range(0, total, depth):
+        share_ref[k : k + depth] = block
 
 
 def share_of(got, slots, many, few, scale):
     channels = got.shape[2]
     return pl.pallas_call(
-        functools.partial(share_kernel, scale, few),
-        out_shape=jax.ShapeDtypeStruct((slots, many + 8, channels), BF),
+        functools.partial(share_kernel, scale, few, many),
+        out_shape=jax.ShapeDtypeStruct((slots * (many + 2 * few), channels), BF),
         in_specs=[pl.BlockSpec(memory_space=pltpu.VMEM)],
         out_specs=pl.BlockSpec(memory_space=pltpu.VMEM),
         compiler_params=pltpu.CompilerParams(vmem_limit_bytes=8 * 1024 * 1024),
@@ -238,24 +228,29 @@
     )(got)
 
 
-def finish_kernel(got_ref, *out_refs):
+def finish_kernel(many, few, got_ref, *out_refs):
     tap_ref, bias_ref, gain_ref, shift_ref, expand_ref, expand_bias_ref, reduce_ref, reduce_bias_ref = (
         out_refs
     )
-    slots, depth, channels = got_ref.shape
+    total, channels = got_ref.shape
     hid = reduce_ref.shape[0]
-    many = 2 * hid // slots
-    for k in range(0, hid, channels):
-        for j in range(0, channels, many):
-            expand_ref[j : j + many, k : k + channels] = got_ref[(k + j) // many, 0:many].astype(F32)
-    for k in range(0, hid, many):
-        reduce_ref[k : k + many] = got_ref[(hid + k) // many, 0:many].astype(F32)
+    depth = many + 2 * few
+    small = []
+    for start in range(0, total, 8 * depth):
+        block = got_ref[start : start + 8 * depth].astype(F32)
+        for k in range(8):
+            slot = start // depth + k
+            part = block[k * depth : (k + 1) * depth]
+            row = slot * many
+            if row < hid:
+                lane, row = row // channels * channels, row % channels
+                expand_ref[row : row + many, lane : lane + channels] = part[:many]
+            else:
+                reduce_ref[row - hid : row - hid + many] = part[:many]
+            if slot % 2 == 0:
+                rest = part[many:]
+                small += [rest[2 * k : 2 * k + 1] + rest[2 * k + 1 : 2 * k + 2] for k in range(few)]
     blocks = hid // channels
-    few = -(-(13 + blocks) // slots)
-    small = []
-    for slot in range(slots):
-        rest = got_ref[slot, many:depth].astype(F32)
-        small += [rest[2 * k : 2 * k + 1] + rest[2 * k + 1 : 2 * k + 2] for k in range(few)]
     for k in range(9):
         tap_ref[k // 3, k % 3 : k % 3 + 1] = small[k]
     bias_ref[...] = small[9]
@@ -266,12 +261,12 @@
     reduce_bias_ref[...] = small[12 + blocks]
 
 
-def finish(got, hid):
-    channels = got.shape[2]
+def finish(got, hid, many, few):
+    channels = got.shape[1]
     shapes = [(3, 3, channels)] + [(1, channels)] * 3
     shapes += [(channels, hid), (1, hid), (hid, channels), (1, channels)]
     return pl.pallas_call(
-        finish_kernel,
+        functools.partial(finish_kernel, many, few),
         out_shape=tuple(jax.ShapeDtypeStruct(shape, F32) for shape in shapes),
         in_specs=[pl.BlockSpec(memory_space=pltpu.VMEM)],
         out_specs=(pl.BlockSpec(memory_space=pltpu.VMEM),) * len(shapes),
@@ -288,7 +283,7 @@
     return lax.dynamic_index_in_dim(slots, index, 0, keepdims=False)
 
 
-def plane_and_line_groups(side):
+def device_groups(side):
     cut = math.isqrt(side)
     steps = range(cut)
 
@@ -306,7 +301,12 @@
         for y in steps
         for x in steps
     ]
-    return planes, lines
+    doubles = [
+        [device(f, y, x, high, low + k) for f in range(2) for y in steps for x in steps for k in range(2)]
+        for high in steps
+        for low in range(0, cut, 2)
+    ]
+    return planes, lines, doubles
 
 
 def frame_sources(entries, f, y, x, sender, target, step, side, cells):
@@ -451,7 +451,7 @@
     r = lax.axis_index("row")
     c = lax.axis_index("col")
     y, x = r // cut, c % cut
-    planes, lines = plane_and_line_groups(side)
+    planes, lines, doubles = device_groups(side)
     place = jnp.stack([f, r, c]).astype(jnp.int32)
     few = -(-(13 + hid // channels) // (2 * side))
     extra = 8
@@ -496,22 +496,29 @@
     )
 
     many = 2 * hid // (2 * side)
-    block_out, sent, base_grad = block_on_tile(
+    grad_cells = out_grad[0].reshape(cells * cells, channels)
+    grad_hidden = lax.dot_general(
+        grad_cells, reduce_weight, (((1,), (1,)), ((), ())), preferred_element_type=F32
+    )
+    hidden, sent, base_grad = block_on_tile(
         place,
         padded,
-        tile,
         out_grad[0],
+        grad_hidden,
         conv_kernel.reshape(9, channels),
         conv_bias.reshape(1, channels),
         norm_gain.reshape(1, channels),
         norm_bias.reshape(1, channels),
         expand_weight,
         expand_bias.reshape(1, hid),
-        reduce_weight,
-        reduce_bias.reshape(1, channels),
         2 * side,
         many + 2 * cells + extra,
     )
+    block_out = (
+        tile.reshape(cells * cells, channels).astype(F32)
+        + jnp.dot(hidden, reduce_weight, preferred_element_type=F32)
+        + reduce_bias
+    ).astype(BF)
     got = swap(sent, planes)
 
     def pairs(small):
@@ -523,6 +530,7 @@
         sums = jnp.sum(rest.astype(F32), axis=0).reshape(few, 2, channels)
         return sums[:, 0] + sums[:, 1]
 
+    half = many // 2
     spare = many + 2 * cells + 4
     weights = jnp.sum(got[:, :many].astype(F32), axis=0)
     small = small_total(got[:, spare : spare + 2 * few])
@@ -531,7 +539,7 @@
     tail = jnp.pad(pairs(small), ((0, 4 - 2 * few), (0, 0)))
     sent = jnp.concatenate(
         [
-            jnp.broadcast_to(weights.astype(BF), (side, many, channels)),
+            jnp.tile(weights.astype(BF).reshape(2, half, channels), (side // 2, 1, 1)),
             passed[:, : 2 * cells],
             jnp.concatenate(
                 [passed[:, 2 * cells : 2 * cells + 4], jnp.broadcast_to(tail, (side, 4, channels))],
@@ -541,9 +549,10 @@
         axis=1,
     )
     got = swap(sent, lines)
-    spread = swap(share_of(got, 2 * side, many, few, 1.0 / width), planes)
-
-    frame = frame_of(got[:, many:])
+    share = share_of(got, 4 * side, half, few, 1.0 / width)
+    spread = swap(share.reshape(4 * side, -1, 2, channels), doubles).reshape(share.shape)
+
+    frame = frame_of(got[:, half:])
     folded = frame[:, 1:-1]
     folded = folded.at[:, 0].add(frame[:, 0]).at[:, -1].add(frame[:, -1])
     west, east = direct(strips[:, :cells], folded)
@@ -553,9 +562,9 @@
     in_grad = in_grad + jnp.pad(west[:, None], ((0, 0), (0, cells - 1), (0, 0)))
     in_grad = in_grad + jnp.pad(east[:, None], ((0, 0), (cells - 1, 0), (0, 0)))
 
-    taps, bias, gain, shift, expand, expand_vector, reduce, reduce_vector = finish(spread, hid)
+    taps, bias, gain, shift, expand, expand_vector, reduce, reduce_vector = finish(spread, hid, half, few)
     return (
-        block_out[None],
+        block_out.reshape(1, cells, cells, channels),
         in_grad.astype(BF)[None],
         taps,
         bias.reshape(channels),

time: 113 us -> 112 us (level)
  waiting for transfers between devices: 52.2 us -> 50.2 us
    all_to_all x5, waiting for transfers between devices: 52.2 us -> 50.2 us  [swap(): lax.all_to_all(slots, ('face', 'row', 'col'), 0, 0, axis_index_groups=gro...]
  transfers between devices with their start and end apart: 5 -> 5, of which waited for: 5 -> 5; matrix products, arithmetic and copies ran while one was open for 1% -> 2% of each run, Pallas kernels for 1% -> 1%
where the time goes in v5:
time: 112 us
  waiting for transfers between devices  50.2 us (45%)
  starting transfers between devices  46.6 us (42%)
  Pallas kernels  6.45 us (6%)
  matrix products  3.45 us (3%)
  local copies, waits for them, and re-layouts  2.16 us (2%)
  other arithmetic  1.67 us (1%)
    all_to_all x5, waiting for transfers between devices, swap(): lax.all_to_all(slots, ('face', 'row', 'col'), 0, 0, axis_index_groups=gro...  50.2 us
    all_to_all x5, starting transfers between devices, swap(): lax.all_to_all(slots, ('face', 'row', 'col'), 0, 0, axis_index_groups=gro...  46.6 us
    pallas_call x1, Pallas kernels, block_on_tile(): pl.pallas_call(block_kernel, out_shape=(jax.ShapeDtypeStruct(grad_hidden....  2.74 us
  transfers between devices with their start and end apart: 5, of which 5 were waited for; matrix products, arithmetic and copies ran while one was open for 2% of the time, Pallas kernels for 1%

profile of v5, /device:TPU:1, one launch (start us, length us, event | category | flops | bytes accessed | tf_op | source)
XLA Modules:
  0.0 111.6 jit_solution(5426342011779200682)
XLA Ops:
  0.8 0.8 copy-done.1
  1.6 1.4 %edges.1 = bf16[32,32,128]{2,1,0:T(8,128)(2,1)} custom-call(s32[3]{0:T(128)S(1)} %pad_add_fusion.1.place_ref.plan_ref, bf16[16,16,128]{2,1,0:T(8,128)(2,1)S(1)} %bitcast.55), custom_call_target="tpu_custom_call" | custom-call | tf_op jit(solution)/shard_map/edges/pallas_call | solution.py:58
  3.0 10.5 %all-to-all-start = ((bf16[32,32,128]{2,1,0:T(8,128)(2,1)}), bf16[32,32,128]{2,1,0:T(8,128)(2,1)S(1)}, u32[]{:S(2)}, u32[]{:S(2)}) async-start(bf16[32,32,128]{2,1,0:T(8,128)(2,1)} %edges.1), calls=%async_computation | async-start | bytes 524288 | tf_op jit(solution)/shard_map/all_to_all | solution.py:279
  13.7 0.7 plan.1
  14.5 7.3 %all-to-all-done = bf16[32,32,128]{2,1,0:T(8,128)(2,1)S(1)} async-done(((bf16[32,32,128]{2,1,0:T(8,128)(2,1)}), bf16[32,32,128]{2,1,0:T(8,128)(2,1)S(1)}, u32[]{:S(2)}, u32[]{:S(2)}) %all-to-all-start) | async-done | bytes 262176 | tf_op jit(solution)/shard_map/all_to_all | solution.py:279
  21.8 1.2 %fusion.5 = bf16[576,128]{1,0:T(8,128)(2,1)} fusion(bf16[1024,128]{1,0:T(8,128)(2,1)S(1)} %bitcast.65, s32[576]{0:T(1024)S(1)} %eq.97), kind=kOutput, calls=%fused_computation.7 | convolution fusion | flops 151658496 | bytes 411904 | tf_op jit(solution)/shard_map/dot_general | solution.py:425
  23.0 13.0 %all-to-all-start.1 = ((bf16[16,9,4,128]{3,2,1,0:T(4,128)(2,1)}), bf16[16,9,4,128]{3,2,1,0:T(4,128)(2,1)S(1)}, u32[]{:S(2)}, u32[]{:S(2)}) async-start(bf16[16,9,4,128]{3,2,1,0:T(4,128)(2,1)} %bitcast.6), calls=%async_computation.1 | async-start | bytes 294912 | tf_op jit(solution)/shard_map/all_to_all | solution.py:279
  36.5 11.6 %all-to-all-done.1 = bf16[16,9,4,128]{3,2,1,0:T(4,128)(2,1)S(1)} async-done(((bf16[16,9,4,128]{3,2,1,0:T(4,128)(2,1)}), bf16[16,9,4,128]{3,2,1,0:T(4,128)(2,1)S(1)}, u32[]{:S(2)}, u32[]{:S(2)}) %all-to-all-start.1) | async-done | bytes 147488 | tf_op jit(solution)/shard_map/all_to_all | solution.py:279
  48.1 0.2 fusion.31
  48.5 2.7 %block.1 = (bf16[256,512]{1,0:T(8,128)(2,1)S(1)}, bf16[32,72,128]{2,1,0:T(8,128)(2,1)}, f32[16,16,128]{2,1,0:T(8,128)S(1)}) custom-call(s32[3]{0:T(128)S(1)} %pad_add_fusion.1.place_ref.plan_ref, bf16[18,18,128]{2,1,0:T(8,128)(2,1)S(1)} %maximum_maximum_fusion.padded_ref, bf16[16,16,128]{2,1,0:T(8,128)(2,1)S(1)} %bitcast.59, ...), custom_call_target="tpu_custom_call" | custom-call | tf_op jit(solution)/shard_map/block/pallas_call | solution.py:184
  51.3 7.8 %all-to-all-start.2 = ((bf16[32,72,128]{2,1,0:T(8,128)(2,1)}), bf16[32,72,128]{2,1,0:T(8,128)(2,1)S(1)}, u32[]{:S(2)}, u32[]{:S(2)}) async-start(bf16[32,72,128]{2,1,0:T(8,128)(2,1)} %get-tuple-element.47), calls=%async_computation.2 | async-start | bytes 1179648 | tf_op jit(solution)/shard_map/all_to_all | solution.py:279
  59.2 11.6 %all-to-all-done.2 = bf16[32,72,128]{2,1,0:T(8,128)(2,1)S(1)} async-done(((bf16[32,72,128]{2,1,0:T(8,128)(2,1)}), bf16[32,72,128]{2,1,0:T(8,128)(2,1)S(1)}, u32[]{:S(2)}, u32[]{:S(2)}) %all-to-all-start.2) | async-done | bytes 589856 | tf_op jit(solution)/shard_map/all_to_all | solution.py:279
  70.9 0.7 fusion.4
  71.7 0.7 pad_maximum_fusion
  72.4 4.0 %all-to-all-start.3 = ((bf16[16,56,128]{2,1,0:T(8,128)(2,1)}), bf16[16,56,128]{2,1,0:T(8,128)(2,1)S(1)}, u32[]{:S(2)}, u32[]{:S(2)}) async-start(bf16[16,56,128]{2,1,0:T(8,128)(2,1)} %pad_maximum_fusion), calls=%async_computation.3 | async-start | bytes 458752 | tf_op jit(solution)/shard_map/all_to_all | solution.py:279
  76.5 12.5 %all-to-all-done.3.got_ref = bf16[16,56,128]{2,1,0:T(8,128)(2,1)S(1)} async-done(((bf16[16,56,128]{2,1,0:T(8,128)(2,1)}), bf16[16,56,128]{2,1,0:T(8,128)(2,1)S(1)}, u32[]{:S(2)}, u32[]{:S(2)}) %all-to-all-start.3) | async-done | bytes 229408 | tf_op jit(solution)/shard_map/all_to_all | solution.py:279
  89.0 0.8 share.1
  89.8 11.3 %all-to-all-start.4 = ((bf16[64,9,2,128]{3,2,1,0:T(2,128)(2,1)}), bf16[64,9,2,128]{3,2,1,0:T(2,128)(2,1)S(1)}, u32[]{:S(2)}, u32[]{:S(2)}) async-start(bf16[64,9,2,128]{3,2,1,0:T(2,128)(2,1)} %bitcast.29), calls=%async_computation.4 | async-start | bytes 589824 | tf_op jit(solution)/shard_map/all_to_all | solution.py:279
  101.1 0.8 fusion.7
  102.0 0.2 fusion.8
  102.3 0.5 slice-done
  102.8 0.7 fusion.18
  103.5 7.3 %all-to-all-done.4 = bf16[64,9,2,128]{3,2,1,0:T(2,128)(2,1)S(1)} async-done(((bf16[64,9,2,128]{3,2,1,0:T(2,128)(2,1)}), bf16[64,9,2,128]{3,2,1,0:T(2,128)(2,1)S(1)}, u32[]{:S(2)}, u32[]{:S(2)}) %all-to-all-start.4) | async-done | bytes 294944 | tf_op jit(solution)/shard_map/all_to_all | solution.py:279
  110.8 0.8 finish.1
  (60 shorter events, 1.3 us)
Async XLA Ops:
  0.6 35.6 %copy-start = (bf16[512,128]{1,0:T(8,128)(2,1)S(1)}, bf16[512,128]{1,0:T(8,128)(2,1)}, u32[]{:S(2)}) copy-start(bf16[512,128]{1,0:T(8,128)(2,1)} %param.22) | copy-start | bytes 393220
  0.7 12.8 %copy-start.11 = (s32[2,4,3]{1,0,2:T(2,128)S(1)}, s32[2,4,3]{1,0,2:T(2,128)}, u32[]{:S(2)}) copy-start(s32[2,4,3]{1,0,2:T(2,128)} %param.24) | copy-start | bytes 292
  0.8 0.8 copy-start.1
  3.0 18.8 %all-to-all-start = ((bf16[32,32,128]{2,1,0:T(8,128)(2,1)}), bf16[32,32,128]{2,1,0:T(8,128)(2,1)S(1)}, u32[]{:S(2)}, u32[]{:S(2)}) async-start(bf16[32,32,128]{2,1,0:T(8,128)(2,1)} %edges.1), calls=%async_computation | async-start | bytes 524288 | tf_op jit(solution)/shard_map/all_to_all | solution.py:279
  21.8 14.3 %copy-start.10 = (f32[3,3,128]{2,1,0:T(4,128)S(1)}, f32[3,3,128]{2,1,0:T(4,128)}, u32[]{:S(2)}) copy-start(f32[3,3,128]{2,1,0:T(4,128)} %param.16) | copy-start | bytes 13828
  21.8 14.4 %copy-start.3 = (bf16[1,16,16,128]{3,2,1,0:T(8,128)(2,1)S(1)}, bf16[1,16,16,128]{3,2,1,0:T(8,128)(2,1)}, u32[]{:S(2)}) copy-start(bf16[1,16,16,128]{3,2,1,0:T(8,128)(2,1)} %param.25) | copy-start | bytes 196612
  23.0 25.1 %all-to-all-start.1 = ((bf16[16,9,4,128]{3,2,1,0:T(4,128)(2,1)}), bf16[16,9,4,128]{3,2,1,0:T(4,128)(2,1)S(1)}, u32[]{:S(2)}, u32[]{:S(2)}) async-start(bf16[16,9,4,128]{3,2,1,0:T(4,128)(2,1)} %bitcast.6), calls=%async_computation.1 | async-start | bytes 294912 | tf_op jit(solution)/shard_map/all_to_all | solution.py:279
  36.2 12.2 %copy-start.2 = (bf16[1,16,16,128]{3,2,1,0:T(8,128)(2,1)S(1)}, bf16[1,16,16,128]{3,2,1,0:T(8,128)(2,1)}, u32[]{:S(2)}) copy-start(bf16[1,16,16,128]{3,2,1,0:T(8,128)(2,1)} %param.15) | copy-start | bytes 196612
  36.2 12.3 %copy-start.4 = (bf16[128,512]{1,0:T(8,128)(2,1)S(1)}, bf16[128,512]{1,0:T(8,128)(2,1)}, u32[]{:S(2)}) copy-start(bf16[128,512]{1,0:T(8,128)(2,1)} %expand_ref.1) | copy-start | bytes 393220
  36.2 12.3 %copy-start.5 = (f32[512]{0:T(512)S(1)}, f32[512]{0:T(512)}, u32[]{:S(2)}) copy-start(f32[512]{0:T(512)} %param.21) | copy-start | bytes 6148
  36.3 12.3 %copy-start.6 = (f32[128]{0:T(128)S(1)}, f32[128]{0:T(128)}, u32[]{:S(2)}) copy-start(f32[128]{0:T(128)} %param.17) | copy-start | bytes 1540
  36.3 12.3 %copy-start.7 = (f32[128]{0:T(128)S(1)}, f32[128]{0:T(128)}, u32[]{:S(2)}) copy-start(f32[128]{0:T(128)} %param.18) | copy-start | bytes 1540
  36.3 12.3 %copy-start.8 = (f32[128]{0:T(128)S(1)}, f32[128]{0:T(128)}, u32[]{:S(2)}) copy-start(f32[128]{0:T(128)} %param.19) | copy-start | bytes 1540
  51.3 19.5 %all-to-all-start.2 = ((bf16[32,72,128]{2,1,0:T(8,128)(2,1)}), bf16[32,72,128]{2,1,0:T(8,128)(2,1)S(1)}, u32[]{:S(2)}, u32[]{:S(2)}) async-start(bf16[32,72,128]{2,1,0:T(8,128)(2,1)} %get-tuple-element.47), calls=%async_computation.2 | async-start | bytes 1179648 | tf_op jit(solution)/shard_map/all_to_all | solution.py:279
  70.8 31.2 %copy-start.9 = (bf16[32,72,128]{2,1,0:T(8,128)(2,1)}, bf16[32,72,128]{2,1,0:T(8,128)(2,1)S(1)}, u32[]{:S(2)}) copy-start(bf16[32,72,128]{2,1,0:T(8,128)(2,1)S(1)} %all-to-all-done.2) | copy-start | bytes 1769476
  72.4 16.6 %all-to-all-start.3 = ((bf16[16,56,128]{2,1,0:T(8,128)(2,1)}), bf16[16,56,128]{2,1,0:T(8,128)(2,1)S(1)}, u32[]{:S(2)}, u32[]{:S(2)}) async-start(bf16[16,56,128]{2,1,0:T(8,128)(2,1)} %pad_maximum_fusion), calls=%async_computation.3 | async-start | bytes 458752 | tf_op jit(solution)/shard_map/all_to_all | solution.py:279
  76.4 24.6 %copy-start.12 = (f32[128]{0:T(128)S(1)}, f32[128]{0:T(128)}, u32[]{:S(2)}) copy-start(f32[128]{0:T(128)} %param.23) | copy-start | bytes 1540
  89.8 21.0 %all-to-all-start.4 = ((bf16[64,9,2,128]{3,2,1,0:T(2,128)(2,1)}), bf16[64,9,2,128]{3,2,1,0:T(2,128)(2,1)S(1)}, u32[]{:S(2)}, u32[]{:S(2)}) async-start(bf16[64,9,2,128]{3,2,1,0:T(2,128)(2,1)} %bitcast.29), calls=%async_computation.4 | async-start | bytes 589824 | tf_op jit(solution)/shard_map/all_to_all | solution.py:279
  101.9 0.9 slice-start

commit v6 on v5

--- a/solution.py
+++ b/solution.py
@@ -247,9 +247,8 @@
                 expand_ref[row : row + many, lane : lane + channels] = part[:many]
             else:
                 reduce_ref[row - hid : row - hid + many] = part[:many]
-            if slot % 2 == 0:
-                rest = part[many:]
-                small += [rest[2 * k : 2 * k + 1] + rest[2 * k + 1 : 2 * k + 2] for k in range(few)]
+            rest = part[many:]
+            small += [rest[2 * k : 2 * k + 1] + rest[2 * k + 1 : 2 * k + 2] for k in range(few)]
     blocks = hid // channels
     for k in range(9):
         tap_ref[k // 3, k % 3 : k % 3 + 1] = small[k]
@@ -301,12 +300,7 @@
         for y in steps
         for x in steps
     ]
-    doubles = [
-        [device(f, y, x, high, low + k) for f in range(2) for y in steps for x in steps for k in range(2)]
-        for high in steps
-        for low in range(0, cut, 2)
-    ]
-    return planes, lines, doubles
+    return planes, lines
 
 
 def frame_sources(entries, f, y, x, sender, target, step, side, cells):
@@ -420,8 +414,13 @@
     )(place, adjacency.reshape(-1))
 
 
+def choice(wanted, count):
+    chosen = (wanted.reshape(-1, 1) == jnp.arange(count, dtype=jnp.int32)).astype(BF)
+    return lax.optimization_barrier(chosen)
+
+
 def picked(wanted, held):
-    chosen = (wanted.reshape(-1, 1) == jnp.arange(held.shape[0], dtype=jnp.int32)).astype(BF)
+    chosen = choice(wanted, held.shape[0])
     cells = jnp.dot(chosen, held, preferred_element_type=F32).astype(BF)
     return cells.reshape(wanted.shape + held.shape[1:])
 
@@ -451,7 +450,7 @@
     r = lax.axis_index("row")
     c = lax.axis_index("col")
     y, x = r // cut, c % cut
-    planes, lines, doubles = device_groups(side)
+    planes, lines = device_groups(side)
     place = jnp.stack([f, r, c]).astype(jnp.int32)
     few = -(-(13 + hid // channels) // (2 * side))
     extra = 8
@@ -530,7 +529,6 @@
         sums = jnp.sum(rest.astype(F32), axis=0).reshape(few, 2, channels)
         return sums[:, 0] + sums[:, 1]
 
-    half = many // 2
     spare = many + 2 * cells + 4
     weights = jnp.sum(got[:, :many].astype(F32), axis=0)
     small = small_total(got[:, spare : spare + 2 * few])
@@ -539,7 +537,7 @@
     tail = jnp.pad(pairs(small), ((0, 4 - 2 * few), (0, 0)))
     sent = jnp.concatenate(
         [
-            jnp.tile(weights.astype(BF).reshape(2, half, channels), (side // 2, 1, 1)),
+            jnp.broadcast_to(weights.astype(BF), (side, many, channels)),
             passed[:, : 2 * cells],
             jnp.concatenate(
                 [passed[:, 2 * cells : 2 * cells + 4], jnp.broadcast_to(tail, (side, 4, channels))],
@@ -549,10 +547,10 @@
         axis=1,
     )
     got = swap(sent, lines)
-    share = share_of(got, 4 * side, half, few, 1.0 / width)
-    spread = swap(share.reshape(4 * side, -1, 2, channels), doubles).reshape(share.shape)
-
-    frame = frame_of(got[:, half:])
+    share = share_of(got, 2 * side, many, few, 1.0 / width)
+    spread = swap(share.reshape(2 * side, -1, 2, channels), planes).reshape(share.shape)
+
+    frame = frame_of(got[:, many:])
     folded = frame[:, 1:-1]
     folded = folded.at[:, 0].add(frame[:, 0]).at[:, -1].add(frame[:, -1])
     west, east = direct(strips[:, :cells], folded)
@@ -562,7 +560,7 @@
     in_grad = in_grad + jnp.pad(west[:, None], ((0, 0), (0, cells - 1), (0, 0)))
     in_grad = in_grad + jnp.pad(east[:, None], ((0, 0), (cells - 1, 0), (0, 0)))
 
-    taps, bias, gain, shift, expand, expand_vector, reduce, reduce_vector = finish(spread, hid, half, few)
+    taps, bias, gain, shift, expand, expand_vector, reduce, reduce_vector = finish(spread, hid, many, few)
     return (
         block_out.reshape(1, cells, cells, channels),
         in_grad.astype(BF)[None],

time: 112 us -> 115 us (1.027)
  other arithmetic: 1.67 us -> 4.11 us
  local copies, waits for them, and re-layouts: 2.16 us -> 4.23 us
  waiting for transfers between devices: 50.2 us -> 48.4 us
    all_to_all x5, waiting for transfers between devices: 50.2 us -> 48.4 us  [swap(): lax.all_to_all(slots, ('face', 'row', 'col'), 0, 0, axis_index_groups=gro...]
  transfers between devices with their start and end apart: 5 -> 5, of which waited for: 5 -> 5; matrix products, arithmetic and copies ran while one was open for 2% -> 4% of each run, Pallas kernels for 1% -> 1%
where the time goes in v6:
time: 115 us; the launch traced here: 114 us
  waiting for transfers between devices  48.4 us (42%)
  starting transfers between devices  46.8 us (41%)
  Pallas kernels  6.43 us (6%)
  local copies, waits for them, and re-layouts  4.23 us (4%)
  other arithmetic  4.11 us (4%)
  matrix products  3.26 us (3%)
    all_to_all x5, waiting for transfers between devices, swap(): lax.all_to_all(slots, ('face', 'row', 'col'), 0, 0, axis_index_groups=gro...  48.4 us
    all_to_all x5, starting transfers between devices, swap(): lax.all_to_all(slots, ('face', 'row', 'col'), 0, 0, axis_index_groups=gro...  46.8 us
    pallas_call x1, Pallas kernels, block_on_tile(): pl.pallas_call(block_kernel, out_shape=(jax.ShapeDtypeStruct(grad_hidden....  2.73 us
  transfers between devices with their start and end apart: 5, of which 5 were waited for; matrix products, arithmetic and copies ran while one was open for 4% of the time, Pallas kernels for 1%

profile of v6, /device:TPU:1, one launch (start us, length us, event | category | flops | bytes accessed | tf_op | source)
XLA Modules:
  0.0 114.4 jit_solution(16089304250850083787)
XLA Ops:
  0.7 0.8 copy-done.1
  1.6 1.4 %edges.1 = bf16[32,32,128]{2,1,0:T(8,128)(2,1)} custom-call(s32[3]{0:T(128)S(1)} %pad_add_fusion.1.place_ref.plan_ref, bf16[16,16,128]{2,1,0:T(8,128)(2,1)S(1)} %bitcast.55), custom_call_target="tpu_custom_call" | custom-call | tf_op jit(solution)/shard_map/edges/pallas_call | solution.py:58
  3.0 10.5 %all-to-all-start = ((bf16[32,32,128]{2,1,0:T(8,128)(2,1)}), bf16[32,32,128]{2,1,0:T(8,128)(2,1)S(1)}, u32[]{:S(2)}, u32[]{:S(2)}) async-start(bf16[32,32,128]{2,1,0:T(8,128)(2,1)} %edges.1), calls=%async_computation | async-start | bytes 524288 | tf_op jit(solution)/shard_map/all_to_all | solution.py:278
  13.5 0.8 copy.29
  14.4 0.7 plan.1
  15.5 6.3 %all-to-all-done = bf16[32,32,128]{2,1,0:T(8,128)(2,1)S(1)} async-done(((bf16[32,32,128]{2,1,0:T(8,128)(2,1)}), bf16[32,32,128]{2,1,0:T(8,128)(2,1)S(1)}, u32[]{:S(2)}, u32[]{:S(2)}) %all-to-all-start) | async-done | bytes 262176 | tf_op jit(solution)/shard_map/all_to_all | solution.py:278
  21.8 1.1 convolution_convert_fusion.1
  22.9 13.0 %all-to-all-start.1 = ((bf16[16,9,4,128]{3,2,1,0:T(4,128)(2,1)}), bf16[16,9,4,128]{3,2,1,0:T(4,128)(2,1)S(1)}, u32[]{:S(2)}, u32[]{:S(2)}) async-start(bf16[16,9,4,128]{3,2,1,0:T(4,128)(2,1)} %bitcast.6), calls=%async_computation.1 | async-start | bytes 294912 | tf_op jit(solution)/shard_map/all_to_all | solution.py:278
  36.4 11.6 %all-to-all-done.1 = bf16[16,9,4,128]{3,2,1,0:T(4,128)(2,1)S(1)} async-done(((bf16[16,9,4,128]{3,2,1,0:T(4,128)(2,1)}), bf16[16,9,4,128]{3,2,1,0:T(4,128)(2,1)S(1)}, u32[]{:S(2)}, u32[]{:S(2)}) %all-to-all-start.1) | async-done | bytes 147488 | tf_op jit(solution)/shard_map/all_to_all | solution.py:278
  48.5 2.7 %block.1 = (bf16[256,512]{1,0:T(8,128)(2,1)S(1)}, bf16[32,72,128]{2,1,0:T(8,128)(2,1)}, f32[16,16,128]{2,1,0:T(8,128)S(1)}) custom-call(s32[3]{0:T(128)S(1)} %pad_add_fusion.1.place_ref.plan_ref, bf16[18,18,128]{2,1,0:T(8,128)(2,1)S(1)} %maximum_maximum_fusion.padded_ref, bf16[16,16,128]{2,1,0:T(8,128)(2,1)S(1)} %bitcast.59, ...), custom_call_target="tpu_custom_call" | custom-call | tf_op jit(solution)/shard_map/block/pallas_call | solution.py:184
  51.2 8.2 %all-to-all-start.2 = ((bf16[32,72,128]{2,1,0:T(8,128)(2,1)}), bf16[32,72,128]{2,1,0:T(8,128)(2,1)}, u32[]{:S(2)}, u32[]{:S(2)}) async-start(bf16[32,72,128]{2,1,0:T(8,128)(2,1)} %get-tuple-element.47), calls=%async_computation.2 | async-start | bytes 1179648 | tf_op jit(solution)/shard_map/all_to_all | solution.py:278
  59.9 11.3 %all-to-all-done.2 = bf16[32,72,128]{2,1,0:T(8,128)(2,1)} async-done(((bf16[32,72,128]{2,1,0:T(8,128)(2,1)}), bf16[32,72,128]{2,1,0:T(8,128)(2,1)}, u32[]{:S(2)}, u32[]{:S(2)}) %all-to-all-start.2) | async-done | bytes 589856 | tf_op jit(solution)/shard_map/all_to_all | solution.py:278
  71.2 0.9 convert_reduce_fusion
  72.2 1.0 slice.205
  73.8 1.0 slice_reduce_fusion
  74.8 0.8 pad_maximum_fusion
  75.6 3.9 %all-to-all-start.3 = ((bf16[16,72,128]{2,1,0:T(8,128)(2,1)}), bf16[16,72,128]{2,1,0:T(8,128)(2,1)S(1)}, u32[]{:S(2)}, u32[]{:S(2)}) async-start(bf16[16,72,128]{2,1,0:T(8,128)(2,1)} %pad_maximum_fusion), calls=%async_computation.3 | async-start | bytes 589824 | tf_op jit(solution)/shard_map/all_to_all | solution.py:278
  79.6 0.8 fusion.3
  80.4 0.9 slice.217
  81.4 11.5 %all-to-all-done.3.got_ref = bf16[16,72,128]{2,1,0:T(8,128)(2,1)S(1)} async-done(((bf16[16,72,128]{2,1,0:T(8,128)(2,1)}), bf16[16,72,128]{2,1,0:T(8,128)(2,1)S(1)}, u32[]{:S(2)}, u32[]{:S(2)}) %all-to-all-start.3) | async-done | bytes 294944 | tf_op jit(solution)/shard_map/all_to_all | solution.py:278
  93.2 0.8 share.1
  94.0 11.2 %all-to-all-start.4 = ((bf16[32,17,2,128]{3,2,1,0:T(2,128)(2,1)}), bf16[32,17,2,128]{3,2,1,0:T(2,128)(2,1)S(1)}, u32[]{:S(2)}, u32[]{:S(2)}) async-start(bf16[32,17,2,128]{3,2,1,0:T(2,128)(2,1)} %bitcast.27), calls=%async_computation.4 | async-start | bytes 557056 | tf_op jit(solution)/shard_map/all_to_all | solution.py:278
  105.9 7.6 %all-to-all-done.4 = bf16[32,17,2,128]{3,2,1,0:T(2,128)(2,1)S(1)} async-done(((bf16[32,17,2,128]{3,2,1,0:T(2,128)(2,1)}), bf16[32,17,2,128]{3,2,1,0:T(2,128)(2,1)S(1)}, u32[]{:S(2)}, u32[]{:S(2)}) %all-to-all-start.4) | async-done | bytes 278560 | tf_op jit(solution)/shard_map/all_to_all | solution.py:278
  113.5 0.8 finish.1
  (57 shorter events, 3.4 us)
Async XLA Ops:
  0.6 35.5 %copy-start = (bf16[512,128]{1,0:T(8,128)(2,1)S(1)}, bf16[512,128]{1,0:T(8,128)(2,1)}, u32[]{:S(2)}) copy-start(bf16[512,128]{1,0:T(8,128)(2,1)} %param.22) | copy-start | bytes 393220
  0.7 0.8 copy-start.1
  3.0 18.8 %all-to-all-start = ((bf16[32,32,128]{2,1,0:T(8,128)(2,1)}), bf16[32,32,128]{2,1,0:T(8,128)(2,1)S(1)}, u32[]{:S(2)}, u32[]{:S(2)}) async-start(bf16[32,32,128]{2,1,0:T(8,128)(2,1)} %edges.1), calls=%async_computation | async-start | bytes 524288 | tf_op jit(solution)/shard_map/all_to_all | solution.py:278
  13.5 22.5 %copy-start.9 = (f32[3,3,128]{2,1,0:T(4,128)S(1)}, f32[3,3,128]{2,1,0:T(4,128)}, u32[]{:S(2)}) copy-start(f32[3,3,128]{2,1,0:T(4,128)} %param.16) | copy-start | bytes 13828
  13.5 22.7 %copy-start.3 = (bf16[1,16,16,128]{3,2,1,0:T(8,128)(2,1)S(1)}, bf16[1,16,16,128]{3,2,1,0:T(8,128)(2,1)}, u32[]{:S(2)}) copy-start(bf16[1,16,16,128]{3,2,1,0:T(8,128)(2,1)} %param.25) | copy-start | bytes 196612
  21.8 26.6 %copy-start.2 = (bf16[1,16,16,128]{3,2,1,0:T(8,128)(2,1)S(1)}, bf16[1,16,16,128]{3,2,1,0:T(8,128)(2,1)}, u32[]{:S(2)}) copy-start(bf16[1,16,16,128]{3,2,1,0:T(8,128)(2,1)} %param.15) | copy-start | bytes 196612
  21.8 26.7 %copy-start.4 = (bf16[128,512]{1,0:T(8,128)(2,1)S(1)}, bf16[128,512]{1,0:T(8,128)(2,1)}, u32[]{:S(2)}) copy-start(bf16[128,512]{1,0:T(8,128)(2,1)} %expand_ref.1) | copy-start | bytes 393220
  21.8 26.7 %copy-start.5 = (f32[512]{0:T(512)S(1)}, f32[512]{0:T(512)}, u32[]{:S(2)}) copy-start(f32[512]{0:T(512)} %param.21) | copy-start | bytes 6148
  21.8 26.7 %copy-start.6 = (f32[128]{0:T(128)S(1)}, f32[128]{0:T(128)}, u32[]{:S(2)}) copy-start(f32[128]{0:T(128)} %param.17) | copy-start | bytes 1540
  21.8 26.7 %copy-start.7 = (f32[128]{0:T(128)S(1)}, f32[128]{0:T(128)}, u32[]{:S(2)}) copy-start(f32[128]{0:T(128)} %param.18) | copy-start | bytes 1540
  21.8 26.7 %copy-start.8 = (f32[128]{0:T(128)S(1)}, f32[128]{0:T(128)}, u32[]{:S(2)}) copy-start(f32[128]{0:T(128)} %param.19) | copy-start | bytes 1540
  22.9 25.1 %all-to-all-start.1 = ((bf16[16,9,4,128]{3,2,1,0:T(4,128)(2,1)}), bf16[16,9,4,128]{3,2,1,0:T(4,128)(2,1)S(1)}, u32[]{:S(2)}, u32[]{:S(2)}) async-start(bf16[16,9,4,128]{3,2,1,0:T(4,128)(2,1)} %bitcast.6), calls=%async_computation.1 | async-start | bytes 294912 | tf_op jit(solution)/shard_map/all_to_all | solution.py:278
  51.2 20.0 %all-to-all-start.2 = ((bf16[32,72,128]{2,1,0:T(8,128)(2,1)}), bf16[32,72,128]{2,1,0:T(8,128)(2,1)}, u32[]{:S(2)}, u32[]{:S(2)}) async-start(bf16[32,72,128]{2,1,0:T(8,128)(2,1)} %get-tuple-element.47), calls=%async_computation.2 | async-start | bytes 1179648 | tf_op jit(solution)/shard_map/all_to_all | solution.py:278
  73.2 6.4 %copy-start.10 = (f32[128]{0:T(128)S(1)}, f32[128]{0:T(128)}, u32[]{:S(2)}) copy-start(f32[128]{0:T(128)} %param.23) | copy-start | bytes 1540
  75.6 17.3 %all-to-all-start.3 = ((bf16[16,72,128]{2,1,0:T(8,128)(2,1)}), bf16[16,72,128]{2,1,0:T(8,128)(2,1)S(1)}, u32[]{:S(2)}, u32[]{:S(2)}) async-start(bf16[16,72,128]{2,1,0:T(8,128)(2,1)} %pad_maximum_fusion), calls=%async_computation.3 | async-start | bytes 589824 | tf_op jit(solution)/shard_map/all_to_all | solution.py:278
  94.0 19.6 %all-to-all-start.4 = ((bf16[32,17,2,128]{3,2,1,0:T(2,128)(2,1)}), bf16[32,17,2,128]{3,2,1,0:T(2,128)(2,1)S(1)}, u32[]{:S(2)}, u32[]{:S(2)}) async-start(bf16[32,17,2,128]{3,2,1,0:T(2,128)(2,1)} %bitcast.27), calls=%async_computation.4 | async-start | bytes 557056 | tf_op jit(solution)/shard_map/all_to_all | solution.py:278

commit v7 on v6

--- a/solution.py
+++ b/solution.py
@@ -414,13 +414,8 @@
     )(place, adjacency.reshape(-1))
 
 
-def choice(wanted, count):
-    chosen = (wanted.reshape(-1, 1) == jnp.arange(count, dtype=jnp.int32)).astype(BF)
-    return lax.optimization_barrier(chosen)
-
-
 def picked(wanted, held):
-    chosen = choice(wanted, held.shape[0])
+    chosen = (wanted.reshape(-1, 1) == jnp.arange(held.shape[0], dtype=jnp.int32)).astype(BF)
     cells = jnp.dot(chosen, held, preferred_element_type=F32).astype(BF)
     return cells.reshape(wanted.shape + held.shape[1:])
 

time: 115 us -> 112 us (0.974)
  local copies, waits for them, and re-layouts: 4.23 us -> 1.64 us
  other arithmetic: 4.11 us -> 1.71 us
  waiting for transfers between devices: 48.4 us -> 50.5 us
    all_to_all x5, waiting for transfers between devices: 48.4 us -> 50.5 us  [swap(): lax.all_to_all(slots, ('face', 'row', 'col'), 0, 0, axis_index_groups=gro...]
  transfers between devices with their start and end apart: 5 -> 5, of which waited for: 5 -> 5; matrix products, arithmetic and copies ran while one was open for 4% -> 2% of each run, Pallas kernels for 1% -> 1%
where the time goes in v7:
time: 112 us; the launch traced here: 111 us
  waiting for transfers between devices  50.5 us (45%)
  starting transfers between devices  46.5 us (42%)
  Pallas kernels  6.45 us (6%)
  matrix products  3.45 us (3%)
  other arithmetic  1.71 us (2%)
  local copies, waits for them, and re-layouts  1.64 us (1%)
  between operations  1.13 us (1%)
    all_to_all x5, waiting for transfers between devices, swap(): lax.all_to_all(slots, ('face', 'row', 'col'), 0, 0, axis_index_groups=gro...  50.5 us
    all_to_all x5, starting transfers between devices, swap(): lax.all_to_all(slots, ('face', 'row', 'col'), 0, 0, axis_index_groups=gro...  46.5 us
    pallas_call x1, Pallas kernels, block_on_tile(): pl.pallas_call(block_kernel, out_shape=(jax.ShapeDtypeStruct(grad_hidden....  2.74 us
  transfers between devices with their start and end apart: 5, of which 5 were waited for; matrix products, arithmetic and copies ran while one was open for 2% of the time, Pallas kernels for 1%

profile of v7, /device:TPU:1, one launch (start us, length us, event | category | flops | bytes accessed | tf_op | source)
XLA Modules:
  0.0 111.4 jit_solution(8480085410975665013)
XLA Ops:
  0.8 0.8 copy-done.1
  1.6 1.4 %edges.1 = bf16[32,32,128]{2,1,0:T(8,128)(2,1)} custom-call(s32[3]{0:T(128)S(1)} %pad_add_fusion.1.place_ref.plan_ref, bf16[16,16,128]{2,1,0:T(8,128)(2,1)S(1)} %bitcast.53), custom_call_target="tpu_custom_call" | custom-call | tf_op jit(solution)/shard_map/edges/pallas_call | solution.py:58
  3.0 10.5 %all-to-all-start = ((bf16[32,32,128]{2,1,0:T(8,128)(2,1)}), bf16[32,32,128]{2,1,0:T(8,128)(2,1)S(1)}, u32[]{:S(2)}, u32[]{:S(2)}) async-start(bf16[32,32,128]{2,1,0:T(8,128)(2,1)} %edges.1), calls=%async_computation | async-start | bytes 524288 | tf_op jit(solution)/shard_map/all_to_all | solution.py:278
  13.7 0.7 plan.1
  14.5 7.3 %all-to-all-done = bf16[32,32,128]{2,1,0:T(8,128)(2,1)S(1)} async-done(((bf16[32,32,128]{2,1,0:T(8,128)(2,1)}), bf16[32,32,128]{2,1,0:T(8,128)(2,1)S(1)}, u32[]{:S(2)}, u32[]{:S(2)}) %all-to-all-start) | async-done | bytes 262176 | tf_op jit(solution)/shard_map/all_to_all | solution.py:278
  21.8 1.2 %fusion.5 = bf16[576,128]{1,0:T(8,128)(2,1)} fusion(bf16[1024,128]{1,0:T(8,128)(2,1)S(1)} %bitcast.63, s32[576]{0:T(1024)S(1)} %eq.97), kind=kOutput, calls=%fused_computation.7 | convolution fusion | flops 151658496 | bytes 411904 | tf_op jit(solution)/shard_map/dot_general | solution.py:419
  23.0 13.0 %all-to-all-start.1 = ((bf16[16,9,4,128]{3,2,1,0:T(4,128)(2,1)}), bf16[16,9,4,128]{3,2,1,0:T(4,128)(2,1)S(1)}, u32[]{:S(2)}, u32[]{:S(2)}) async-start(bf16[16,9,4,128]{3,2,1,0:T(4,128)(2,1)} %bitcast.6), calls=%async_computation.1 | async-start | bytes 294912 | tf_op jit(solution)/shard_map/all_to_all | solution.py:278
  36.3 0.2 fusion.32.grad_hidden_ref
  36.5 11.6 %all-to-all-done.1 = bf16[16,9,4,128]{3,2,1,0:T(4,128)(2,1)S(1)} async-done(((bf16[16,9,4,128]{3,2,1,0:T(4,128)(2,1)}), bf16[16,9,4,128]{3,2,1,0:T(4,128)(2,1)S(1)}, u32[]{:S(2)}, u32[]{:S(2)}) %all-to-all-start.1) | async-done | bytes 147488 | tf_op jit(solution)/shard_map/all_to_all | solution.py:278
  48.1 0.2 fusion.31
  48.5 2.7 %block.1 = (bf16[256,512]{1,0:T(8,128)(2,1)S(1)}, bf16[32,72,128]{2,1,0:T(8,128)(2,1)}, f32[16,16,128]{2,1,0:T(8,128)S(1)}) custom-call(s32[3]{0:T(128)S(1)} %pad_add_fusion.1.place_ref.plan_ref, bf16[18,18,128]{2,1,0:T(8,128)(2,1)S(1)} %maximum_maximum_fusion.padded_ref, bf16[16,16,128]{2,1,0:T(8,128)(2,1)S(1)} %bitcast.57, ...), custom_call_target="tpu_custom_call" | custom-call | tf_op jit(solution)/shard_map/block/pallas_call | solution.py:184
  51.3 7.8 %all-to-all-start.2 = ((bf16[32,72,128]{2,1,0:T(8,128)(2,1)}), bf16[32,72,128]{2,1,0:T(8,128)(2,1)S(1)}, u32[]{:S(2)}, u32[]{:S(2)}) async-start(bf16[32,72,128]{2,1,0:T(8,128)(2,1)} %get-tuple-element.47), calls=%async_computation.2 | async-start | bytes 1179648 | tf_op jit(solution)/shard_map/all_to_all | solution.py:278
  59.2 11.6 %all-to-all-done.2 = bf16[32,72,128]{2,1,0:T(8,128)(2,1)S(1)} async-done(((bf16[32,72,128]{2,1,0:T(8,128)(2,1)}), bf16[32,72,128]{2,1,0:T(8,128)(2,1)S(1)}, u32[]{:S(2)}, u32[]{:S(2)}) %all-to-all-start.2) | async-done | bytes 589856 | tf_op jit(solution)/shard_map/all_to_all | solution.py:278
  70.9 0.7 fusion.4
  71.7 0.8 pad_maximum_fusion
  72.5 4.0 %all-to-all-start.3 = ((bf16[16,72,128]{2,1,0:T(8,128)(2,1)}), bf16[16,72,128]{2,1,0:T(8,128)(2,1)S(1)}, u32[]{:S(2)}, u32[]{:S(2)}) async-start(bf16[16,72,128]{2,1,0:T(8,128)(2,1)} %pad_maximum_fusion), calls=%async_computation.3 | async-start | bytes 589824 | tf_op jit(solution)/shard_map/all_to_all | solution.py:278
  76.6 0.8 fusion.7
  77.4 12.4 %all-to-all-done.3.got_ref = bf16[16,72,128]{2,1,0:T(8,128)(2,1)S(1)} async-done(((bf16[16,72,128]{2,1,0:T(8,128)(2,1)}), bf16[16,72,128]{2,1,0:T(8,128)(2,1)S(1)}, u32[]{:S(2)}, u32[]{:S(2)}) %all-to-all-start.3) | async-done | bytes 294944 | tf_op jit(solution)/shard_map/all_to_all | solution.py:278
  89.9 0.2 fusion.8
  90.2 0.8 share.1
  91.0 11.2 %all-to-all-start.4 = ((bf16[32,17,2,128]{3,2,1,0:T(2,128)(2,1)}), bf16[32,17,2,128]{3,2,1,0:T(2,128)(2,1)S(1)}, u32[]{:S(2)}, u32[]{:S(2)}) async-start(bf16[32,17,2,128]{3,2,1,0:T(2,128)(2,1)} %bitcast.27), calls=%async_computation.4 | async-start | bytes 557056 | tf_op jit(solution)/shard_map/all_to_all | solution.py:278
  102.3 0.7 fusion.18
  102.9 7.6 %all-to-all-done.4 = bf16[32,17,2,128]{3,2,1,0:T(2,128)(2,1)S(1)} async-done(((bf16[32,17,2,128]{3,2,1,0:T(2,128)(2,1)}), bf16[32,17,2,128]{3,2,1,0:T(2,128)(2,1)S(1)}, u32[]{:S(2)}, u32[]{:S(2)}) %all-to-all-start.4) | async-done | bytes 278560 | tf_op jit(solution)/shard_map/all_to_all | solution.py:278
  110.5 0.8 finish.1
  (60 shorter events, 1.1 us)
Async XLA Ops:
  0.6 35.6 %copy-start = (bf16[512,128]{1,0:T(8,128)(2,1)S(1)}, bf16[512,128]{1,0:T(8,128)(2,1)}, u32[]{:S(2)}) copy-start(bf16[512,128]{1,0:T(8,128)(2,1)} %param.22) | copy-start | bytes 393220
  0.7 12.8 %copy-start.11 = (s32[2,4,3]{1,0,2:T(2,128)S(1)}, s32[2,4,3]{1,0,2:T(2,128)}, u32[]{:S(2)}) copy-start(s32[2,4,3]{1,0,2:T(2,128)} %param.24) | copy-start | bytes 292
  0.8 0.8 copy-start.1
  3.0 18.8 %all-to-all-start = ((bf16[32,32,128]{2,1,0:T(8,128)(2,1)}), bf16[32,32,128]{2,1,0:T(8,128)(2,1)S(1)}, u32[]{:S(2)}, u32[]{:S(2)}) async-start(bf16[32,32,128]{2,1,0:T(8,128)(2,1)} %edges.1), calls=%async_computation | async-start | bytes 524288 | tf_op jit(solution)/shard_map/all_to_all | solution.py:278
  21.8 14.3 %copy-start.10 = (f32[3,3,128]{2,1,0:T(4,128)S(1)}, f32[3,3,128]{2,1,0:T(4,128)}, u32[]{:S(2)}) copy-start(f32[3,3,128]{2,1,0:T(4,128)} %param.16) | copy-start | bytes 13828
  21.8 14.4 %copy-start.3 = (bf16[1,16,16,128]{3,2,1,0:T(8,128)(2,1)S(1)}, bf16[1,16,16,128]{3,2,1,0:T(8,128)(2,1)}, u32[]{:S(2)}) copy-start(bf16[1,16,16,128]{3,2,1,0:T(8,128)(2,1)} %param.25) | copy-start | bytes 196612
  23.0 25.1 %all-to-all-start.1 = ((bf16[16,9,4,128]{3,2,1,0:T(4,128)(2,1)}), bf16[16,9,4,128]{3,2,1,0:T(4,128)(2,1)S(1)}, u32[]{:S(2)}, u32[]{:S(2)}) async-start(bf16[16,9,4,128]{3,2,1,0:T(4,128)(2,1)} %bitcast.6), calls=%async_computation.1 | async-start | bytes 294912 | tf_op jit(solution)/shard_map/all_to_all | solution.py:278
  36.2 12.2 %copy-start.2 = (bf16[1,16,16,128]{3,2,1,0:T(8,128)(2,1)S(1)}, bf16[1,16,16,128]{3,2,1,0:T(8,128)(2,1)}, u32[]{:S(2)}) copy-start(bf16[1,16,16,128]{3,2,1,0:T(8,128)(2,1)} %param.15) | copy-start | bytes 196612
  36.2 12.3 %copy-start.4 = (bf16[128,512]{1,0:T(8,128)(2,1)S(1)}, bf16[128,512]{1,0:T(8,128)(2,1)}, u32[]{:S(2)}) copy-start(bf16[128,512]{1,0:T(8,128)(2,1)} %expand_ref.1) | copy-start | bytes 393220
  36.2 12.3 %copy-start.5 = (f32[512]{0:T(512)S(1)}, f32[512]{0:T(512)}, u32[]{:S(2)}) copy-start(f32[512]{0:T(512)} %param.21) | copy-start | bytes 6148
  36.3 12.3 %copy-start.6 = (f32[128]{0:T(128)S(1)}, f32[128]{0:T(128)}, u32[]{:S(2)}) copy-start(f32[128]{0:T(128)} %param.17) | copy-start | bytes 1540
  36.3 12.3 %copy-start.7 = (f32[128]{0:T(128)S(1)}, f32[128]{0:T(128)}, u32[]{:S(2)}) copy-start(f32[128]{0:T(128)} %param.18) | copy-start | bytes 1540
  36.3 12.3 %copy-start.8 = (f32[128]{0:T(128)S(1)}, f32[128]{0:T(128)}, u32[]{:S(2)}) copy-start(f32[128]{0:T(128)} %param.19) | copy-start | bytes 1540
  51.3 19.5 %all-to-all-start.2 = ((bf16[32,72,128]{2,1,0:T(8,128)(2,1)}), bf16[32,72,128]{2,1,0:T(8,128)(2,1)S(1)}, u32[]{:S(2)}, u32[]{:S(2)}) async-start(bf16[32,72,128]{2,1,0:T(8,128)(2,1)} %get-tuple-element.47), calls=%async_computation.2 | async-start | bytes 1179648 | tf_op jit(solution)/shard_map/all_to_all | solution.py:278
  70.8 6.7 %copy-start.9 = (bf16[32,72,128]{2,1,0:T(8,128)(2,1)}, bf16[32,72,128]{2,1,0:T(8,128)(2,1)S(1)}, u32[]{:S(2)}) copy-start(bf16[32,72,128]{2,1,0:T(8,128)(2,1)S(1)} %all-to-all-done.2) | copy-start | bytes 1769476
  71.7 4.9 %copy-start.12 = (f32[128]{0:T(128)S(1)}, f32[128]{0:T(128)}, u32[]{:S(2)}) copy-start(f32[128]{0:T(128)} %param.23) | copy-start | bytes 1540
  72.5 17.4 %all-to-all-start.3 = ((bf16[16,72,128]{2,1,0:T(8,128)(2,1)}), bf16[16,72,128]{2,1,0:T(8,128)(2,1)S(1)}, u32[]{:S(2)}, u32[]{:S(2)}) async-start(bf16[16,72,128]{2,1,0:T(8,128)(2,1)} %pad_maximum_fusion), calls=%async_computation.3 | async-start | bytes 589824 | tf_op jit(solution)/shard_map/all_to_all | solution.py:278
  90.2 12.1 %slice-start = ((bf16[32,72,128]{2,1,0:T(8,128)(2,1)}), bf16[32,16,128]{2,1,0:T(8,128)(2,1)S(1)}, s32[]{:S(2)}) async-start(bf16[32,72,128]{2,1,0:T(8,128)(2,1)} %copy-done.9), calls=%async_computation.5 | async-start | bytes 262144 | tf_op jit(solution)/shard_map/slice | solution.py:551
  91.0 19.6 %all-to-all-start.4 = ((bf16[32,17,2,128]{3,2,1,0:T(2,128)(2,1)}), bf16[32,17,2,128]{3,2,1,0:T(2,128)(2,1)S(1)}, u32[]{:S(2)}, u32[]{:S(2)}) async-start(bf16[32,17,2,128]{3,2,1,0:T(2,128)(2,1)} %bitcast.27), calls=%async_computation.4 | async-start | bytes 557056 | tf_op jit(solution)/shard_map/all_to_all | solution.py:278

commit v8 on v7

--- a/solution.py
+++ b/solution.py
@@ -295,7 +295,7 @@
         for low in steps
     ]
     lines = [
-        [device(f, y, x, high, low) for high in steps for low in steps]
+        [device(f, y, x, high, low) for high in steps for low in steps][:: 1 - 2 * f]
         for f in range(2)
         for y in steps
         for x in steps
@@ -368,6 +368,7 @@
     y, x = r // cut, c % cut
     here = c // cut * cut + r % cut
     others = lax.broadcasted_iota(jnp.int32, (side, 128), 0)
+    others = jnp.where(f == 1, side - 1 - others, others)
     lane = lax.broadcasted_iota(jnp.int32, (side, 128), 1)
     main = lane < 2 * cells
     step = jnp.where(main, lane & (cells - 1), jnp.where((lane & 1) == 0, -1, cells))

time: 112 us -> 112 us (level)
  waiting for transfers between devices: 50.5 us -> 56.5 us
  starting transfers between devices: 46.5 us -> 40.6 us
    all_to_all x5, waiting for transfers between devices: 50.5 us -> 56.5 us  [swap(): lax.all_to_all(slots, ('face', 'row', 'col'), 0, 0, axis_index_groups=gro...]
    all_to_all x5, starting transfers between devices: 46.5 us -> 40.6 us  [swap(): lax.all_to_all(slots, ('face', 'row', 'col'), 0, 0, axis_index_groups=gro...]
where the time goes in v8:
time: 112 us; the launch traced here: 111 us
  waiting for transfers between devices  56.5 us (50%)
  starting transfers between devices  40.6 us (36%)
  Pallas kernels  6.45 us (6%)
  matrix products  3.45 us (3%)
  other arithmetic  1.71 us (2%)
  local copies, waits for them, and re-layouts  1.64 us (1%)
    all_to_all x5, waiting for transfers between devices, swap(): lax.all_to_all(slots, ('face', 'row', 'col'), 0, 0, axis_index_groups=gro...  56.5 us
    all_to_all x5, starting transfers between devices, swap(): lax.all_to_all(slots, ('face', 'row', 'col'), 0, 0, axis_index_groups=gro...  40.6 us
    pallas_call x1, Pallas kernels, block_on_tile(): pl.pallas_call(block_kernel, out_shape=(jax.ShapeDtypeStruct(grad_hidden....  2.74 us
  transfers between devices with their start and end apart: 5, of which 5 were waited for; matrix products, arithmetic and copies ran while one was open for 2% of the time, Pallas kernels for 1%

profile of v8, /device:TPU:1, one launch (start us, length us, event | category | flops | bytes accessed | tf_op | source)
XLA Modules:
  0.0 111.5 jit_solution(7008329337774428785)
XLA Ops:
  0.8 0.8 copy-done.1
  1.6 1.4 %edges.1 = bf16[32,32,128]{2,1,0:T(8,128)(2,1)} custom-call(s32[3]{0:T(128)S(1)} %pad_add_fusion.1.place_ref.plan_ref, bf16[16,16,128]{2,1,0:T(8,128)(2,1)S(1)} %bitcast.53), custom_call_target="tpu_custom_call" | custom-call | tf_op jit(solution)/shard_map/edges/pallas_call | solution.py:58
  3.0 10.5 %all-to-all-start = ((bf16[32,32,128]{2,1,0:T(8,128)(2,1)}), bf16[32,32,128]{2,1,0:T(8,128)(2,1)S(1)}, u32[]{:S(2)}, u32[]{:S(2)}) async-start(bf16[32,32,128]{2,1,0:T(8,128)(2,1)} %edges.1), calls=%async_computation | async-start | bytes 524288 | tf_op jit(solution)/shard_map/all_to_all | solution.py:278
  13.7 0.7 plan.1
  14.5 7.3 %all-to-all-done = bf16[32,32,128]{2,1,0:T(8,128)(2,1)S(1)} async-done(((bf16[32,32,128]{2,1,0:T(8,128)(2,1)}), bf16[32,32,128]{2,1,0:T(8,128)(2,1)S(1)}, u32[]{:S(2)}, u32[]{:S(2)}) %all-to-all-start) | async-done | bytes 262176 | tf_op jit(solution)/shard_map/all_to_all | solution.py:278
  21.8 1.2 %fusion.5 = bf16[576,128]{1,0:T(8,128)(2,1)} fusion(bf16[1024,128]{1,0:T(8,128)(2,1)S(1)} %bitcast.63, s32[576]{0:T(1024)S(1)} %eq.97), kind=kOutput, calls=%fused_computation.7 | convolution fusion | flops 151658496 | bytes 411904 | tf_op jit(solution)/shard_map/dot_general | solution.py:420
  23.0 13.2 %all-to-all-start.1 = ((bf16[16,9,4,128]{3,2,1,0:T(4,128)(2,1)}), bf16[16,9,4,128]{3,2,1,0:T(4,128)(2,1)S(1)}, u32[]{:S(2)}, u32[]{:S(2)}) async-start(bf16[16,9,4,128]{3,2,1,0:T(4,128)(2,1)} %bitcast.6), calls=%async_computation.1 | async-start | bytes 294912 | tf_op jit(solution)/shard_map/all_to_all | solution.py:278
  36.4 0.2 fusion.32.grad_hidden_ref
  36.7 11.8 %all-to-all-done.1 = bf16[16,9,4,128]{3,2,1,0:T(4,128)(2,1)S(1)} async-done(((bf16[16,9,4,128]{3,2,1,0:T(4,128)(2,1)}), bf16[16,9,4,128]{3,2,1,0:T(4,128)(2,1)S(1)}, u32[]{:S(2)}, u32[]{:S(2)}) %all-to-all-start.1) | async-done | bytes 147488 | tf_op jit(solution)/shard_map/all_to_all | solution.py:278
  48.4 0.2 fusion.31
  48.9 2.7 %block.1 = (bf16[256,512]{1,0:T(8,128)(2,1)S(1)}, bf16[32,72,128]{2,1,0:T(8,128)(2,1)}, f32[16,16,128]{2,1,0:T(8,128)S(1)}) custom-call(s32[3]{0:T(128)S(1)} %pad_add_fusion.1.place_ref.plan_ref, bf16[18,18,128]{2,1,0:T(8,128)(2,1)S(1)} %maximum_maximum_fusion.padded_ref, bf16[16,16,128]{2,1,0:T(8,128)(2,1)S(1)} %bitcast.57, ...), custom_call_target="tpu_custom_call" | custom-call | tf_op jit(solution)/shard_map/block/pallas_call | solution.py:184
  51.6 7.1 %all-to-all-start.2 = ((bf16[32,72,128]{2,1,0:T(8,128)(2,1)}), bf16[32,72,128]{2,1,0:T(8,128)(2,1)S(1)}, u32[]{:S(2)}, u32[]{:S(2)}) async-start(bf16[32,72,128]{2,1,0:T(8,128)(2,1)} %get-tuple-element.47), calls=%async_computation.2 | async-start | bytes 1179648 | tf_op jit(solution)/shard_map/all_to_all | solution.py:278
  58.8 11.6 %all-to-all-done.2 = bf16[32,72,128]{2,1,0:T(8,128)(2,1)S(1)} async-done(((bf16[32,72,128]{2,1,0:T(8,128)(2,1)}), bf16[32,72,128]{2,1,0:T(8,128)(2,1)S(1)}, u32[]{:S(2)}, u32[]{:S(2)}) %all-to-all-start.2) | async-done | bytes 589856 | tf_op jit(solution)/shard_map/all_to_all | solution.py:278
  70.5 0.7 fusion.4
  71.4 0.8 pad_maximum_fusion
  72.1 5.1 %all-to-all-start.3 = ((bf16[16,72,128]{2,1,0:T(8,128)(2,1)}), bf16[16,72,128]{2,1,0:T(8,128)(2,1)S(1)}, u32[]{:S(2)}, u32[]{:S(2)}) async-start(bf16[16,72,128]{2,1,0:T(8,128)(2,1)} %pad_maximum_fusion), calls=%async_computation.3 | async-start | bytes 589824 | tf_op jit(solution)/shard_map/all_to_all | solution.py:278
  77.3 0.8 fusion.7
  78.1 18.3 %all-to-all-done.3.got_ref = bf16[16,72,128]{2,1,0:T(8,128)(2,1)S(1)} async-done(((bf16[16,72,128]{2,1,0:T(8,128)(2,1)}), bf16[16,72,128]{2,1,0:T(8,128)(2,1)S(1)}, u32[]{:S(2)}, u32[]{:S(2)}) %all-to-all-start.3) | async-done | bytes 294944 | tf_op jit(solution)/shard_map/all_to_all | solution.py:278
  96.4 0.2 fusion.8
  96.7 0.8 share.1
  97.4 4.8 %all-to-all-start.4 = ((bf16[32,17,2,128]{3,2,1,0:T(2,128)(2,1)}), bf16[32,17,2,128]{3,2,1,0:T(2,128)(2,1)S(1)}, u32[]{:S(2)}, u32[]{:S(2)}) async-start(bf16[32,17,2,128]{3,2,1,0:T(2,128)(2,1)} %bitcast.27), calls=%async_computation.4 | async-start | bytes 557056 | tf_op jit(solution)/shard_map/all_to_all | solution.py:278
  102.3 0.7 fusion.18
  103.0 7.6 %all-to-all-done.4 = bf16[32,17,2,128]{3,2,1,0:T(2,128)(2,1)S(1)} async-done(((bf16[32,17,2,128]{3,2,1,0:T(2,128)(2,1)}), bf16[32,17,2,128]{3,2,1,0:T(2,128)(2,1)S(1)}, u32[]{:S(2)}, u32[]{:S(2)}) %all-to-all-start.4) | async-done | bytes 278560 | tf_op jit(solution)/shard_map/all_to_all | solution.py:278
  110.6 0.8 finish.1
  (60 shorter events, 1.1 us)
Async XLA Ops:
  0.6 35.7 %copy-start = (bf16[512,128]{1,0:T(8,128)(2,1)S(1)}, bf16[512,128]{1,0:T(8,128)(2,1)}, u32[]{:S(2)}) copy-start(bf16[512,128]{1,0:T(8,128)(2,1)} %param.22) | copy-start | bytes 393220
  0.7 12.8 %copy-start.11 = (s32[2,4,3]{1,0,2:T(2,128)S(1)}, s32[2,4,3]{1,0,2:T(2,128)}, u32[]{:S(2)}) copy-start(s32[2,4,3]{1,0,2:T(2,128)} %param.24) | copy-start | bytes 292
  0.8 0.8 copy-start.1
  3.0 18.8 %all-to-all-start = ((bf16[32,32,128]{2,1,0:T(8,128)(2,1)}), bf16[32,32,128]{2,1,0:T(8,128)(2,1)S(1)}, u32[]{:S(2)}, u32[]{:S(2)}) async-start(bf16[32,32,128]{2,1,0:T(8,128)(2,1)} %edges.1), calls=%async_computation | async-start | bytes 524288 | tf_op jit(solution)/shard_map/all_to_all | solution.py:278
  21.8 14.4 %copy-start.10 = (f32[3,3,128]{2,1,0:T(4,128)S(1)}, f32[3,3,128]{2,1,0:T(4,128)}, u32[]{:S(2)}) copy-start(f32[3,3,128]{2,1,0:T(4,128)} %param.16) | copy-start | bytes 13828
  21.8 14.6 %copy-start.3 = (bf16[1,16,16,128]{3,2,1,0:T(8,128)(2,1)S(1)}, bf16[1,16,16,128]{3,2,1,0:T(8,128)(2,1)}, u32[]{:S(2)}) copy-start(bf16[1,16,16,128]{3,2,1,0:T(8,128)(2,1)} %param.25) | copy-start | bytes 196612
  23.0 25.4 %all-to-all-start.1 = ((bf16[16,9,4,128]{3,2,1,0:T(4,128)(2,1)}), bf16[16,9,4,128]{3,2,1,0:T(4,128)(2,1)S(1)}, u32[]{:S(2)}, u32[]{:S(2)}) async-start(bf16[16,9,4,128]{3,2,1,0:T(4,128)(2,1)} %bitcast.6), calls=%async_computation.1 | async-start | bytes 294912 | tf_op jit(solution)/shard_map/all_to_all | solution.py:278
  36.4 12.4 %copy-start.2 = (bf16[1,16,16,128]{3,2,1,0:T(8,128)(2,1)S(1)}, bf16[1,16,16,128]{3,2,1,0:T(8,128)(2,1)}, u32[]{:S(2)}) copy-start(bf16[1,16,16,128]{3,2,1,0:T(8,128)(2,1)} %param.15) | copy-start | bytes 196612
  36.4 12.5 %copy-start.4 = (bf16[128,512]{1,0:T(8,128)(2,1)S(1)}, bf16[128,512]{1,0:T(8,128)(2,1)}, u32[]{:S(2)}) copy-start(bf16[128,512]{1,0:T(8,128)(2,1)} %expand_ref.1) | copy-start | bytes 393220
  36.4 12.5 %copy-start.5 = (f32[512]{0:T(512)S(1)}, f32[512]{0:T(512)}, u32[]{:S(2)}) copy-start(f32[512]{0:T(512)} %param.21) | copy-start | bytes 6148
  36.4 12.5 %copy-start.6 = (f32[128]{0:T(128)S(1)}, f32[128]{0:T(128)}, u32[]{:S(2)}) copy-start(f32[128]{0:T(128)} %param.17) | copy-start | bytes 1540
  36.4 12.5 %copy-start.7 = (f32[128]{0:T(128)S(1)}, f32[128]{0:T(128)}, u32[]{:S(2)}) copy-start(f32[128]{0:T(128)} %param.18) | copy-start | bytes 1540
  36.4 12.5 %copy-start.8 = (f32[128]{0:T(128)S(1)}, f32[128]{0:T(128)}, u32[]{:S(2)}) copy-start(f32[128]{0:T(128)} %param.19) | copy-start | bytes 1540
  51.6 18.8 %all-to-all-start.2 = ((bf16[32,72,128]{2,1,0:T(8,128)(2,1)}), bf16[32,72,128]{2,1,0:T(8,128)(2,1)S(1)}, u32[]{:S(2)}, u32[]{:S(2)}) async-start(bf16[32,72,128]{2,1,0:T(8,128)(2,1)} %get-tuple-element.47), calls=%async_computation.2 | async-start | bytes 1179648 | tf_op jit(solution)/shard_map/all_to_all | solution.py:278
  70.4 7.7 %copy-start.9 = (bf16[32,72,128]{2,1,0:T(8,128)(2,1)}, bf16[32,72,128]{2,1,0:T(8,128)(2,1)S(1)}, u32[]{:S(2)}) copy-start(bf16[32,72,128]{2,1,0:T(8,128)(2,1)S(1)} %all-to-all-done.2) | copy-start | bytes 1769476
  71.3 5.9 %copy-start.12 = (f32[128]{0:T(128)S(1)}, f32[128]{0:T(128)}, u32[]{:S(2)}) copy-start(f32[128]{0:T(128)} %param.23) | copy-start | bytes 1540
  72.1 24.3 %all-to-all-start.3 = ((bf16[16,72,128]{2,1,0:T(8,128)(2,1)}), bf16[16,72,128]{2,1,0:T(8,128)(2,1)S(1)}, u32[]{:S(2)}, u32[]{:S(2)}) async-start(bf16[16,72,128]{2,1,0:T(8,128)(2,1)} %pad_maximum_fusion), calls=%async_computation.3 | async-start | bytes 589824 | tf_op jit(solution)/shard_map/all_to_all | solution.py:278
  96.7 5.7 %slice-start = ((bf16[32,72,128]{2,1,0:T(8,128)(2,1)}), bf16[32,16,128]{2,1,0:T(8,128)(2,1)S(1)}, s32[]{:S(2)}) async-start(bf16[32,72,128]{2,1,0:T(8,128)(2,1)} %copy-done.9), calls=%async_computation.5 | async-start | bytes 262144 | tf_op jit(solution)/shard_map/slice | solution.py:552
  97.4 13.2 %all-to-all-start.4 = ((bf16[32,17,2,128]{3,2,1,0:T(2,128)(2,1)}), bf16[32,17,2,128]{3,2,1,0:T(2,128)(2,1)S(1)}, u32[]{:S(2)}, u32[]{:S(2)}) async-start(bf16[32,17,2,128]{3,2,1,0:T(2,128)(2,1)} %bitcast.27), calls=%async_computation.4 | async-start | bytes 557056 | tf_op jit(solution)/shard_map/all_to_all | solution.py:278

commit v9 on v8

--- a/solution.py
+++ b/solution.py
@@ -42,15 +42,15 @@
     slots, depth, _ = sent_ref.shape
     rows = depth // 2
     tile = tile_ref[...].astype(F32)
-    north, south = tile[0], tile[rows - 1]
-    west = jnp.concatenate([tile[k, 0:1] for k in range(rows)])
-    east = jnp.concatenate([tile[k, rows - 1 : rows] for k in range(rows)])
+    north, south = tile_ref[0], tile_ref[rows - 1]
+    west = jnp.concatenate([tile[k, 0:1] for k in range(rows)]).astype(BF)
+    east = jnp.concatenate([tile[k, rows - 1 : rows] for k in range(rows)]).astype(BF)
     for slot in range(slots):
         near, far = slot_strips(
             place_ref[0], place_ref[1], place_ref[2], slot, slots // 2, north, south, west, east
         )
-        sent_ref[slot, 0:rows] = near.astype(BF)
-        sent_ref[slot, rows:depth] = far.astype(BF)
+        sent_ref[slot, 0:rows] = near
+        sent_ref[slot, rows:depth] = far
 
 
 def edges_of(place, tile, slots):
@@ -163,18 +163,29 @@
     extra = sent_ref.shape[1] - many - 2 * rows
     place = lax.broadcasted_iota(jnp.int32, (extra, channels), 0)
     near = many + rows
+    rims = (north, south, west, east)
+    inner = [strip[1 : rim - 1].astype(BF) for strip in rims]
+
+    def ends_at(start):
+        return [
+            jnp.where(
+                place == start, strip[0:1], jnp.where(place == start + 1, strip[rim - 1 : rim], 0.0)
+            )
+            for strip in rims
+        ]
+
+    near_ends, far_ends = ends_at(0), ends_at(2)
     for slot in range(slots):
-        strip, side_strip = slot_strips(face, row, col, slot, side, north, south, west, east)
-        sent_ref[slot, many:near] = strip[1 : rim - 1].astype(BF)
-        sent_ref[slot, near : near + rows] = side_strip[1 : rim - 1].astype(BF)
-        ends = [strip[0:1], strip[rim - 1 : rim], side_strip[0:1], side_strip[rim - 1 : rim]]
-        values = ends
-        for k in range(few * slot, min(few * slot + few, len(small))):
+        strip, side_strip = slot_strips(face, row, col, slot, side, *inner)
+        sent_ref[slot, many:near] = strip
+        sent_ref[slot, near : near + rows] = side_strip
+        block, _ = slot_strips(face, row, col, slot, side, *near_ends)
+        _, side_block = slot_strips(face, row, col, slot, side, *far_ends)
+        block = block + side_block
+        for j, k in enumerate(range(few * slot, min(few * slot + few, len(small)))):
             high = small[k].astype(BF).astype(F32)
-            values = values + [high, small[k] - high]
-        block = jnp.zeros((extra, channels), F32)
-        for k, value in enumerate(values):
-            block = jnp.where(place == k, value, block)
+            block = jnp.where(place == 4 + 2 * j, high, block)
+            block = jnp.where(place == 5 + 2 * j, small[k] - high, block)
         sent_ref[slot, near + rows : near + rows + extra] = block.astype(BF)
 
 

time: 112 us -> 112 us (level)
  no operation moved by 1% of the time
where the time goes in v9:
time: 112 us; the launch traced here: 111 us
  waiting for transfers between devices  56.5 us (50%)
  starting transfers between devices  40.6 us (36%)
  Pallas kernels  6.45 us (6%)
  matrix products  3.46 us (3%)
  other arithmetic  1.71 us (2%)
  local copies, waits for them, and re-layouts  1.64 us (1%)
    all_to_all x5, waiting for transfers between devices, swap(): lax.all_to_all(slots, ('face', 'row', 'col'), 0, 0, axis_index_groups=gro...  56.5 us
    all_to_all x5, starting transfers between devices, swap(): lax.all_to_all(slots, ('face', 'row', 'col'), 0, 0, axis_index_groups=gro...  40.6 us
    pallas_call x1, Pallas kernels, block_on_tile(): pl.pallas_call(block_kernel, out_shape=(jax.ShapeDtypeStruct(grad_hidden....  2.73 us
  transfers between devices with their start and end apart: 5, of which 5 were waited for; matrix products, arithmetic and copies ran while one was open for 2% of the time, Pallas kernels for 1%

profile of v9, /device:TPU:1, one launch (start us, length us, event | category | flops | bytes accessed | tf_op | source)
XLA Modules:
  0.0 111.5 jit_solution(17372104412638942487)
XLA Ops:
  0.8 0.8 copy-done.1
  1.6 1.4 %edges.1 = bf16[32,32,128]{2,1,0:T(8,128)(2,1)} custom-call(s32[3]{0:T(128)S(1)} %pad_add_fusion.1.place_ref.plan_ref, bf16[16,16,128]{2,1,0:T(8,128)(2,1)S(1)} %bitcast.53), custom_call_target="tpu_custom_call" | custom-call | tf_op jit(solution)/shard_map/edges/pallas_call | solution.py:58
  3.0 10.5 %all-to-all-start = ((bf16[32,32,128]{2,1,0:T(8,128)(2,1)}), bf16[32,32,128]{2,1,0:T(8,128)(2,1)S(1)}, u32[]{:S(2)}, u32[]{:S(2)}) async-start(bf16[32,32,128]{2,1,0:T(8,128)(2,1)} %edges.1), calls=%async_computation | async-start | bytes 524288 | tf_op jit(solution)/shard_map/all_to_all | solution.py:289
  13.7 0.7 plan.1
  14.5 7.3 %all-to-all-done = bf16[32,32,128]{2,1,0:T(8,128)(2,1)S(1)} async-done(((bf16[32,32,128]{2,1,0:T(8,128)(2,1)}), bf16[32,32,128]{2,1,0:T(8,128)(2,1)S(1)}, u32[]{:S(2)}, u32[]{:S(2)}) %all-to-all-start) | async-done | bytes 262176 | tf_op jit(solution)/shard_map/all_to_all | solution.py:289
  21.8 1.2 %fusion.5 = bf16[576,128]{1,0:T(8,128)(2,1)} fusion(bf16[1024,128]{1,0:T(8,128)(2,1)S(1)} %bitcast.63, s32[576]{0:T(1024)S(1)} %eq.97), kind=kOutput, calls=%fused_computation.7 | convolution fusion | flops 151658496 | bytes 411904 | tf_op jit(solution)/shard_map/dot_general | solution.py:431
  23.0 13.2 %all-to-all-start.1 = ((bf16[16,9,4,128]{3,2,1,0:T(4,128)(2,1)}), bf16[16,9,4,128]{3,2,1,0:T(4,128)(2,1)S(1)}, u32[]{:S(2)}, u32[]{:S(2)}) async-start(bf16[16,9,4,128]{3,2,1,0:T(4,128)(2,1)} %bitcast.6), calls=%async_computation.1 | async-start | bytes 294912 | tf_op jit(solution)/shard_map/all_to_all | solution.py:289
  36.4 0.2 fusion.32.grad_hidden_ref
  36.7 11.8 %all-to-all-done.1 = bf16[16,9,4,128]{3,2,1,0:T(4,128)(2,1)S(1)} async-done(((bf16[16,9,4,128]{3,2,1,0:T(4,128)(2,1)}), bf16[16,9,4,128]{3,2,1,0:T(4,128)(2,1)S(1)}, u32[]{:S(2)}, u32[]{:S(2)}) %all-to-all-start.1) | async-done | bytes 147488 | tf_op jit(solution)/shard_map/all_to_all | solution.py:289
  48.4 0.2 fusion.31
  48.9 2.7 %block.1 = (bf16[256,512]{1,0:T(8,128)(2,1)S(1)}, bf16[32,72,128]{2,1,0:T(8,128)(2,1)}, f32[16,16,128]{2,1,0:T(8,128)S(1)}) custom-call(s32[3]{0:T(128)S(1)} %pad_add_fusion.1.place_ref.plan_ref, bf16[18,18,128]{2,1,0:T(8,128)(2,1)S(1)} %maximum_maximum_fusion.padded_ref, bf16[16,16,128]{2,1,0:T(8,128)(2,1)S(1)} %bitcast.57, ...), custom_call_target="tpu_custom_call" | custom-call | tf_op jit(solution)/shard_map/block/pallas_call | solution.py:195
  51.6 7.1 %all-to-all-start.2 = ((bf16[32,72,128]{2,1,0:T(8,128)(2,1)}), bf16[32,72,128]{2,1,0:T(8,128)(2,1)S(1)}, u32[]{:S(2)}, u32[]{:S(2)}) async-start(bf16[32,72,128]{2,1,0:T(8,128)(2,1)} %get-tuple-element.47), calls=%async_computation.2 | async-start | bytes 1179648 | tf_op jit(solution)/shard_map/all_to_all | solution.py:289
  58.8 11.6 %all-to-all-done.2 = bf16[32,72,128]{2,1,0:T(8,128)(2,1)S(1)} async-done(((bf16[32,72,128]{2,1,0:T(8,128)(2,1)}), bf16[32,72,128]{2,1,0:T(8,128)(2,1)S(1)}, u32[]{:S(2)}, u32[]{:S(2)}) %all-to-all-start.2) | async-done | bytes 589856 | tf_op jit(solution)/shard_map/all_to_all | solution.py:289
  70.5 0.7 fusion.4
  71.3 0.8 pad_maximum_fusion
  72.1 5.1 %all-to-all-start.3 = ((bf16[16,72,128]{2,1,0:T(8,128)(2,1)}), bf16[16,72,128]{2,1,0:T(8,128)(2,1)S(1)}, u32[]{:S(2)}, u32[]{:S(2)}) async-start(bf16[16,72,128]{2,1,0:T(8,128)(2,1)} %pad_maximum_fusion), calls=%async_computation.3 | async-start | bytes 589824 | tf_op jit(solution)/shard_map/all_to_all | solution.py:289
  77.3 0.9 fusion.7
  78.1 18.3 %all-to-all-done.3.got_ref = bf16[16,72,128]{2,1,0:T(8,128)(2,1)S(1)} async-done(((bf16[16,72,128]{2,1,0:T(8,128)(2,1)}), bf16[16,72,128]{2,1,0:T(8,128)(2,1)S(1)}, u32[]{:S(2)}, u32[]{:S(2)}) %all-to-all-start.3) | async-done | bytes 294944 | tf_op jit(solution)/shard_map/all_to_all | solution.py:289
  96.4 0.2 fusion.8
  96.7 0.8 share.1
  97.4 4.8 %all-to-all-start.4 = ((bf16[32,17,2,128]{3,2,1,0:T(2,128)(2,1)}), bf16[32,17,2,128]{3,2,1,0:T(2,128)(2,1)S(1)}, u32[]{:S(2)}, u32[]{:S(2)}) async-start(bf16[32,17,2,128]{3,2,1,0:T(2,128)(2,1)} %bitcast.27), calls=%async_computation.4 | async-start | bytes 557056 | tf_op jit(solution)/shard_map/all_to_all | solution.py:289
  102.3 0.7 fusion.18
  103.0 7.6 %all-to-all-done.4 = bf16[32,17,2,128]{3,2,1,0:T(2,128)(2,1)S(1)} async-done(((bf16[32,17,2,128]{3,2,1,0:T(2,128)(2,1)}), bf16[32,17,2,128]{3,2,1,0:T(2,128)(2,1)S(1)}, u32[]{:S(2)}, u32[]{:S(2)}) %all-to-all-start.4) | async-done | bytes 278560 | tf_op jit(solution)/shard_map/all_to_all | solution.py:289
  110.6 0.8 finish.1
  (60 shorter events, 1.1 us)
Async XLA Ops:
  0.6 35.7 %copy-start = (bf16[512,128]{1,0:T(8,128)(2,1)S(1)}, bf16[512,128]{1,0:T(8,128)(2,1)}, u32[]{:S(2)}) copy-start(bf16[512,128]{1,0:T(8,128)(2,1)} %param.22) | copy-start | bytes 393220
  0.7 12.8 %copy-start.11 = (s32[2,4,3]{1,0,2:T(2,128)S(1)}, s32[2,4,3]{1,0,2:T(2,128)}, u32[]{:S(2)}) copy-start(s32[2,4,3]{1,0,2:T(2,128)} %param.24) | copy-start | bytes 292
  0.8 0.8 copy-start.1
  3.0 18.8 %all-to-all-start = ((bf16[32,32,128]{2,1,0:T(8,128)(2,1)}), bf16[32,32,128]{2,1,0:T(8,128)(2,1)S(1)}, u32[]{:S(2)}, u32[]{:S(2)}) async-start(bf16[32,32,128]{2,1,0:T(8,128)(2,1)} %edges.1), calls=%async_computation | async-start | bytes 524288 | tf_op jit(solution)/shard_map/all_to_all | solution.py:289
  21.8 14.4 %copy-start.10 = (f32[3,3,128]{2,1,0:T(4,128)S(1)}, f32[3,3,128]{2,1,0:T(4,128)}, u32[]{:S(2)}) copy-start(f32[3,3,128]{2,1,0:T(4,128)} %param.16) | copy-start | bytes 13828
  21.8 14.6 %copy-start.3 = (bf16[1,16,16,128]{3,2,1,0:T(8,128)(2,1)S(1)}, bf16[1,16,16,128]{3,2,1,0:T(8,128)(2,1)}, u32[]{:S(2)}) copy-start(bf16[1,16,16,128]{3,2,1,0:T(8,128)(2,1)} %param.25) | copy-start | bytes 196612
  23.0 25.4 %all-to-all-start.1 = ((bf16[16,9,4,128]{3,2,1,0:T(4,128)(2,1)}), bf16[16,9,4,128]{3,2,1,0:T(4,128)(2,1)S(1)}, u32[]{:S(2)}, u32[]{:S(2)}) async-start(bf16[16,9,4,128]{3,2,1,0:T(4,128)(2,1)} %bitcast.6), calls=%async_computation.1 | async-start | bytes 294912 | tf_op jit(solution)/shard_map/all_to_all | solution.py:289
  36.4 12.4 %copy-start.2 = (bf16[1,16,16,128]{3,2,1,0:T(8,128)(2,1)S(1)}, bf16[1,16,16,128]{3,2,1,0:T(8,128)(2,1)}, u32[]{:S(2)}) copy-start(bf16[1,16,16,128]{3,2,1,0:T(8,128)(2,1)} %param.15) | copy-start | bytes 196612
  36.4 12.5 %copy-start.4 = (bf16[128,512]{1,0:T(8,128)(2,1)S(1)}, bf16[128,512]{1,0:T(8,128)(2,1)}, u32[]{:S(2)}) copy-start(bf16[128,512]{1,0:T(8,128)(2,1)} %expand_ref.1) | copy-start | bytes 393220
  36.4 12.5 %copy-start.5 = (f32[512]{0:T(512)S(1)}, f32[512]{0:T(512)}, u32[]{:S(2)}) copy-start(f32[512]{0:T(512)} %param.21) | copy-start | bytes 6148
  36.4 12.5 %copy-start.6 = (f32[128]{0:T(128)S(1)}, f32[128]{0:T(128)}, u32[]{:S(2)}) copy-start(f32[128]{0:T(128)} %param.17) | copy-start | bytes 1540
  36.4 12.5 %copy-start.7 = (f32[128]{0:T(128)S(1)}, f32[128]{0:T(128)}, u32[]{:S(2)}) copy-start(f32[128]{0:T(128)} %param.18) | copy-start | bytes 1540
  36.4 12.5 %copy-start.8 = (f32[128]{0:T(128)S(1)}, f32[128]{0:T(128)}, u32[]{:S(2)}) copy-start(f32[128]{0:T(128)} %param.19) | copy-start | bytes 1540
  51.6 18.8 %all-to-all-start.2 = ((bf16[32,72,128]{2,1,0:T(8,128)(2,1)}), bf16[32,72,128]{2,1,0:T(8,128)(2,1)S(1)}, u32[]{:S(2)}, u32[]{:S(2)}) async-start(bf16[32,72,128]{2,1,0:T(8,128)(2,1)} %get-tuple-element.47), calls=%async_computation.2 | async-start | bytes 1179648 | tf_op jit(solution)/shard_map/all_to_all | solution.py:289
  70.4 7.7 %copy-start.9 = (bf16[32,72,128]{2,1,0:T(8,128)(2,1)}, bf16[32,72,128]{2,1,0:T(8,128)(2,1)S(1)}, u32[]{:S(2)}) copy-start(bf16[32,72,128]{2,1,0:T(8,128)(2,1)S(1)} %all-to-all-done.2) | copy-start | bytes 1769476
  71.3 5.9 %copy-start.12 = (f32[128]{0:T(128)S(1)}, f32[128]{0:T(128)}, u32[]{:S(2)}) copy-start(f32[128]{0:T(128)} %param.23) | copy-start | bytes 1540
  72.1 24.3 %all-to-all-start.3 = ((bf16[16,72,128]{2,1,0:T(8,128)(2,1)}), bf16[16,72,128]{2,1,0:T(8,128)(2,1)S(1)}, u32[]{:S(2)}, u32[]{:S(2)}) async-start(bf16[16,72,128]{2,1,0:T(8,128)(2,1)} %pad_maximum_fusion), calls=%async_computation.3 | async-start | bytes 589824 | tf_op jit(solution)/shard_map/all_to_all | solution.py:289
  96.7 5.7 %slice-start = ((bf16[32,72,128]{2,1,0:T(8,128)(2,1)}), bf16[32,16,128]{2,1,0:T(8,128)(2,1)S(1)}, s32[]{:S(2)}) async-start(bf16[32,72,128]{2,1,0:T(8,128)(2,1)} %copy-done.9), calls=%async_computation.5 | async-start | bytes 262144 | tf_op jit(solution)/shard_map/slice | solution.py:563
  97.4 13.2 %all-to-all-start.4 = ((bf16[32,17,2,128]{3,2,1,0:T(2,128)(2,1)}), bf16[32,17,2,128]{3,2,1,0:T(2,128)(2,1)S(1)}, u32[]{:S(2)}, u32[]{:S(2)}) async-start(bf16[32,17,2,128]{3,2,1,0:T(2,128)(2,1)} %bitcast.27), calls=%async_computation.4 | async-start | bytes 557056 | tf_op jit(solution)/shard_map/all_to_all | solution.py:289

commit v10 on v7

--- a/solution.py
+++ b/solution.py
@@ -295,7 +295,7 @@
         for low in steps
     ]
     lines = [
-        [device(f, y, x, high, low) for high in steps for low in steps]
+        [device(f, y, x, (high + f * cut // 2) % cut, low) for high in steps for low in steps]
         for f in range(2)
         for y in steps
         for x in steps
@@ -368,6 +368,7 @@
     y, x = r // cut, c % cut
     here = c // cut * cut + r % cut
     others = lax.broadcasted_iota(jnp.int32, (side, 128), 0)
+    others = (others + f * (side // 2)) & (side - 1)
     lane = lax.broadcasted_iota(jnp.int32, (side, 128), 1)
     main = lane < 2 * cells
     step = jnp.where(main, lane & (cells - 1), jnp.where((lane & 1) == 0, -1, cells))

time: 112 us -> 111 us (level)
  waiting for transfers between devices: 50.5 us -> 44.7 us
  starting transfers between devices: 46.5 us -> 51.2 us
    all_to_all x5, waiting for transfers between devices: 50.5 us -> 44.7 us  [swap(): lax.all_to_all(slots, ('face', 'row', 'col'), 0, 0, axis_index_groups=gro...]
    all_to_all x5, starting transfers between devices: 46.5 us -> 51.2 us  [swap(): lax.all_to_all(slots, ('face', 'row', 'col'), 0, 0, axis_index_groups=gro...]
where the time goes in v10:
time: 111 us; the launch traced here: 110 us
  starting transfers between devices  51.2 us (46%)
  waiting for transfers between devices  44.7 us (40%)
  Pallas kernels  6.45 us (6%)
  matrix products  3.46 us (3%)
  other arithmetic  1.71 us (2%)
  local copies, waits for them, and re-layouts  1.64 us (1%)
    all_to_all x5, starting transfers between devices, swap(): lax.all_to_all(slots, ('face', 'row', 'col'), 0, 0, axis_index_groups=gro...  51.2 us
    all_to_all x5, waiting for transfers between devices, swap(): lax.all_to_all(slots, ('face', 'row', 'col'), 0, 0, axis_index_groups=gro...  44.7 us
    pallas_call x1, Pallas kernels, block_on_tile(): pl.pallas_call(block_kernel, out_shape=(jax.ShapeDtypeStruct(grad_hidden....  2.75 us
  transfers between devices with their start and end apart: 5, of which 5 were waited for; matrix products, arithmetic and copies ran while one was open for 2% of the time, Pallas kernels for 1%

profile of v10, /device:TPU:1, one launch (start us, length us, event | category | flops | bytes accessed | tf_op | source)
XLA Modules:
  0.0 110.2 jit_solution(15587376195200823572)
XLA Ops:
  0.8 0.8 copy-done.1
  1.6 1.4 %edges.1 = bf16[32,32,128]{2,1,0:T(8,128)(2,1)} custom-call(s32[3]{0:T(128)S(1)} %pad_add_fusion.1.place_ref.plan_ref, bf16[16,16,128]{2,1,0:T(8,128)(2,1)S(1)} %bitcast.53), custom_call_target="tpu_custom_call" | custom-call | tf_op jit(solution)/shard_map/edges/pallas_call | solution.py:58
  3.0 10.5 %all-to-all-start = ((bf16[32,32,128]{2,1,0:T(8,128)(2,1)}), bf16[32,32,128]{2,1,0:T(8,128)(2,1)S(1)}, u32[]{:S(2)}, u32[]{:S(2)}) async-start(bf16[32,32,128]{2,1,0:T(8,128)(2,1)} %edges.1), calls=%async_computation | async-start | bytes 524288 | tf_op jit(solution)/shard_map/all_to_all | solution.py:278
  13.7 0.7 plan.1
  14.5 7.3 %all-to-all-done = bf16[32,32,128]{2,1,0:T(8,128)(2,1)S(1)} async-done(((bf16[32,32,128]{2,1,0:T(8,128)(2,1)}), bf16[32,32,128]{2,1,0:T(8,128)(2,1)S(1)}, u32[]{:S(2)}, u32[]{:S(2)}) %all-to-all-start) | async-done | bytes 262176 | tf_op jit(solution)/shard_map/all_to_all | solution.py:278
  21.8 1.2 %fusion.5 = bf16[576,128]{1,0:T(8,128)(2,1)} fusion(bf16[1024,128]{1,0:T(8,128)(2,1)S(1)} %bitcast.63, s32[576]{0:T(1024)S(1)} %eq.97), kind=kOutput, calls=%fused_computation.7 | convolution fusion | flops 151658496 | bytes 411904 | tf_op jit(solution)/shard_map/dot_general | solution.py:420
  23.0 16.4 %all-to-all-start.1 = ((bf16[16,9,4,128]{3,2,1,0:T(4,128)(2,1)}), bf16[16,9,4,128]{3,2,1,0:T(4,128)(2,1)S(1)}, u32[]{:S(2)}, u32[]{:S(2)}) async-start(bf16[16,9,4,128]{3,2,1,0:T(4,128)(2,1)} %bitcast.6), calls=%async_computation.1 | async-start | bytes 294912 | tf_op jit(solution)/shard_map/all_to_all | solution.py:278
  39.6 0.2 fusion.32.grad_hidden_ref
  39.9 6.9 %all-to-all-done.1 = bf16[16,9,4,128]{3,2,1,0:T(4,128)(2,1)S(1)} async-done(((bf16[16,9,4,128]{3,2,1,0:T(4,128)(2,1)}), bf16[16,9,4,128]{3,2,1,0:T(4,128)(2,1)S(1)}, u32[]{:S(2)}, u32[]{:S(2)}) %all-to-all-start.1) | async-done | bytes 147488 | tf_op jit(solution)/shard_map/all_to_all | solution.py:278
  46.8 0.2 fusion.31
  47.2 2.7 %block.1 = (bf16[256,512]{1,0:T(8,128)(2,1)S(1)}, bf16[32,72,128]{2,1,0:T(8,128)(2,1)}, f32[16,16,128]{2,1,0:T(8,128)S(1)}) custom-call(s32[3]{0:T(128)S(1)} %pad_add_fusion.1.place_ref.plan_ref, bf16[18,18,128]{2,1,0:T(8,128)(2,1)S(1)} %maximum_maximum_fusion.padded_ref, bf16[16,16,128]{2,1,0:T(8,128)(2,1)S(1)} %bitcast.57, ...), custom_call_target="tpu_custom_call" | custom-call | tf_op jit(solution)/shard_map/block/pallas_call | solution.py:184
  50.0 7.5 %all-to-all-start.2 = ((bf16[32,72,128]{2,1,0:T(8,128)(2,1)}), bf16[32,72,128]{2,1,0:T(8,128)(2,1)S(1)}, u32[]{:S(2)}, u32[]{:S(2)}) async-start(bf16[32,72,128]{2,1,0:T(8,128)(2,1)} %get-tuple-element.47), calls=%async_computation.2 | async-start | bytes 1179648 | tf_op jit(solution)/shard_map/all_to_all | solution.py:278
  57.6 11.6 %all-to-all-done.2 = bf16[32,72,128]{2,1,0:T(8,128)(2,1)S(1)} async-done(((bf16[32,72,128]{2,1,0:T(8,128)(2,1)}), bf16[32,72,128]{2,1,0:T(8,128)(2,1)S(1)}, u32[]{:S(2)}, u32[]{:S(2)}) %all-to-all-start.2) | async-done | bytes 589856 | tf_op jit(solution)/shard_map/all_to_all | solution.py:278
  69.3 0.7 fusion.4
  70.2 0.8 pad_maximum_fusion
  70.9 11.6 %all-to-all-start.3 = ((bf16[16,72,128]{2,1,0:T(8,128)(2,1)}), bf16[16,72,128]{2,1,0:T(8,128)(2,1)S(1)}, u32[]{:S(2)}, u32[]{:S(2)}) async-start(bf16[16,72,128]{2,1,0:T(8,128)(2,1)} %pad_maximum_fusion), calls=%async_computation.3 | async-start | bytes 589824 | tf_op jit(solution)/shard_map/all_to_all | solution.py:278
  82.6 0.9 fusion.7
  83.5 11.2 %all-to-all-done.3.got_ref = bf16[16,72,128]{2,1,0:T(8,128)(2,1)S(1)} async-done(((bf16[16,72,128]{2,1,0:T(8,128)(2,1)}), bf16[16,72,128]{2,1,0:T(8,128)(2,1)S(1)}, u32[]{:S(2)}, u32[]{:S(2)}) %all-to-all-start.3) | async-done | bytes 294944 | tf_op jit(solution)/shard_map/all_to_all | solution.py:278
  94.7 0.2 fusion.8
  95.0 0.8 share.1
  95.8 5.2 %all-to-all-start.4 = ((bf16[32,17,2,128]{3,2,1,0:T(2,128)(2,1)}), bf16[32,17,2,128]{3,2,1,0:T(2,128)(2,1)S(1)}, u32[]{:S(2)}, u32[]{:S(2)}) async-start(bf16[32,17,2,128]{3,2,1,0:T(2,128)(2,1)} %bitcast.27), calls=%async_computation.4 | async-start | bytes 557056 | tf_op jit(solution)/shard_map/all_to_all | solution.py:278
  101.1 0.7 fusion.18
  101.7 7.6 %all-to-all-done.4 = bf16[32,17,2,128]{3,2,1,0:T(2,128)(2,1)S(1)} async-done(((bf16[32,17,2,128]{3,2,1,0:T(2,128)(2,1)}), bf16[32,17,2,128]{3,2,1,0:T(2,128)(2,1)S(1)}, u32[]{:S(2)}, u32[]{:S(2)}) %all-to-all-start.4) | async-done | bytes 278560 | tf_op jit(solution)/shard_map/all_to_all | solution.py:278
  109.4 0.8 finish.1
  (60 shorter events, 1.1 us)
Async XLA Ops:
  0.6 38.9 %copy-start = (bf16[512,128]{1,0:T(8,128)(2,1)S(1)}, bf16[512,128]{1,0:T(8,128)(2,1)}, u32[]{:S(2)}) copy-start(bf16[512,128]{1,0:T(8,128)(2,1)} %param.22) | copy-start | bytes 393220
  0.7 12.8 %copy-start.11 = (s32[2,4,3]{1,0,2:T(2,128)S(1)}, s32[2,4,3]{1,0,2:T(2,128)}, u32[]{:S(2)}) copy-start(s32[2,4,3]{1,0,2:T(2,128)} %param.24) | copy-start | bytes 292
  0.8 0.8 copy-start.1
  3.0 18.8 %all-to-all-start = ((bf16[32,32,128]{2,1,0:T(8,128)(2,1)}), bf16[32,32,128]{2,1,0:T(8,128)(2,1)S(1)}, u32[]{:S(2)}, u32[]{:S(2)}) async-start(bf16[32,32,128]{2,1,0:T(8,128)(2,1)} %edges.1), calls=%async_computation | async-start | bytes 524288 | tf_op jit(solution)/shard_map/all_to_all | solution.py:278
  21.8 17.6 %copy-start.10 = (f32[3,3,128]{2,1,0:T(4,128)S(1)}, f32[3,3,128]{2,1,0:T(4,128)}, u32[]{:S(2)}) copy-start(f32[3,3,128]{2,1,0:T(4,128)} %param.16) | copy-start | bytes 13828
  21.8 17.8 %copy-start.3 = (bf16[1,16,16,128]{3,2,1,0:T(8,128)(2,1)S(1)}, bf16[1,16,16,128]{3,2,1,0:T(8,128)(2,1)}, u32[]{:S(2)}) copy-start(bf16[1,16,16,128]{3,2,1,0:T(8,128)(2,1)} %param.25) | copy-start | bytes 196612
  23.0 23.8 %all-to-all-start.1 = ((bf16[16,9,4,128]{3,2,1,0:T(4,128)(2,1)}), bf16[16,9,4,128]{3,2,1,0:T(4,128)(2,1)S(1)}, u32[]{:S(2)}, u32[]{:S(2)}) async-start(bf16[16,9,4,128]{3,2,1,0:T(4,128)(2,1)} %bitcast.6), calls=%async_computation.1 | async-start | bytes 294912 | tf_op jit(solution)/shard_map/all_to_all | solution.py:278
  39.5 7.6 %copy-start.2 = (bf16[1,16,16,128]{3,2,1,0:T(8,128)(2,1)S(1)}, bf16[1,16,16,128]{3,2,1,0:T(8,128)(2,1)}, u32[]{:S(2)}) copy-start(bf16[1,16,16,128]{3,2,1,0:T(8,128)(2,1)} %param.15) | copy-start | bytes 196612
  39.5 7.6 %copy-start.4 = (bf16[128,512]{1,0:T(8,128)(2,1)S(1)}, bf16[128,512]{1,0:T(8,128)(2,1)}, u32[]{:S(2)}) copy-start(bf16[128,512]{1,0:T(8,128)(2,1)} %expand_ref.1) | copy-start | bytes 393220
  39.6 7.6 %copy-start.5 = (f32[512]{0:T(512)S(1)}, f32[512]{0:T(512)}, u32[]{:S(2)}) copy-start(f32[512]{0:T(512)} %param.21) | copy-start | bytes 6148
  39.6 7.6 %copy-start.6 = (f32[128]{0:T(128)S(1)}, f32[128]{0:T(128)}, u32[]{:S(2)}) copy-start(f32[128]{0:T(128)} %param.17) | copy-start | bytes 1540
  39.6 7.6 %copy-start.7 = (f32[128]{0:T(128)S(1)}, f32[128]{0:T(128)}, u32[]{:S(2)}) copy-start(f32[128]{0:T(128)} %param.18) | copy-start | bytes 1540
  39.6 7.6 %copy-start.8 = (f32[128]{0:T(128)S(1)}, f32[128]{0:T(128)}, u32[]{:S(2)}) copy-start(f32[128]{0:T(128)} %param.19) | copy-start | bytes 1540
  50.0 19.3 %all-to-all-start.2 = ((bf16[32,72,128]{2,1,0:T(8,128)(2,1)}), bf16[32,72,128]{2,1,0:T(8,128)(2,1)S(1)}, u32[]{:S(2)}, u32[]{:S(2)}) async-start(bf16[32,72,128]{2,1,0:T(8,128)(2,1)} %get-tuple-element.47), calls=%async_computation.2 | async-start | bytes 1179648 | tf_op jit(solution)/shard_map/all_to_all | solution.py:278
  69.2 14.2 %copy-start.9 = (bf16[32,72,128]{2,1,0:T(8,128)(2,1)}, bf16[32,72,128]{2,1,0:T(8,128)(2,1)S(1)}, u32[]{:S(2)}) copy-start(bf16[32,72,128]{2,1,0:T(8,128)(2,1)S(1)} %all-to-all-done.2) | copy-start | bytes 1769476
  70.2 12.4 %copy-start.12 = (f32[128]{0:T(128)S(1)}, f32[128]{0:T(128)}, u32[]{:S(2)}) copy-start(f32[128]{0:T(128)} %param.23) | copy-start | bytes 1540
  70.9 23.8 %all-to-all-start.3 = ((bf16[16,72,128]{2,1,0:T(8,128)(2,1)}), bf16[16,72,128]{2,1,0:T(8,128)(2,1)S(1)}, u32[]{:S(2)}, u32[]{:S(2)}) async-start(bf16[16,72,128]{2,1,0:T(8,128)(2,1)} %pad_maximum_fusion), calls=%async_computation.3 | async-start | bytes 589824 | tf_op jit(solution)/shard_map/all_to_all | solution.py:278
  95.0 6.1 %slice-start = ((bf16[32,72,128]{2,1,0:T(8,128)(2,1)}), bf16[32,16,128]{2,1,0:T(8,128)(2,1)S(1)}, s32[]{:S(2)}) async-start(bf16[32,72,128]{2,1,0:T(8,128)(2,1)} %copy-done.9), calls=%async_computation.5 | async-start | bytes 262144 | tf_op jit(solution)/shard_map/slice | solution.py:552
  95.8 13.6 %all-to-all-start.4 = ((bf16[32,17,2,128]{3,2,1,0:T(2,128)(2,1)}), bf16[32,17,2,128]{3,2,1,0:T(2,128)(2,1)S(1)}, u32[]{:S(2)}, u32[]{:S(2)}) async-start(bf16[32,17,2,128]{3,2,1,0:T(2,128)(2,1)} %bitcast.27), calls=%async_computation.4 | async-start | bytes 557056 | tf_op jit(solution)/shard_map/all_to_all | solution.py:278
